TPU v7x, 512 devices: a whole 4x4x16 slice. The times are simulated.
512 devices in a mesh: section: 8 (over y_hi, x), dp: 64 (over z, y_lo, core).
Axes of the slice: x: 4, y: 4 (y_hi: 2, y_lo: 2; y = y_hi * 2 + y_lo), z: 16, core: 2. Of those that a mesh axis runs over, the one named last changes fastest.
Arguments:
- acts: bfloat16 [8, 8704, 8192], P('section', 'dp'), may hold values from -6 to 6
- value_grad: bfloat16 [8, 8704, 512], P('section', 'dp'), may hold values from -6 to 6
- loss_weight: int32 [8, 8704], P('section', 'dp'), may hold values from 1 to 4
- value_weight: bfloat16 [8, 8192, 512], P('section', 'dp'), may hold values from -0.0625 to 0.0625
- down_master: float32 [8, 8192, 64], P('section', 'dp'), may hold values from -0.0625 to 0.0625
- down_first: float32 [8, 8192, 64], P('section', 'dp'), may hold values from -0.006 to 0.006
- down_second: float32 [8, 8192, 64], P('section', 'dp'), may hold values from 1e-06 to 0.0001
- up_master: float32 [8, 64, 512], P('section', 'dp'), may hold values from -0.75 to 0.75
- up_first: float32 [8, 64, 512], P('section', 'dp'), may hold values from -0.006 to 0.006
- up_second: float32 [8, 64, 512], P('section', 'dp'), may hold values from 1e-06 to 0.0001
- step_count: int32 [1], replicated, may hold values from 1 to 99
Outputs:
- upstream_grad: bfloat16 [8, 8704, 8192], P('section', 'dp')
- refreshed: bfloat16 [8, 8704, 512], P('section', 'dp')
- down_new: float32 [8, 8192, 64], P('section', 'dp')
- down_first_new: float32 [8, 8192, 64], P('section', 'dp')
- down_second_new: float32 [8, 8192, 64], P('section', 'dp')
- up_new: float32 [8, 64, 512], P('section', 'dp')
- up_first_new: float32 [8, 64, 512], P('section', 'dp')
- up_second_new: float32 [8, 64, 512], P('section', 'dp')
All inputs are finite; a program needn't handle non-finite values.
Results may differ from a plain program's by a relative error of at most 0.007.
The roundings to bfloat16 on the way count: a program that leaves them out, or rounds other values in their place, can miss the bound.
Values may be sent and summed in bfloat16 or wider, within the bound.
No kernel may reach another device: no remote copies, remote signals or barrier semaphores. Data moves between devices by JAX's collectives and lax.ppermute only.
A program may use at most 64 MiB of HBM per device.

v0:
```python
import jax
import jax.numpy as jnp
from jax import lax
from jax.sharding import PartitionSpec as P

adapter_scale = 2.0
beta_one = 0.9
beta_two = 0.999
learn_rate = 0.05
adam_eps = 1e-08


def passed_along(array, axis, by):
    size = lax.axis_size(axis)
    pairs = [(i, i + by) for i in range(size) if 0 <= i + by < size]
    return lax.ppermute(array, axis, pairs)


def adam_update(master, first, second, grad, count):
    first_new = beta_one * first + (1.0 - beta_one) * grad
    second_new = beta_two * second + (1.0 - beta_two) * grad * grad
    fix_first = 1.0 - jnp.power(jnp.float32(beta_one), count)
    fix_second = 1.0 - jnp.power(jnp.float32(beta_two), count)
    master_new = master - learn_rate * (first_new / fix_first) / (
        jnp.sqrt(second_new / fix_second) + adam_eps
    )
    return (master_new, first_new, second_new)


def per_device(
    acts,
    value_grad,
    loss_weight,
    value_weight,
    down_master,
    down_first,
    down_second,
    up_master,
    up_first,
    up_second,
    step_count,
):
    weight_f = loss_weight.astype(jnp.float32)
    total = lax.psum(jnp.sum(weight_f), "dp")
    share = weight_f / total
    scaled = (value_grad.astype(jnp.float32) * share[:, :, None]).astype(jnp.bfloat16)
    down_cur = down_master.astype(jnp.bfloat16)
    up_cur = up_master.astype(jnp.bfloat16)
    down_all, up_all = (
        lax.all_gather(down_cur, "dp", axis=1, tiled=True),
        lax.all_gather(up_cur, "dp", axis=1, tiled=True),
    )
    mid = (
        adapter_scale
        * jnp.einsum("btk,brk->btr", scaled, up_all, preferred_element_type=jnp.float32)
    ).astype(jnp.bfloat16)
    low = jnp.einsum("btd,bdr->btr", acts, down_all, preferred_element_type=jnp.float32).astype(
        jnp.bfloat16
    )
    grad_down = jnp.einsum("btd,btr->bdr", acts, mid, preferred_element_type=jnp.float32)
    grad_up = adapter_scale * jnp.einsum(
        "btr,btk->brk", low, scaled, preferred_element_type=jnp.float32
    )
    down_grad, up_grad = (
        lax.psum_scatter(grad_down, "dp", scatter_dimension=1, tiled=True),
        lax.psum_scatter(grad_up, "dp", scatter_dimension=1, tiled=True),
    )
    base_part = jnp.einsum(
        "btk,bdk->btd",
        scaled,
        lax.all_gather(value_weight, "dp", axis=1, tiled=True),
        preferred_element_type=jnp.float32,
    )
    adapter_part = jnp.einsum("btr,bdr->btd", mid, down_all, preferred_element_type=jnp.float32)
    input_grad = (base_part + adapter_part).astype(jnp.bfloat16)
    upstream_grad = passed_along(input_grad, "section", -1)
    count = step_count.astype(jnp.float32)[0]
    down_new, down_first_new, down_second_new = adam_update(
        down_master, down_first, down_second, down_grad, count
    )
    up_new, up_first_new, up_second_new = adam_update(
        up_master, up_first, up_second, up_grad, count
    )
    down_next, up_next = (
        lax.all_gather(down_new.astype(jnp.bfloat16), "dp", axis=1, tiled=True),
        lax.all_gather(up_new.astype(jnp.bfloat16), "dp", axis=1, tiled=True),
    )
    low_new = jnp.einsum(
        "btd,bdr->btr", acts, down_next, preferred_element_type=jnp.float32
    ).astype(jnp.bfloat16)
    refreshed = (
        adapter_scale
        * jnp.einsum("btr,brk->btk", low_new, up_next, preferred_element_type=jnp.float32)
    ).astype(jnp.bfloat16)
    return (
        upstream_grad,
        refreshed,
        down_new,
        down_first_new,
        down_second_new,
        up_new,
        up_first_new,
        up_second_new,
    )


def solution(mesh):
    in_specs = (
        P("section", "dp", None),
        P("section", "dp", None),
        P("section", "dp"),
        P("section", "dp", None),
        P("section", "dp", None),
        P("section", "dp", None),
        P("section", "dp", None),
        P("section", "dp", None),
        P("section", "dp", None),
        P("section", "dp", None),
        P(),
    )
    out_specs = (
        P("section", "dp", None),
        P("section", "dp", None),
        P("section", "dp", None),
        P("section", "dp", None),
        P("section", "dp", None),
        P("section", "dp", None),
        P("section", "dp", None),
        P("section", "dp", None),
    )
    return jax.shard_map(
        per_device, mesh=mesh, in_specs=in_specs, out_specs=out_specs, check_vma=False
    )
```

profile of v0, /device:TPU:7, one launch (start us, length us, event | category | flops | bytes accessed | tf_op | source)
XLA Modules:
  0.0 1196.2 jit_solution(7771709832385450422)
XLA Ops:
  7.2 0.0 copy-start
  7.2 0.0 reduce-scatter.3.cloned.1.call-start
  7.2 1.4 convert_reduce_fusion
  8.7 112.1 %psum.7 = f32[]{:T(128)} all-reduce(f32[]{:T(128)} %convert_reduce_fusion), channel_id=1, replica_groups=mesh['section'=8,'dp'=64] {'dp'}, use_global_device_ids=true, to_apply=%region_1.0 | all-reduce | flops 1 | bytes 8 | tf_op jit(solution)/shard_map/psum | solution.py:44
  120.8 1.3 convert_divide_fusion
  122.1 0.7 bitcast_convert_fusion
  122.8 63.2 %all_gather.16 = bf16[1,64,512]{2,0,1:T(2,128)(2,1)S(1)} all-gather(bf16[1,1,512]{2,0,1:T(2,128)(2,1)S(1)} %bitcast_convert_fusion), channel_id=1, replica_groups=mesh['section'=8,'dp'=64] {'dp'}, dimensions={1}, use_global_device_ids=true | all-gather | bytes 66560 | tf_op jit(solution)/shard_map/all_gather | solution.py:51
  186.0 1.1 fusion.12
  187.1 0.0 copy-done
  187.2 0.0 copy-start.3
  187.2 0.0 copy-start.4
  187.2 0.0 copy-start.5
  187.2 1.9 convolution_bitcast_fusion
  189.1 0.0 copy-start.2
  189.1 0.0 reduce-scatter.3.cloned.1.call-update
  189.1 0.0 all-gather.6.cloned.1.call-start
  189.9 218.8 %reduce-scatter.3.cloned.1.call-done = f32[1,128,64]{1,2,0:T(8,128)} async-done(((f32[1,8192,64]{1,2,0:T(8,128)}), f32[1,128,64]{1,2,0:T(8,128)}) %reduce-scatter.3.cloned.1.call-update) | async-done | bytes 32784 | tf_op jit(solution)/shard_map/reduce_scatter | solution.py:65
  408.7 0.0 copy-done.3
  408.7 0.0 copy-done.4
  408.7 0.0 copy-done.5
  408.7 1.4 fusion.41
  410.1 0.0 all-gather.6.cloned.1.call-update
  410.1 0.0 all-gather.4.cloned.1.call-start
  410.2 0.7 all-gather.4.cloned.1.call-update
  410.9 0.0 all-reduce.3.cloned.1.call-start
  410.9 120.0 %all-gather.6.cloned.1.call-done = bf16[1,8192,64]{1,2,0:T(8,128)(2,1)} async-done(((bf16[1,128,64]{1,2,0:T(8,128)(2,1)}), bf16[1,8192,64]{1,2,0:T(8,128)(2,1)}) %all-gather.6.cloned.1.call-update) | async-done | bytes 1048592 | tf_op jit(solution)/shard_map/all_gather | solution.py:50
  530.9 0.0 copy-done.2
  530.9 2.9 fusion.11
  533.9 0.0 all-reduce.3.cloned.1.call-update
  533.9 0.0 all-gather.8.cloned.1.call-start
  533.9 0.5 all-gather.8.cloned.1.call-update
  534.5 0.0 copy-start.1
  534.5 124.0 %all-gather.4.cloned.1.call-done = bf16[1,8192,512]{2,1,0:T(8,128)(2,1)} async-done(((bf16[1,128,512]{2,1,0:T(8,128)(2,1)}), bf16[1,8192,512]{2,1,0:T(8,128)(2,1)}) %all-gather.4.cloned.1.call-update) | async-done | bytes 8388624 | tf_op jit(solution)/shard_map/all_gather | solution.py:71
  658.5 6.2 fusion.2
  664.7 0.0 copy-done.1
  664.7 0.0 copy-start.6
  664.7 0.0 copy-start.7
  664.7 0.0 copy-start.8
  664.7 2.1 fusion.1
  666.9 2.4 collective-permute-start
  669.3 1.3 dynamic-slice
  670.7 397.4 %all-reduce.3.cloned.1.call-done = f32[1,64,512]{2,1,0:T(8,128)} async-done(((f32[1,64,512]{2,1,0:T(8,128)}), f32[1,64,512]{2,1,0:T(8,128)}) %all-reduce.3.cloned.1.call-update) | async-done | bytes 131088
  1068.1 0.0 copy-done.6
  1068.1 0.0 copy-done.7
  1068.1 0.0 copy-done.8
  1068.1 2.0 convert_bitcast_fusion
  1070.1 61.4 %all_gather.19 = bf16[1,64,512]{2,0,1:T(2,128)(2,1)S(1)} all-gather(bf16[1,1,512]{2,0,1:T(2,128)(2,1)S(1)} %get-tuple-element.8), channel_id=1, replica_groups=mesh['section'=8,'dp'=64] {'dp'}, dimensions={1}, use_global_device_ids=true | all-gather | bytes 66560 | tf_op jit(solution)/shard_map/all_gather | solution.py:86
  1131.5 52.0 %all-gather.8.cloned.1.call-done = bf16[1,8192,64]{1,2,0:T(8,128)(2,1)} async-done(((bf16[1,128,64]{1,2,0:T(8,128)(2,1)}), bf16[1,8192,64]{1,2,0:T(8,128)(2,1)}) %all-gather.8.cloned.1.call-update) | async-done | bytes 1048592 | tf_op jit(solution)/shard_map/all_gather | solution.py:85
  1183.5 3.0 fusion.10
  1186.5 0.0 collective-permute-done
  1186.5 3.2 copy.38
Async XLA Ops:
  7.2 180.0 %copy-start = (bf16[1,136,8192]{2,1,0:T(8,128)(2,1)S(1)}, bf16[1,136,8192]{2,1,0:T(8,128)(2,1)}, u32[]{:S(2)}) copy-start(bf16[1,136,8192]{2,1,0:T(8,128)(2,1)} %param.11) | copy-start | bytes 6684676
  7.2 401.5 %reduce-scatter.3.cloned.1.call-start = ((), (), s32[]{:S(2)}) async-start(), calls=%async_computation.3 | async-start | bytes 2129920 | tf_op jit(solution)/shard_map/reduce_scatter | solution.py:65
  187.2 221.5 %copy-start.3 = (f32[1,128,64]{1,2,0:T(8,128)S(1)}, f32[1,128,64]{1,2,0:T(8,128)}, u32[]{:S(2)}) copy-start(f32[1,128,64]{1,2,0:T(8,128)} %param.15) | copy-start | bytes 98308
  187.2 221.5 %copy-start.4 = (f32[1,128,64]{1,2,0:T(8,128)S(1)}, f32[1,128,64]{1,2,0:T(8,128)}, u32[]{:S(2)}) copy-start(f32[1,128,64]{1,2,0:T(8,128)} %param.16) | copy-start | bytes 98308
  187.2 221.5 %copy-start.5 = (f32[1,128,64]{1,2,0:T(8,128)S(1)}, f32[1,128,64]{1,2,0:T(8,128)}, u32[]{:S(2)}) copy-start(f32[1,128,64]{1,2,0:T(8,128)} %param.17) | copy-start | bytes 98308
  189.1 341.8 %copy-start.2 = (bf16[1,136,512]{2,1,0:T(8,128)(2,1)S(1)}, bf16[1,136,512]{2,1,0:T(8,128)(2,1)}, u32[]{:S(2)}) copy-start(bf16[1,136,512]{2,1,0:T(8,128)(2,1)} %param.12) | copy-start | bytes 417796
  189.1 341.8 %all-gather.6.cloned.1.call-start = ((), (), s32[]{:S(2)}) async-start(), calls=%async_computation.2 | async-start | bytes 1064960 | tf_op jit(solution)/shard_map/all_gather | solution.py:50
  410.1 248.3 %all-gather.4.cloned.1.call-start = ((), (), s32[]{:S(2)}) async-start(), calls=%async_computation.1 | async-start | bytes 8519680 | tf_op jit(solution)/shard_map/all_gather | solution.py:71
  410.9 657.2 %all-reduce.3.cloned.1.call-start = ((), (), s32[]{:S(2)}) async-start(), calls=%async_computation.5 | async-start | bytes 262144
  533.9 649.6 %all-gather.8.cloned.1.call-start = ((), (), s32[]{:S(2)}) async-start(), calls=%async_computation.4 | async-start | bytes 1064960 | tf_op jit(solution)/shard_map/all_gather | solution.py:85
  534.5 130.2 %copy-start.1 = (bf16[1,8192,64]{1,2,0:T(8,128)(2,1)S(1)}, bf16[1,8192,64]{1,2,0:T(8,128)(2,1)}, u32[]{:S(2)}) copy-start(bf16[1,8192,64]{1,2,0:T(8,128)(2,1)} %all-gather.6.cloned.1.call-done) | copy-start | bytes 3145732
  664.7 403.4 %copy-start.6 = (f32[1,1,512]{2,1,0:T(1,128)S(1)}, f32[1,1,512]{2,1,0:T(1,128)}, u32[]{:S(2)}) copy-start(f32[1,1,512]{2,1,0:T(1,128)} %param.18) | copy-start | bytes 6148
  664.7 403.4 %copy-start.7 = (f32[1,1,512]{2,1,0:T(1,128)S(1)}, f32[1,1,512]{2,1,0:T(1,128)}, u32[]{:S(2)}) copy-start(f32[1,1,512]{2,1,0:T(1,128)} %param.19) | copy-start | bytes 6148
  664.7 403.3 %copy-start.8 = (f32[1,1,512]{2,1,0:T(1,128)S(1)}, f32[1,1,512]{2,1,0:T(1,128)}, u32[]{:S(2)}) copy-start(f32[1,1,512]{2,1,0:T(1,128)} %param.20) | copy-start | bytes 6148
  666.9 519.7 %collective-permute-start = (bf16[1,136,8192]{2,1,0:T(8,128)(2,1)}, bf16[1,136,8192]{2,1,0:T(8,128)(2,1)}, u32[]{:S(2)}, u32[]{:S(2)}) collective-permute-start(bf16[1,136,8192]{2,1,0:T(8,128)(2,1)} %fusion.1), channel_id=1, source_target_pairs={{64,0},{128,64},{192,128},{256,192},{320,256},{384,320},{448,384},... | collective-permute-start | bytes 6684680 | tf_op jit(solution)/shard_map/ppermute | solution.py:16
Sparse Core Ops, SparseCore 0:
  189.3 219.3 reduce-scatter.2
  411.5 119.3 all-gather.5
  533.3 125.1 all-gather.3
  662.1 405.9 all-reduce.2
  1070.0 113.4 all-gather.7
where the time goes:
time: 1200 us
  waiting for transfers between devices  913 us (76%)
  blocking collectives  237 us (20%)
  matrix products  17.4 us (1%)
  between operations  14.6 us (1%)
    unnamed x6, waiting for transfers between devices  399 us
    reduce_scatter x1, waiting for transfers between devices, per_device(): lax.psum_scatter(grad_down, 'dp', scatter_dimension=1, tiled=True)  219 us
    all_gather x1, waiting for transfers between devices, per_device(): lax.all_gather(value_weight, 'dp', axis=1, tiled=True)  124 us
    all_gather x1, waiting for transfers between devices, per_device(): lax.all_gather(down_cur, 'dp', axis=1, tiled=True)  120 us
    psum x1, blocking collectives, per_device(): total = lax.psum(jnp.sum(weight_f), 'dp')  112 us
    all_gather x1, blocking collectives, per_device(): lax.all_gather(up_cur, 'dp', axis=1, tiled=True)  63.2 us
    all_gather x1, blocking collectives, per_device(): lax.all_gather(up_new.astype(jnp.bfloat16), 'dp', axis=1, tiled=True)  61.4 us
    all_gather x1, waiting for transfers between devices, per_device(): lax.all_gather(down_new.astype(jnp.bfloat16), 'dp', axis=1, tiled=True)  52 us
  transfers between devices with their start and end apart: 6, of which 5 were waited for; matrix products, arithmetic and copies ran while one was open for 1% of the time, Pallas kernels for 0%

commit v1 on v0

v1 whole, which is shorter than its diff:
```python
import jax
import jax.numpy as jnp
from jax import lax
from jax.sharding import Mesh, PartitionSpec as P

adapter_scale = 2.0
beta_one = 0.9
beta_two = 0.999
learn_rate = 0.05
adam_eps = 1e-08

LANES = 128
bf16 = jnp.bfloat16
f32 = jnp.float32


def adam_update(master, first, second, grad, count):
    first_new = beta_one * first + (1.0 - beta_one) * grad
    second_new = beta_two * second + (1.0 - beta_two) * grad * grad
    fix_first = 1.0 - jnp.power(jnp.float32(beta_one), count)
    fix_second = 1.0 - jnp.power(jnp.float32(beta_two), count)
    master_new = master - learn_rate * (first_new / fix_first) / (
        jnp.sqrt(second_new / fix_second) + adam_eps
    )
    return (master_new, first_new, second_new)


def from_next_section(array):
    size = lax.axis_size("section")
    return lax.ppermute(array, "section", [(i, i - 1) for i in range(1, size)])


def gather_blocks(block):
    got = lax.all_gather(block, "z")
    got = lax.all_gather(got, "yl")
    return lax.all_gather(got, "core")


def reduce_blocks(blocks):
    got = lax.all_to_all(blocks, "core", 0, 0)
    kept = got[0] + got[1]
    got = lax.all_to_all(kept.astype(bf16), "yl", 0, 0)
    kept = got[0].astype(f32) + got[1].astype(f32)
    got = lax.all_to_all(kept.astype(bf16), "z", 0, 0)
    return jnp.sum(got.astype(f32), axis=0)


def pad_rows(parts, rows):
    have = sum(p.shape[0] for p in parts)
    if have < rows:
        parts = parts + [jnp.zeros((rows - have, LANES), parts[0].dtype)]
    return jnp.concatenate(parts, axis=0)


def per_device(
    acts,
    value_grad,
    loss_weight,
    value_weight,
    down_master,
    down_first,
    down_second,
    up_master,
    up_first,
    up_second,
    step_count,
):
    tokens, width = acts.shape[1:]
    features = value_grad.shape[2]
    rank = down_master.shape[2]
    up_rows = features // LANES
    rows = -(-(rank + up_rows + 2) // 8) * 8
    acts = acts[0]
    down_cur = down_master[0].T.astype(bf16)
    up_cur = up_master[0].astype(bf16).reshape(up_rows, LANES)

    weights = jnp.concatenate([value_weight[0].T, down_cur], axis=0)
    weights = from_next_section(weights)
    weights_all = lax.all_gather(weights, ("z", "yl", "core"))

    part = jnp.sum(loss_weight)
    high, low_bits = part // 128, part % 128
    count_rows = jnp.stack([high, low_bits]).astype(bf16)[:, None] * jnp.ones((1, LANES), bf16)
    got = gather_blocks(pad_rows([down_cur, up_cur, count_rows], rows))
    got = jnp.transpose(got, (2, 1, 0, 3, 4)).reshape(-1, rows, LANES)
    counts = got[:, rank + up_rows : rank + up_rows + 2, 0].astype(f32)
    total = jnp.sum(counts[:, 0] * 128.0 + counts[:, 1])
    share = loss_weight[0].astype(f32) / total
    scaled = (value_grad[0].astype(f32) * share[:, None]).astype(bf16)
    down_all = jnp.transpose(got[:, :rank], (1, 0, 2)).reshape(rank, width)
    up_all = got[:, rank : rank + up_rows].reshape(rank, features)

    mid = (adapter_scale * jnp.einsum("tk,rk->tr", scaled, up_all, preferred_element_type=f32)).astype(bf16)
    low = jnp.einsum("td,rd->tr", acts, down_all, preferred_element_type=f32).astype(bf16)
    next_rows = from_next_section(jnp.concatenate([scaled, mid], axis=1))
    grad_down = jnp.einsum("tr,td->rd", mid, acts, preferred_element_type=f32)
    grad_up = adapter_scale * jnp.einsum("tr,tk->rk", low, scaled, preferred_element_type=f32)

    z = lax.axis_size("z")
    grad = jnp.concatenate(
        [
            jnp.transpose(grad_down.reshape(rank, -1, LANES), (1, 0, 2)),
            grad_up.reshape(-1, up_rows, LANES),
            jnp.zeros((4 * z, rows - rank - up_rows, LANES), f32),
        ],
        axis=1,
    )
    grad = jnp.transpose(grad.reshape(z, 2, 2, rows, LANES), (2, 1, 0, 3, 4))
    grad = reduce_blocks(grad)

    count = step_count.astype(f32)[0]
    down_new, down_first_new, down_second_new = adam_update(
        down_master[0].T, down_first[0].T, down_second[0].T, grad[:rank], count
    )
    up_new, up_first_new, up_second_new = adam_update(
        up_master[0], up_first[0], up_second[0], grad[rank : rank + up_rows].reshape(1, features), count
    )
    got = gather_blocks(
        pad_rows([down_new.astype(bf16), up_new.astype(bf16).reshape(up_rows, LANES)], rows)
    )
    got = jnp.transpose(got, (2, 1, 0, 3, 4)).reshape(-1, rows, LANES)
    down_next = jnp.transpose(got[:, :rank], (1, 0, 2)).reshape(rank, width)
    up_next = got[:, rank : rank + up_rows].reshape(rank, features)
    low_new = jnp.einsum("td,rd->tr", acts, down_next, preferred_element_type=f32).astype(bf16)
    refreshed = (
        adapter_scale * jnp.einsum("tr,rk->tk", low_new, up_next, preferred_element_type=f32)
    ).astype(bf16)

    upstream = jnp.einsum("tk,bkd->tbd", next_rows, weights_all, preferred_element_type=f32)
    upstream = upstream.astype(bf16).reshape(tokens, width)
    return (
        upstream[None],
        refreshed[None],
        down_new.T[None],
        down_first_new.T[None],
        down_second_new.T[None],
        up_new[None],
        up_first_new[None],
        up_second_new[None],
    )


def solution(mesh):
    sections, dp = mesh.devices.shape
    staged = Mesh(mesh.devices.reshape(sections, dp // 4, 2, 2), ("section", "z", "yl", "core"))
    split = P("section", ("z", "yl", "core"))
    return jax.shard_map(
        per_device,
        mesh=staged,
        in_specs=(split,) * 10 + (P(),),
        out_specs=(split,) * 8,
        check_vma=False,
    )
```

time: 1200 us -> 344 us (0.29)
  waiting for transfers between devices: 913 us -> 188 us
  blocking collectives: 237 us -> 86.8 us
  starting transfers between devices: 2.65 us -> 16.5 us
    unnamed x6 -> x3, waiting for transfers between devices: 399 us -> 0.05 us
    reduce_scatter x1 -> x0, waiting for transfers between devices: 219 us -> none  [per_device(): lax.psum_scatter(grad_down, 'dp', scatter_dimension=1, tiled=True)]
    all_gather x3, waiting for transfers between devices: 296 us -> 168 us  [the longest x1 131 us: per_device(): weights_all = lax.all_gather(weights, ('z', 'yl', 'core'))]
    psum x1 -> x0, blocking collectives: 112 us -> none  [per_device(): total = lax.psum(jnp.sum(weight_f), 'dp')]
    all_gather x2 -> x4, blocking collectives: 125 us -> 70.7 us  [the longest x2 58 us: gather_blocks(): got = lax.all_gather(block, 'z')]
    all_to_all x0 -> x2, blocking collectives: none -> 16.2 us  [the longest x1 10.7 us: reduce_blocks(): got = lax.all_to_all(kept.astype(bf16), 'yl', 0, 0)]
    all_to_all x0 -> x1, waiting for transfers between devices: none -> 12.4 us  [reduce_blocks(): got = lax.all_to_all(kept.astype(bf16), 'z', 0, 0)]
    all_to_all x0 -> x1, starting transfers between devices: none -> 12 us  [reduce_blocks(): got = lax.all_to_all(kept.astype(bf16), 'z', 0, 0)]
where the time goes in v1:
time: 344 us; the launch traced here: 342 us
  waiting for transfers between devices  188 us (55%)
  blocking collectives  86.8 us (25%)
  between operations  17.4 us (5%)
  starting transfers between devices  16.5 us (5%)
  local copies, waits for them, and re-layouts  12.4 us (4%)
  matrix products  12.3 us (4%)
  other arithmetic  8.67 us (3%)
    all_gather x1, waiting for transfers between devices, per_device(): weights_all = lax.all_gather(weights, ('z', 'yl', 'core'))  131 us
    all_gather x2, blocking collectives, gather_blocks(): got = lax.all_gather(block, 'z')  58 us
    all_gather x2, waiting for transfers between devices, gather_blocks(): return lax.all_gather(got, 'core')  37.3 us
    all_gather x2, blocking collectives, gather_blocks(): got = lax.all_gather(got, 'yl')  12.7 us
    all_to_all x1, waiting for transfers between devices, reduce_blocks(): got = lax.all_to_all(kept.astype(bf16), 'z', 0, 0)  12.4 us
    all_to_all x1, starting transfers between devices, reduce_blocks(): got = lax.all_to_all(kept.astype(bf16), 'z', 0, 0)  12 us
    all_to_all x1, blocking collectives, reduce_blocks(): got = lax.all_to_all(kept.astype(bf16), 'yl', 0, 0)  10.7 us
    ppermute x2, waiting for transfers between devices, from_next_section(): return lax.ppermute(array, 'section', [(i, i - 1) for i in range(1, size)])  7.12 us
  transfers between devices with their start and end apart: 6, of which 5 were waited for; matrix products, arithmetic and copies ran while one was open for 1% of the time, Pallas kernels for 0%

profile of v1, /device:TPU:7, one launch (start us, length us, event | category | flops | bytes accessed | tf_op | source)
XLA Modules:
  0.0 342.0 jit_solution(13419110934945673688)
XLA Ops:
  7.2 0.0 copy-start
  7.2 0.0 all-gather.11.cloned.1.call-start
  7.2 1.5 reduce_sum.27
  11.3 0.7 convert_element_type.101
  12.0 0.8 bitcast_convert_fusion
  12.8 0.1 pad_maximum_fusion.2
  12.8 0.1 pad.13.clone
  12.9 0.1 maximum_maximum_fusion
  13.0 29.8 %all-gather = bf16[1152,128]{1,0:T(8,128)(2,1)S(1)} all-gather(bf16[72,128]{1,0:T(8,128)(2,1)S(1)} %maximum_maximum_fusion), channel_id=2, replica_groups=mesh['section'=8,'z'=16,'yl'=2,'core'=2] {'z'}, dimensions={0}, use_global_device_ids=true | all-gather | bytes 313344 | tf_op jit(solution)/shard_map/all_gather | solution.py:34
  42.8 6.3 %all-gather.1 = bf16[32,72,128]{2,1,0:T(8,128)(2,1)} all-gather(bf16[16,72,128]{2,1,0:T(8,128)(2,1)S(1)} %bitcast.151), channel_id=3, replica_groups=mesh['section'=8,'z'=16,'yl'=2,'core'=2] {'yl'}, dimensions={0}, use_global_device_ids=true | all-gather | bytes 884736 | tf_op jit(solution)/shard_map/all_gather | solution.py:35
  49.2 0.0 copy-done.1
  49.2 0.0 all-gather.11.cloned.1.call-update
  49.2 0.1 pad.5.clone
  49.3 24.5 %all-gather.11.cloned.1.call-done = bf16[4,16,72,128]{3,2,1,0:T(8,128)(2,1)} async-done(((bf16[2,16,72,128]{3,2,1,0:T(8,128)(2,1)}), bf16[4,16,72,128]{3,2,1,0:T(8,128)(2,1)}) %all-gather.11.cloned.1.call-update) | async-done | bytes 1179664 | tf_op jit(solution)/shard_map/all_gather | solution.py:36
  73.8 1.4 copy.54
  75.2 0.6 slice.53
  75.9 0.1 copy.66
  76.0 0.6 add_reduce_fusion
  76.6 0.0 copy-done.12
  76.6 0.6 convert_divide_fusion
  77.2 1.0 fusion.32
  78.2 1.8 fusion.10
  80.0 1.7 convolution_multiply_fusion.1
  81.7 0.9 concatenate.29
  82.7 1.4 fusion
  84.0 0.3 maximum_bitcast_fusion
  84.4 5.5 %all_to_all.15 = f32[2,2,16,72,128]{4,3,1,2,0:T(8,128)S(1)} all-to-all(f32[2,2,16,72,128]{4,3,1,2,0:T(8,128)S(1)} %maximum_bitcast_fusion), channel_id=1, replica_groups=mesh['section'=8,'z'=16,'yl'=2,'core'=2] {'core'}, dimensions={0} | all-to-all | bytes 4718592 | tf_op jit(solution)/shard_map/all_to_all | solution.py:40
  89.8 0.1 fusion.29
  89.9 0.0 copy-start.11
  90.0 0.0 copy-start.10
  90.0 0.0 copy-start.9
  90.0 0.0 copy-start.5
  90.0 0.0 copy-start.7
  90.0 0.0 copy-start.8
  90.1 10.7 %all_to_all.16 = bf16[2,16,72,128]{3,2,1,0:T(8,128)(2,1)S(1)} all-to-all(bf16[2,16,72,128]{3,2,1,0:T(8,128)(2,1)S(1)} %copy.63), channel_id=1, replica_groups=mesh['section'=8,'z'=16,'yl'=2,'core'=2] {'yl'}, dimensions={0} | all-to-all | bytes 1179648 | tf_op jit(solution)/shard_map/all_to_all | solution.py:42
  100.8 0.8 fusion.30
  101.6 12.0 %all-to-all-start.2 = ((bf16[16,72,128]{2,1,0:T(8,128)(2,1)}), bf16[16,72,128]{2,1,0:T(8,128)(2,1)S(1)}, u32[]{:S(2)}, u32[]{:S(2)}) async-start(bf16[16,72,128]{2,1,0:T(8,128)(2,1)} %fusion.30), calls=%async_computation.2 | async-start | bytes 589824 | tf_op jit(solution)/shard_map/all_to_all | solution.py:44
  113.6 0.0 all-gather.15.cloned.1.call-start
  114.4 0.1 pad.2.clone
  114.5 12.4 %all-to-all-done.2 = bf16[16,72,128]{2,1,0:T(8,128)(2,1)S(1)} async-done(((bf16[16,72,128]{2,1,0:T(8,128)(2,1)}), bf16[16,72,128]{2,1,0:T(8,128)(2,1)S(1)}, u32[]{:S(2)}, u32[]{:S(2)}) %all-to-all-start.2) | async-done | bytes 294944 | tf_op jit(solution)/shard_map/all_to_all | solution.py:44
  127.0 0.7 fusion.50
  127.7 0.1 maximum_maximum_fusion.1
  127.7 28.2 %all-gather.4 = bf16[1152,128]{1,0:T(8,128)(2,1)S(1)} all-gather(bf16[72,128]{1,0:T(8,128)(2,1)S(1)} %maximum_maximum_fusion.1), channel_id=6, replica_groups=mesh['section'=8,'z'=16,'yl'=2,'core'=2] {'z'}, dimensions={0}, use_global_device_ids=true | all-gather | bytes 313344 | tf_op jit(solution)/shard_map/all_gather | solution.py:34
  155.9 6.3 %all-gather.5 = bf16[32,72,128]{2,1,0:T(8,128)(2,1)} all-gather(bf16[16,72,128]{2,1,0:T(8,128)(2,1)S(1)} %bitcast.152), channel_id=7, replica_groups=mesh['section'=8,'z'=16,'yl'=2,'core'=2] {'yl'}, dimensions={0}, use_global_device_ids=true | all-gather | bytes 884736 | tf_op jit(solution)/shard_map/all_gather | solution.py:35
  162.3 0.0 all-gather.15.cloned.1.call-update
  162.3 0.0 all-gather.13.cloned.1.call-start
  162.3 0.0 copy-done.6
  162.3 0.1 copy.57
  162.5 2.5 collective-permute-start.1
  165.0 7.1 %collective-permute-done.1 = bf16[576,128]{1,0:T(8,128)(2,1)S(1)} collective-permute-done((bf16[576,128]{1,0:T(8,128)(2,1)S(1)}, bf16[576,128]{1,0:T(8,128)(2,1)S(1)}, u32[]{:S(2)}, u32[]{:S(2)}) %collective-permute-start.1) | collective-permute-done | bytes 147488 | tf_op jit(solution)/shard_map/ppermute | solution.py:30
  172.1 0.7 copy-done.3
  172.8 0.0 all-gather.13.cloned.1.call-update
  172.8 0.1 copy.56
  172.9 0.7 pad_maximum_fusion
  173.6 1.9 collective-permute-start
  175.5 0.6 divide_subtract_fusion
  176.1 12.8 %all-gather.15.cloned.1.call-done = bf16[4,16,72,128]{3,2,1,0:T(8,128)(2,1)} async-done(((bf16[2,16,72,128]{3,2,1,0:T(8,128)(2,1)}), bf16[4,16,72,128]{3,2,1,0:T(8,128)(2,1)}) %all-gather.15.cloned.1.call-update) | async-done | bytes 1179664 | tf_op jit(solution)/shard_map/all_gather | solution.py:36
  188.9 1.4 copy.64
  190.3 1.8 fusion.9
  192.1 0.0 collective-permute-done
  192.1 131.0 %all-gather.13.cloned.1.call-done = bf16[36864,128]{1,0:T(8,128)(2,1)} async-done(((bf16[576,128]{1,0:T(8,128)(2,1)}), bf16[36864,128]{1,0:T(8,128)(2,1)}) %all-gather.13.cloned.1.call-update) | async-done | bytes 9437200 | tf_op jit(solution)/shard_map/all_gather | solution.py:79
  323.1 5.7 %convolution_convert_fusion = bf16[136,64,128]{2,0,1:T(8,128)(2,1)S(1)} fusion(bf16[64,576,128]{2,1,0:T(8,128)(2,1)} %bitcast.142, bf16[136,576]{1,0:T(8,128)(2,1)} %collective-permute-done), kind=kOutput, calls=%fused_computation.8 | convolution fusion | flops 1284571136 | bytes 11822080 | tf_op jit(solution)/shard_map/tk,bkd->tbd/dot_general | solution.py:129
  328.8 2.0 copy.58
  330.7 4.7 %broadcast_in_dim_reshape.3 = bf16[1,136,8192]{2,1,0:T(8,128)(2,1)} reshape(bf16[136,64,128]{2,1,0:T(8,128)(2,1)} %copy.58) | data formatting | bytes 4456448 | tf_op jit(solution)/shard_map/broadcast_in_dim;reshape | solution.py:132
  (27 shorter events, 0.2 us)
Async XLA Ops:
  7.2 72.8 %copy-start = (bf16[1,136,8192]{2,1,0:T(8,128)(2,1)S(1)}, bf16[1,136,8192]{2,1,0:T(8,128)(2,1)}, u32[]{:S(2)}) copy-start(bf16[1,136,8192]{2,1,0:T(8,128)(2,1)} %param.11) | copy-start | bytes 6684676
  7.2 66.6 %all-gather.11.cloned.1.call-start = ((), (), s32[]{:S(2)}) async-start(), calls=%async_computation.3 | async-start | bytes 1769472 | tf_op jit(solution)/shard_map/all_gather | solution.py:36
  12.8 36.4 %copy-start.1 = (bf16[64,128]{1,0:T(8,128)(2,1)}, bf16[64,128]{1,0:T(8,128)(2,1)S(1)}, u32[]{:S(2)}) copy-start(bf16[64,128]{1,0:T(8,128)(2,1)S(1)} %bitcast_convert_fusion) | copy-start | bytes 49156
  12.8 63.8 %copy-start.12 = (s32[1,136]{1,0:T(1,128)S(1)}, s32[1,136]{1,0:T(1,128)}, u32[]{:S(2)}) copy-start(s32[1,136]{1,0:T(1,128)} %param.13) | copy-start | bytes 1636
  89.9 24.5 %copy-start.11 = (f32[1,1,512]{2,1,0:T(1,128)S(1)}, f32[1,1,512]{2,1,0:T(1,128)}, u32[]{:S(2)}) copy-start(f32[1,1,512]{2,1,0:T(1,128)} %param.19) | copy-start | bytes 6148
  90.0 24.5 %copy-start.10 = (f32[1,1,512]{2,1,0:T(1,128)S(1)}, f32[1,1,512]{2,1,0:T(1,128)}, u32[]{:S(2)}) copy-start(f32[1,1,512]{2,1,0:T(1,128)} %param.20) | copy-start | bytes 6148
  90.0 37.0 %copy-start.9 = (f32[1,1,512]{2,1,0:T(1,128)S(1)}, f32[1,1,512]{2,1,0:T(1,128)}, u32[]{:S(2)}) copy-start(f32[1,1,512]{2,1,0:T(1,128)} %param.18) | copy-start | bytes 6148
  90.0 37.0 %copy-start.5 = (f32[1,128,64]{1,2,0:T(8,128)S(1)}, f32[1,128,64]{1,2,0:T(8,128)}, u32[]{:S(2)}) copy-start(f32[1,128,64]{1,2,0:T(8,128)} %param.15) | copy-start | bytes 98308
  90.0 37.0 %copy-start.7 = (f32[1,128,64]{1,2,0:T(8,128)S(1)}, f32[1,128,64]{1,2,0:T(8,128)}, u32[]{:S(2)}) copy-start(f32[1,128,64]{1,2,0:T(8,128)} %param.17) | copy-start | bytes 98308
  90.0 37.0 %copy-start.8 = (f32[1,128,64]{1,2,0:T(8,128)S(1)}, f32[1,128,64]{1,2,0:T(8,128)}, u32[]{:S(2)}) copy-start(f32[1,128,64]{1,2,0:T(8,128)} %param.16) | copy-start | bytes 98308
  100.8 61.6 %copy-start.6 = (bf16[1,128,512]{2,1,0:T(8,128)(2,1)S(1)}, bf16[1,128,512]{2,1,0:T(8,128)(2,1)}, u32[]{:S(2)}) copy-start(bf16[1,128,512]{2,1,0:T(8,128)(2,1)} %param.14) | copy-start | bytes 393220
  100.8 61.7 %copy-start.2 = (bf16[64,128]{1,0:T(8,128)(2,1)S(1)}, bf16[64,128]{1,0:T(8,128)(2,1)}, u32[]{:S(2)}) copy-start(bf16[64,128]{1,0:T(8,128)(2,1)} %copy-done.1) | copy-start | bytes 49156
  100.8 72.0 %copy-start.4 = (bf16[136,64]{0,1:T(8,128)(2,1)S(1)}, bf16[136,64]{0,1:T(8,128)(2,1)}, u32[]{:S(2)}) copy-start(bf16[136,64]{0,1:T(8,128)(2,1)} %fusion.10) | copy-start | bytes 52228
  101.6 25.3 %all-to-all-start.2 = ((bf16[16,72,128]{2,1,0:T(8,128)(2,1)}), bf16[16,72,128]{2,1,0:T(8,128)(2,1)S(1)}, u32[]{:S(2)}, u32[]{:S(2)}) async-start(bf16[16,72,128]{2,1,0:T(8,128)(2,1)} %fusion.30), calls=%async_computation.2 | async-start | bytes 589824 | tf_op jit(solution)/shard_map/all_to_all | solution.py:44
  113.6 75.3 %all-gather.15.cloned.1.call-start = ((), (), s32[]{:S(2)}) async-start(), calls=%async_computation.5 | async-start | bytes 1769472 | tf_op jit(solution)/shard_map/all_gather | solution.py:36
  162.3 160.8 %all-gather.13.cloned.1.call-start = ((), (), s32[]{:S(2)}) async-start(), calls=%async_computation.4 | async-start | bytes 9584640 | tf_op jit(solution)/shard_map/all_gather | solution.py:79
  162.5 9.6 %collective-permute-start.1 = (bf16[576,128]{1,0:T(8,128)(2,1)S(1)}, bf16[576,128]{1,0:T(8,128)(2,1)S(1)}, u32[]{:S(2)}, u32[]{:S(2)}) collective-permute-start(bf16[576,128]{1,0:T(8,128)(2,1)S(1)} %pad_maximum_fusion.1), channel_id=1, source_target_pairs={{64,0},{128,64},{192,128},{256,192},{320,256},{384,320},{448,384},... | collective-permute-start | bytes 442376 | tf_op jit(solution)/shard_map/ppermute | solution.py:30
  172.1 0.7 copy-start.3
  173.6 18.5 %collective-permute-start = (bf16[136,576]{1,0:T(8,128)(2,1)}, bf16[136,576]{1,0:T(8,128)(2,1)}, u32[]{:S(2)}, u32[]{:S(2)}) collective-permute-start(bf16[136,576]{1,0:T(8,128)(2,1)} %pad_maximum_fusion), channel_id=1, source_target_pairs={{64,0},{128,64},{192,128},{256,192},{320,256},{384,320},{448,384},... | collective-permute-start | bytes 470024 | tf_op jit(solution)/shard_map/ppermute | solution.py:30
Sparse Core Ops, SparseCore 0:
  49.3 24.4 all-gather.10
  162.4 26.4 all-gather.14
  191.0 131.9 all-gather.12

commit v2 on v1

v2 whole, which is shorter than its diff:
```python
import functools
import jax
import jax.numpy as jnp
from jax import lax
from jax.experimental import pallas as pl
from jax.experimental.pallas import tpu as pltpu
from jax.sharding import Mesh, PartitionSpec as P

adapter_scale = 2.0
beta_one = 0.9
beta_two = 0.999
learn_rate = 0.05
adam_eps = 1e-08

LANES = 128
EXTRA = 8
bf16 = jnp.bfloat16
f32 = jnp.float32
VMEM_BYTES = 20 * 1024 * 1024


def adam_update(master, first, second, grad, count):
    first_new = beta_one * first + (1.0 - beta_one) * grad
    second_new = beta_two * second + (1.0 - beta_two) * grad * grad
    fix_first = 1.0 - jnp.power(jnp.float32(beta_one), count)
    fix_second = 1.0 - jnp.power(jnp.float32(beta_two), count)
    master_new = master - learn_rate * (first_new / fix_first) / (
        jnp.sqrt(second_new / fix_second) + adam_eps
    )
    return (master_new, first_new, second_new)


def swap(array, axis):
    return lax.ppermute(array, axis, [(0, 1), (1, 0)])


def after(value, *others):
    return lax.optimization_barrier((value,) + others)


def spread(block):
    z = lax.axis_size("z")
    return lax.all_to_all(jnp.broadcast_to(block[None], (z,) + block.shape), "z", 0, 0)


def pad_rows(parts, rows):
    have = sum(p.shape[0] for p in parts)
    if have < rows:
        parts = parts + [jnp.zeros((rows - have, LANES), parts[0].dtype)]
    return jnp.concatenate(parts, axis=0)


def nn(a, b):
    return jnp.dot(a, b, preferred_element_type=f32)


def nt(a, b):
    return lax.dot_general(a, b, (((1,), (1,)), ((), ())), preferred_element_type=f32)


def target_of(q, core, z, rank, up_rows):
    j = q % EXTRA
    block = q // EXTRA
    half = block // (2 * z)
    yl = (block // z) % 2
    row = (block % z) * 4 + yl * 2 + jnp.where(half == 0, core, 1 - core)
    return jnp.where(j < up_rows, j * rank + row, jnp.where(j < up_rows + 2, up_rows * rank + j - up_rows, -1))


def unpack(core, halves, down, extra, rank):
    z = halves[0].shape[1]
    for half, ref in enumerate(halves):
        owner = core if half == 0 else 1 - core
        for yl in range(2):
            for i in range(z):
                at = pl.multiple_of((i * 2 + yl) * 2 * LANES + owner * LANES, LANES)
                down[:, pl.ds(at, LANES)] = ref[yl, i, :rank, :]
                row = ((half * 2 + yl) * z + i) * EXTRA
                extra[row : row + EXTRA, :] = ref[yl, i, rank:, :]


def up_rows_of(core, extra, z, rank, up_rows):
    places = up_rows * rank + 16
    shape = (places, extra.shape[0])
    q = lax.broadcasted_iota(jnp.int32, (1, shape[1]), 1)
    pick = lax.broadcasted_iota(jnp.int32, shape, 0) == target_of(q, core, z, rank, up_rows)
    found = nn(pick.astype(f32).astype(bf16), extra[...])
    up = jnp.concatenate(
        [found[k * rank : (k + 1) * rank].astype(bf16) for k in range(up_rows)], axis=1
    )
    return up, found[up_rows * rank :]


def backward_kernel(
    place, mine, other, acts, value_grad, loss_weight, keep, send, rows_out, down, extra
):
    core, yl_here = place[0], place[1]
    z = mine.shape[1]
    rank = down.shape[0]
    tokens, features = value_grad.shape
    up_rows = features // LANES
    unpack(core, (mine, other), down, extra, rank)
    up, counts = up_rows_of(core, extra, z, rank, up_rows)
    total = counts[0:1, :1] * 128.0 + counts[1:2, :1]
    weight = jnp.broadcast_to(loss_weight[...].astype(f32), (tokens, tokens))
    square = (tokens, tokens)
    diagonal = lax.broadcasted_iota(jnp.int32, square, 0) == lax.broadcasted_iota(jnp.int32, square, 1)
    share = jnp.sum(jnp.where(diagonal, weight, 0.0), axis=1, keepdims=True) / total
    scaled = (value_grad[...].astype(f32) * share).astype(bf16)
    rows_out[:, :features] = scaled
    rows_out[:, features:] = (adapter_scale * nt(scaled, up)).astype(bf16)
    mid_t = (adapter_scale * nt(up, scaled)).astype(bf16)
    low_t = nt(down[...], acts[...]).astype(bf16)

    shape = (extra.shape[0], up_rows * rank)
    q = lax.broadcasted_iota(jnp.int32, (shape[0], 1), 0)
    put = lax.broadcasted_iota(jnp.int32, shape, 1) == target_of(q, core, z, rank, up_rows)
    put = put.astype(f32).astype(bf16)
    up_grad = jnp.zeros((shape[0], LANES), f32)
    for k in range(up_rows):
        low_k = nn(put[:, k * rank : (k + 1) * rank], low_t).astype(bf16)
        up_grad = up_grad + nn(low_k, scaled[:, k * LANES : (k + 1) * LANES])
    up_grad = adapter_scale * up_grad

    for yl in range(2):
        to = jnp.bitwise_xor(yl, yl_here)
        for i in range(z):
            at = (i * 2 + yl) * 2 * LANES
            grad = nn(mid_t, acts[:, at : at + 2 * LANES])
            first, second = grad[:, :LANES], grad[:, LANES:]
            row = (yl * z + i) * EXTRA
            keep[to, i, :rank, :] = jnp.where(core == 0, first, second)
            keep[to, i, rank:, :] = up_grad[row : row + EXTRA]
            row = ((2 + yl) * z + i) * EXTRA
            send[to, i, :rank, :] = jnp.where(core == 0, second, first).astype(bf16)
            send[to, i, rank:, :] = up_grad[row : row + EXTRA].astype(bf16)


def refresh_kernel(place, mine, other, acts, out, down, extra):
    core = place[0]
    rank = down.shape[0]
    unpack(core, (mine, other), down, extra, rank)
    up, _ = up_rows_of(core, extra, mine.shape[1], rank, out.shape[1] // LANES)
    low = nt(acts[...], down[...]).astype(bf16)
    out[...] = (adapter_scale * nn(low, up)).astype(bf16)


def input_grad_kernel(place, rows, mine, other, out):
    core = place[0]
    for i in range(mine.shape[0]):
        w_mine, w_other = mine[i], other[i]
        pair = jnp.concatenate(
            [jnp.where(core == 0, w_mine, w_other), jnp.where(core == 0, w_other, w_mine)], axis=1
        )
        out[:, i * 2 * LANES : (i + 1) * 2 * LANES] = nn(rows[...], pair).astype(bf16)


def whole(n):
    return [pl.BlockSpec(memory_space=pltpu.VMEM)] * n


SCALARS = pl.BlockSpec(memory_space=pltpu.SMEM)


def per_device(
    acts,
    value_grad,
    loss_weight,
    value_weight,
    down_master,
    down_first,
    down_second,
    up_master,
    up_first,
    up_second,
    step_count,
):
    tokens, width = acts.shape[1:]
    features = value_grad.shape[2]
    rank = down_master.shape[2]
    up_rows = features // LANES
    rows = rank + EXTRA
    z, sections = lax.axis_size("z"), lax.axis_size("section")
    place = jnp.stack([lax.axis_index("core"), lax.axis_index("yl")]).astype(jnp.int32)
    params = pltpu.CompilerParams(vmem_limit_bytes=VMEM_BYTES)
    acts = acts[0]
    down_cur = down_master[0].T.astype(bf16)
    up_cur = up_master[0].astype(bf16).reshape(up_rows, LANES)

    weights = jnp.concatenate([value_weight[0].T, down_cur], axis=0)

    def from_next(flip):
        return [
            (s * 2 + (yl ^ flip), (s - 1) * 2 + yl) for s in range(1, sections) for yl in range(2)
        ]

    same = lax.ppermute(weights, ("section", "yl"), from_next(0))
    flipped = lax.ppermute(weights, ("section", "yl"), from_next(1))

    part = jnp.sum(loss_weight)
    count_rows = jnp.stack([part // 128, part % 128]).astype(bf16)[:, None] * jnp.ones((1, LANES), bf16)
    got = spread(pad_rows([down_cur, up_cur, count_rows], rows))
    got, same, flipped = after(got, same, flipped)
    even = lax.axis_index("yl") == 0
    weights = jnp.stack([jnp.where(even, same, flipped), jnp.where(even, flipped, same)])
    weights_mine = lax.all_gather(weights, "z").reshape(2 * z, features + rank, LANES)

    got = lax.all_gather(got, "yl")
    keep, send, next_rows = pl.pallas_call(
        backward_kernel,
        out_shape=(
            jax.ShapeDtypeStruct((2, z, rows, LANES), f32),
            jax.ShapeDtypeStruct((2, z, rows, LANES), bf16),
            jax.ShapeDtypeStruct((tokens, features + rank), bf16),
        ),
        in_specs=[SCALARS] + whole(5),
        out_specs=tuple(whole(3)),
        scratch_shapes=[
            pltpu.VMEM((rank, width), bf16),
            pltpu.VMEM((4 * z * EXTRA, LANES), bf16),
        ],
        compiler_params=params,
        name="backward",
    )(place, got, swap(got, "core"), acts, value_grad[0], loss_weight)
    next_rows = lax.ppermute(next_rows, "section", [(s, s - 1) for s in range(1, sections)])

    kept = keep + swap(send, "core").astype(f32)
    kept = kept[0] + swap(kept[1].astype(bf16), "yl").astype(f32)
    grad = jnp.sum(lax.all_to_all(kept.astype(bf16), "z", 0, 0).astype(f32), axis=0)

    count = step_count.astype(f32)[0]
    down_new, down_first_new, down_second_new = adam_update(
        down_master[0].T, down_first[0].T, down_second[0].T, grad[:rank], count
    )
    up_new, up_first_new, up_second_new = adam_update(
        up_master[0], up_first[0], up_second[0], grad[rank : rank + up_rows].reshape(1, features), count
    )
    got = spread(pad_rows([down_new.astype(bf16), up_new.astype(bf16).reshape(up_rows, LANES)], rows))
    got, weights_mine = after(got, weights_mine)
    weights_other = swap(weights_mine, "core")
    got = lax.all_gather(got, "yl")
    refreshed = pl.pallas_call(
        refresh_kernel,
        out_shape=jax.ShapeDtypeStruct((tokens, features), bf16),
        in_specs=[SCALARS] + whole(3),
        out_specs=whole(1)[0],
        scratch_shapes=[
            pltpu.VMEM((rank, width), bf16),
            pltpu.VMEM((4 * z * EXTRA, LANES), bf16),
        ],
        compiler_params=params,
        name="refresh",
    )(place, got, swap(got, "core"), acts)

    chunk = min(4, 2 * z)
    w_spec = pl.BlockSpec((chunk, features + rank, LANES), lambda i: (i, 0, 0))
    upstream = pl.pallas_call(
        input_grad_kernel,
        out_shape=jax.ShapeDtypeStruct((tokens, width), bf16),
        grid=(2 * z // chunk,),
        in_specs=[
            SCALARS,
            pl.BlockSpec((tokens, features + rank), lambda i: (0, 0)),
            w_spec,
            w_spec,
        ],
        out_specs=pl.BlockSpec((tokens, chunk * 2 * LANES), lambda i: (0, i)),
        compiler_params=params,
        name="input_grad",
    )(place, next_rows, weights_mine, weights_other)
    return (
        upstream[None],
        refreshed[None],
        down_new.T[None],
        down_first_new.T[None],
        down_second_new.T[None],
        up_new[None],
        up_first_new[None],
        up_second_new[None],
    )


def solution(mesh):
    sections, dp = mesh.devices.shape
    staged = Mesh(mesh.devices.reshape(sections, dp // 4, 2, 2), ("section", "z", "yl", "core"))
    split = P("section", ("z", "yl", "core"))
    return jax.shard_map(
        per_device,
        mesh=staged,
        in_specs=(split,) * 10 + (P(),),
        out_specs=(split,) * 8,
        check_vma=False,
    )
```

time: 344 us -> 189 us (0.55)
  waiting for transfers between devices: 188 us -> 45.4 us
  blocking collectives: 86.8 us -> 45.6 us
  starting transfers between devices: 16.5 us -> 57 us
  matrix products: 12.3 us -> 0 us
  Pallas kernels: 0 us -> 12.1 us
  local copies, waits for them, and re-layouts: 12.4 us -> 4.42 us
    all_gather x3 -> x1, waiting for transfers between devices: 168 us -> 2.76 us  [per_device(): lax.all_gather(weights, 'z').reshape(2 * z, features + rank, LANES)]
    all_gather x4 -> x2, blocking collectives: 70.7 us -> 16.2 us  [per_device(): got = lax.all_gather(got, 'yl')]
    ppermute x2 -> x8, starting transfers between devices: 4.39 us -> 33 us  [the longest x5 24.6 us: swap(): return lax.ppermute(array, axis, [(0, 1), (1, 0)])]
    ppermute x2 -> x8, waiting for transfers between devices: 7.12 us -> 24.1 us  [the longest x5 10.1 us: swap(): return lax.ppermute(array, axis, [(0, 1), (1, 0)])]
    all_to_all x2 -> x1, blocking collectives: 16.2 us -> 29.4 us  [spread(): lax.all_to_all(jnp.broadcast_to(block[None], (z,) + block.shape), 'z', 0, 0)]
    dot_general x5 -> x0, matrix products: 12.3 us -> none  [the longest x1 5.69 us: per_device(): jnp.einsum('tk,bkd->tbd', next_rows, weights_all, preferred_element_type=...]
    pallas_call x0 -> x3, Pallas kernels: none -> 12.1 us  [the longest x1 5.43 us: per_device(): pl.pallas_call(input_grad_kernel, out_shape=jax.ShapeDtypeStruct((tokens,...]
    all_to_all x1 -> x2, starting transfers between devices: 12 us -> 24 us  [the longest x1 14.9 us: spread(): lax.all_to_all(jnp.broadcast_to(block[None], (z,) + block.shape), 'z', 0, 0)]
  transfers between devices with their start and end apart: 6 -> 11, of which waited for: 5 -> 8; matrix products, arithmetic and copies ran while one was open for 1% -> 2% of each run, Pallas kernels for 0% -> 4%
where the time goes in v2:
time: 189 us; the launch traced here: 188 us
  starting transfers between devices  57 us (30%)
  blocking collectives  45.6 us (24%)
  waiting for transfers between devices  45.4 us (24%)
  between operations  17.7 us (9%)
  Pallas kernels  12.1 us (6%)
  other arithmetic  6.07 us (3%)
  local copies, waits for them, and re-layouts  4.42 us (2%)
    all_to_all x1, blocking collectives, spread(): lax.all_to_all(jnp.broadcast_to(block[None], (z,) + block.shape), 'z', 0, 0)  29.4 us
    ppermute x5, starting transfers between devices, swap(): return lax.ppermute(array, axis, [(0, 1), (1, 0)])  24.6 us
    all_to_all x1, waiting for transfers between devices, per_device(): lax.all_to_all(kept.astype(bf16), 'z', 0, 0).astype(f32)  18.5 us
    all_gather x2, blocking collectives, per_device(): got = lax.all_gather(got, 'yl')  16.2 us
    all_to_all x1, starting transfers between devices, spread(): lax.all_to_all(jnp.broadcast_to(block[None], (z,) + block.shape), 'z', 0, 0)  14.9 us
    ppermute x5, waiting for transfers between devices, swap(): return lax.ppermute(array, axis, [(0, 1), (1, 0)])  10.1 us
    all_to_all x1, starting transfers between devices, per_device(): lax.all_to_all(kept.astype(bf16), 'z', 0, 0).astype(f32)  9.05 us
    ppermute x1, waiting for transfers between devices, per_device(): lax.ppermute(next_rows, 'section', [(s, s - 1) for s in range(1, sections)])  5.71 us
  transfers between devices with their start and end apart: 11, of which 8 were waited for; matrix products, arithmetic and copies ran while one was open for 2% of the time, Pallas kernels for 4%

profile of v2, /device:TPU:7, one launch (start us, length us, event | category | flops | bytes accessed | tf_op | source)
XLA Modules:
  0.0 188.3 jit_solution(6896749594292298783)
XLA Ops:
  7.2 1.3 reduce_sum.18
  11.1 0.8 bitcast_convert_fusion
  11.9 0.7 convert_element_type.43
  12.6 0.1 pad_maximum_fusion.2
  12.6 0.1 pad.10.clone
  12.7 0.1 maximum_maximum_fusion
  12.8 0.8 broadcast_in_dim.38
  13.6 14.9 %all-to-all-start = ((bf16[16,72,128]{2,1,0:T(8,128)(2,1)}), bf16[16,72,128]{2,1,0:T(8,128)(2,1)S(1)}, u32[]{:S(2)}, u32[]{:S(2)}) async-start(bf16[16,72,128]{2,1,0:T(8,128)(2,1)} %broadcast_in_dim.38), calls=%async_computation | async-start | bytes 589824 | tf_op jit(solution)/shard_map/all_to_all | solution.py:43
  28.5 0.0 all-gather.5.cloned.1.call-start
  28.5 1.0 copy.20
  29.6 2.5 %collective-permute-start = (bf16[576,128]{1,0:T(8,128)(2,1)S(1)}, bf16[576,128]{1,0:T(8,128)(2,1)S(1)}, u32[]{:S(2)}, u32[]{:S(2)}) collective-permute-start(bf16[576,128]{1,0:T(8,128)(2,1)S(1)} %pad_maximum_fusion.1), channel_id=1, source_target_pairs={{64,0},{66,2},{128,64},{130,66},{192,128},{194,130},{256,192},{258... | collective-permute-start | bytes 442376 | tf_op jit(solution)/shard_map/ppermute | solution.py:197
  32.0 3.2 %collective-permute-start.1 = (bf16[576,128]{1,0:T(8,128)(2,1)S(1)}, bf16[576,128]{1,0:T(8,128)(2,1)S(1)}, u32[]{:S(2)}, u32[]{:S(2)}) collective-permute-start(bf16[576,128]{1,0:T(8,128)(2,1)S(1)} %pad_maximum_fusion.1), channel_id=1, source_target_pairs={{66,0},{64,2},{130,64},{128,66},{194,128},{192,130},{258,192},{256... | collective-permute-start | bytes 442376 | tf_op jit(solution)/shard_map/ppermute | solution.py:198
  35.2 0.0 copy-start
  35.3 0.0 copy-start.2
  35.3 0.0 copy-start.3
  35.3 4.2 %collective-permute-done = bf16[576,128]{1,0:T(8,128)(2,1)S(1)} collective-permute-done((bf16[576,128]{1,0:T(8,128)(2,1)S(1)}, bf16[576,128]{1,0:T(8,128)(2,1)S(1)}, u32[]{:S(2)}, u32[]{:S(2)}) %collective-permute-start) | collective-permute-done | bytes 147488 | tf_op jit(solution)/shard_map/ppermute | solution.py:197
  39.5 4.0 %collective-permute-done.1 = bf16[576,128]{1,0:T(8,128)(2,1)S(1)} collective-permute-done((bf16[576,128]{1,0:T(8,128)(2,1)S(1)}, bf16[576,128]{1,0:T(8,128)(2,1)S(1)}, u32[]{:S(2)}, u32[]{:S(2)}) %collective-permute-start.1) | collective-permute-done | bytes 147488 | tf_op jit(solution)/shard_map/ppermute | solution.py:198
  43.5 0.0 all-to-all-done
  43.6 0.7 pad_maximum_fusion
  44.3 0.0 all-gather.5.cloned.1.call-update
  44.3 6.3 %all-gather = bf16[32,72,128]{2,1,0:T(8,128)(2,1)S(1)} all-gather(bf16[16,72,128]{2,1,0:T(8,128)(2,1)S(1)} %all-to-all-done), channel_id=2, replica_groups=mesh['section'=8,'z'=16,'yl'=2,'core'=2] {'yl'}, dimensions={0}, use_global_device_ids=true | all-gather | bytes 884736 | tf_op jit(solution)/shard_map/all_gather | solution.py:208
  50.6 8.2 %collective-permute-start.2 = (bf16[2,16,72,128]{3,2,1,0:T(8,128)(2,1)S(1)}, bf16[2,16,72,128]{3,2,1,0:T(8,128)(2,1)S(1)}, u32[]{:S(2)}, u32[]{:S(2)}) collective-permute-start(bf16[2,16,72,128]{3,2,1,0:T(8,128)(2,1)S(1)} %bitcast.68), channel_id=1, source_target_pairs={{0,1},{1,0},{2,3},{3,2},{4,5},{5,4},{6,7},{7,6},{8,9},{9,8},{10,11... | collective-permute-start | bytes 1769480 | tf_op jit(solution)/shard_map/ppermute | solution.py:34
  58.8 0.1 pad_add_fusion.place
  58.9 1.5 collective-permute-done.2.other
  60.4 0.0 copy-done
  60.4 0.0 copy-done.2
  60.4 0.0 copy-done.3
  60.4 4.2 %backward.1 = (f32[2,16,72,128]{3,2,1,0:T(8,128)S(1)}, bf16[2,16,72,128]{3,2,1,0:T(8,128)(2,1)S(1)}, bf16[136,576]{1,0:T(8,128)(2,1)S(1)}) custom-call(s32[2]{0:T(128)S(1)} %pad_add_fusion.place, bf16[2,16,72,128]{3,2,1,0:T(8,128)(2,1)S(1)} %bitcast.69, bf16[2,16,72,128]{3,2,1,0:T(8,128)(2,1)S(1)} %collective-permute-done.2.other, ...), custom_call_target="tpu_custom_call" | custom-call | tf_op jit(solution)/shard_map/backward/pallas_call | solution.py:209
  64.7 0.0 copy-start.4
  64.7 2.3 %collective-permute-start.4 = (bf16[2,16,72,128]{3,2,1,0:T(8,128)(2,1)S(1)}, bf16[2,16,72,128]{3,2,1,0:T(8,128)(2,1)S(1)}, u32[]{:S(2)}, u32[]{:S(2)}) collective-permute-start(bf16[2,16,72,128]{3,2,1,0:T(8,128)(2,1)S(1)} %get-tuple-element.19), channel_id=1, source_target_pairs={{0,1},{1,0},{2,3},{3,2},{4,5},{5,4},{6,7},{7,6},{8,9},{9,8},{10,11... | collective-permute-start | bytes 1769480 | tf_op jit(solution)/shard_map/ppermute | solution.py:34
  67.0 1.6 collective-permute-done.4
  68.6 0.1 convert_add_fusion
  68.7 0.0 copy-done.4
  68.7 0.0 copy-start.11
  68.7 0.0 copy-start.10
  68.8 0.0 copy-start.9
  68.8 0.0 copy-start.6
  68.8 0.0 copy-start.7
  68.8 0.0 copy-start.8
  68.8 3.3 %collective-permute-start.5 = (bf16[16,72,128]{2,1,0:T(8,128)(2,1)S(1)}, bf16[16,72,128]{2,1,0:T(8,128)(2,1)S(1)}, u32[]{:S(2)}, u32[]{:S(2)}) collective-permute-start(bf16[16,72,128]{2,1,0:T(8,128)(2,1)S(1)} %fusion.2), channel_id=1, source_target_pairs={{0,2},{2,0},{1,3},{3,1},{4,6},{6,4},{5,7},{7,5},{8,10},{10,8},{9,1... | collective-permute-start | bytes 884744 | tf_op jit(solution)/shard_map/ppermute | solution.py:34
  72.2 7.0 %collective-permute-done.5 = bf16[16,72,128]{2,1,0:T(8,128)(2,1)S(1)} collective-permute-done((bf16[16,72,128]{2,1,0:T(8,128)(2,1)S(1)}, bf16[16,72,128]{2,1,0:T(8,128)(2,1)S(1)}, u32[]{:S(2)}, u32[]{:S(2)}) %collective-permute-start.5) | collective-permute-done | bytes 294944 | tf_op jit(solution)/shard_map/ppermute | solution.py:34
  79.2 0.8 fusion.1
  79.9 9.0 %all-to-all-start.1 = ((bf16[16,72,128]{2,1,0:T(8,128)(2,1)}), bf16[16,72,128]{2,1,0:T(8,128)(2,1)S(1)}, u32[]{:S(2)}, u32[]{:S(2)}) async-start(bf16[16,72,128]{2,1,0:T(8,128)(2,1)} %fusion.1), calls=%async_computation.1 | async-start | bytes 589824 | tf_op jit(solution)/shard_map/all_to_all | solution.py:229
  89.7 0.1 pad.4.clone
  89.8 0.0 copy-done.11
  89.8 0.0 copy-done.10
  89.8 0.0 copy-start.5
  89.8 18.5 %all-to-all-done.1 = bf16[16,72,128]{2,1,0:T(8,128)(2,1)S(1)} async-done(((bf16[16,72,128]{2,1,0:T(8,128)(2,1)}), bf16[16,72,128]{2,1,0:T(8,128)(2,1)S(1)}, u32[]{:S(2)}, u32[]{:S(2)}) %all-to-all-start.1) | async-done | bytes 294944 | tf_op jit(solution)/shard_map/all_to_all | solution.py:229
  108.4 0.0 copy-done.9
  108.5 0.7 fusion.10
  109.1 0.1 maximum_maximum_fusion.1
  109.3 29.4 %all_to_all.15 = bf16[16,72,128]{2,1,0:T(8,128)(2,1)S(1)} all-to-all(bf16[16,72,128]{2,1,0:T(8,128)(2,1)S(1)} %broadcast_in_dim.40), channel_id=1, replica_groups=mesh['section'=8,'z'=16,'yl'=2,'core'=2] {'z'}, dimensions={0} | all-to-all | bytes 589824 | tf_op jit(solution)/shard_map/all_to_all | solution.py:43
  138.6 2.8 %all-gather.5.cloned.1.call-done.mine = bf16[32,576,128]{2,1,0:T(8,128)(2,1)} async-done(((bf16[2,576,128]{2,1,0:T(8,128)(2,1)}), bf16[32,576,128]{2,1,0:T(8,128)(2,1)}) %all-gather.5.cloned.1.call-update) | async-done | bytes 4718608 | tf_op jit(solution)/shard_map/all_gather | solution.py:206
  141.4 8.3 %collective-permute-start.6 = (bf16[32,576,128]{2,1,0:T(8,128)(2,1)}, bf16[32,576,128]{2,1,0:T(8,128)(2,1)S(1)}, u32[]{:S(2)}, u32[]{:S(2)}) collective-permute-start(bf16[32,576,128]{2,1,0:T(8,128)(2,1)} %all-gather.5.cloned.1.call-done.mine), channel_id=1, source_target_pairs={{0,1},{1,0},{2,3},{3,2},{4,5},{5,4},{6,7},{7,6},{8,9},{9,8},{10,11... | collective-permute-start | bytes 14155784 | tf_op jit(solution)/shard_map/ppermute | solution.py:34
  149.7 9.9 %all-gather.2 = bf16[32,72,128]{2,1,0:T(8,128)(2,1)S(1)} all-gather(bf16[16,72,128]{2,1,0:T(8,128)(2,1)S(1)} %all_to_all.15), channel_id=4, replica_groups=mesh['section'=8,'z'=16,'yl'=2,'core'=2] {'yl'}, dimensions={0}, use_global_device_ids=true | all-gather | bytes 884736 | tf_op jit(solution)/shard_map/all_gather | solution.py:241
  159.6 2.5 %collective-permute-start.7 = (bf16[2,16,72,128]{3,2,1,0:T(8,128)(2,1)S(1)}, bf16[2,16,72,128]{3,2,1,0:T(8,128)(2,1)S(1)}, u32[]{:S(2)}, u32[]{:S(2)}) collective-permute-start(bf16[2,16,72,128]{3,2,1,0:T(8,128)(2,1)S(1)} %bitcast.70), channel_id=1, source_target_pairs={{0,1},{1,0},{2,3},{3,2},{4,5},{5,4},{6,7},{7,6},{8,9},{9,8},{10,11... | collective-permute-start | bytes 1769480 | tf_op jit(solution)/shard_map/ppermute | solution.py:34
  162.1 2.8 %collective-permute-start.3 = (bf16[136,576]{1,0:T(8,128)(2,1)S(1)}, bf16[136,576]{1,0:T(8,128)(2,1)S(1)}, u32[]{:S(2)}, u32[]{:S(2)}) collective-permute-start(bf16[136,576]{1,0:T(8,128)(2,1)S(1)} %copy-done.5), channel_id=1, source_target_pairs={{64,0},{128,64},{192,128},{256,192},{320,256},{384,320},{448,384},... | collective-permute-start | bytes 470024 | tf_op jit(solution)/shard_map/ppermute | solution.py:225
  164.9 0.6 divide_subtract_fusion
  165.5 0.0 collective-permute-done.7.other
  165.5 2.5 %refresh.1 = bf16[136,512]{1,0:T(8,128)(2,1)} custom-call(s32[2]{0:T(128)S(1)} %pad_add_fusion.place, bf16[2,16,72,128]{3,2,1,0:T(8,128)(2,1)S(1)} %bitcast.71, bf16[2,16,72,128]{3,2,1,0:T(8,128)(2,1)S(1)} %collective-permute-done.7.other, bf16[136,8192]{1,0:T(8,128)(2,1)S(1)} %bitcast.67), custom_call_target="tpu_custom_call" | custom-call | tf_op jit(solution)/shard_map/refresh/pallas_call | solution.py:242
  168.0 5.7 %collective-permute-done.3.rows = bf16[136,576]{1,0:T(8,128)(2,1)S(1)} collective-permute-done((bf16[136,576]{1,0:T(8,128)(2,1)S(1)}, bf16[136,576]{1,0:T(8,128)(2,1)S(1)}, u32[]{:S(2)}, u32[]{:S(2)}) %collective-permute-start.3) | collective-permute-done | bytes 156704 | tf_op jit(solution)/shard_map/ppermute | solution.py:225
  173.7 0.0 collective-permute-done.6.other
  173.7 2.3 %copy-done.1 = bf16[32,576,128]{2,1,0:T(8,128)(2,1)S(1)} copy-done((bf16[32,576,128]{2,1,0:T(8,128)(2,1)S(1)}, bf16[32,576,128]{2,1,0:T(8,128)(2,1)}, u32[]{:S(2)}) %copy-start.1) | copy-done | bytes 4718616
  176.0 5.4 %input_grad.1 = bf16[136,8192]{1,0:T(8,128)(2,1)} custom-call(s32[2]{0:T(128)S(1)} %pad_add_fusion.place, bf16[136,576]{1,0:T(8,128)(2,1)S(1)} %collective-permute-done.3.rows, bf16[32,576,128]{2,1,0:T(8,128)(2,1)S(1)} %copy-done.1, bf16[32,576,128]{2,1,0:T(8,128)(2,1)S(1)} %collective-permute-done.6.other), custom_call_target="tpu_custom_call" | custom-call | tf_op jit(solution)/shard_map/input_grad/pallas_call | solution.py:257
  (15 shorter events, 0.2 us)
Async XLA Ops:
  13.6 30.0 %all-to-all-start = ((bf16[16,72,128]{2,1,0:T(8,128)(2,1)}), bf16[16,72,128]{2,1,0:T(8,128)(2,1)S(1)}, u32[]{:S(2)}, u32[]{:S(2)}) async-start(bf16[16,72,128]{2,1,0:T(8,128)(2,1)} %broadcast_in_dim.38), calls=%async_computation | async-start | bytes 589824 | tf_op jit(solution)/shard_map/all_to_all | solution.py:43
  28.5 112.9 %all-gather.5.cloned.1.call-start = ((), (), s32[]{:S(2)}) async-start(), calls=%async_computation.3 | async-start | bytes 5013504 | tf_op jit(solution)/shard_map/all_gather | solution.py:206
  29.6 9.9 %collective-permute-start = (bf16[576,128]{1,0:T(8,128)(2,1)S(1)}, bf16[576,128]{1,0:T(8,128)(2,1)S(1)}, u32[]{:S(2)}, u32[]{:S(2)}) collective-permute-start(bf16[576,128]{1,0:T(8,128)(2,1)S(1)} %pad_maximum_fusion.1), channel_id=1, source_target_pairs={{64,0},{66,2},{128,64},{130,66},{192,128},{194,130},{256,192},{258... | collective-permute-start | bytes 442376 | tf_op jit(solution)/shard_map/ppermute | solution.py:197
  32.0 11.5 %collective-permute-start.1 = (bf16[576,128]{1,0:T(8,128)(2,1)S(1)}, bf16[576,128]{1,0:T(8,128)(2,1)S(1)}, u32[]{:S(2)}, u32[]{:S(2)}) collective-permute-start(bf16[576,128]{1,0:T(8,128)(2,1)S(1)} %pad_maximum_fusion.1), channel_id=1, source_target_pairs={{66,0},{64,2},{130,64},{128,66},{194,128},{192,130},{258,192},{256... | collective-permute-start | bytes 442376 | tf_op jit(solution)/shard_map/ppermute | solution.py:198
  35.2 25.2 %copy-start = (bf16[1,136,8192]{2,1,0:T(8,128)(2,1)S(1)}, bf16[1,136,8192]{2,1,0:T(8,128)(2,1)}, u32[]{:S(2)}) copy-start(bf16[1,136,8192]{2,1,0:T(8,128)(2,1)} %param.11) | copy-start | bytes 6684676
  35.3 25.2 %copy-start.2 = (bf16[1,136,512]{2,1,0:T(8,128)(2,1)S(1)}, bf16[1,136,512]{2,1,0:T(8,128)(2,1)}, u32[]{:S(2)}) copy-start(bf16[1,136,512]{2,1,0:T(8,128)(2,1)} %param.12) | copy-start | bytes 417796
  35.3 25.2 %copy-start.3 = (s32[1,136]{1,0:T(1,128)S(1)}, s32[1,136]{1,0:T(1,128)}, u32[]{:S(2)}) copy-start(s32[1,136]{1,0:T(1,128)} %loss_weight.1) | copy-start | bytes 1636
  50.6 9.8 %collective-permute-start.2 = (bf16[2,16,72,128]{3,2,1,0:T(8,128)(2,1)S(1)}, bf16[2,16,72,128]{3,2,1,0:T(8,128)(2,1)S(1)}, u32[]{:S(2)}, u32[]{:S(2)}) collective-permute-start(bf16[2,16,72,128]{3,2,1,0:T(8,128)(2,1)S(1)} %bitcast.68), channel_id=1, source_target_pairs={{0,1},{1,0},{2,3},{3,2},{4,5},{5,4},{6,7},{7,6},{8,9},{9,8},{10,11... | collective-permute-start | bytes 1769480 | tf_op jit(solution)/shard_map/ppermute | solution.py:34
  64.7 4.0 %copy-start.4 = (bf16[136,576]{1,0:T(8,128)(2,1)}, bf16[136,576]{1,0:T(8,128)(2,1)S(1)}, u32[]{:S(2)}) copy-start(bf16[136,576]{1,0:T(8,128)(2,1)S(1)} %get-tuple-element.17) | copy-start | bytes 470020
  64.7 3.9 %collective-permute-start.4 = (bf16[2,16,72,128]{3,2,1,0:T(8,128)(2,1)S(1)}, bf16[2,16,72,128]{3,2,1,0:T(8,128)(2,1)S(1)}, u32[]{:S(2)}, u32[]{:S(2)}) collective-permute-start(bf16[2,16,72,128]{3,2,1,0:T(8,128)(2,1)S(1)} %get-tuple-element.19), channel_id=1, source_target_pairs={{0,1},{1,0},{2,3},{3,2},{4,5},{5,4},{6,7},{7,6},{8,9},{9,8},{10,11... | collective-permute-start | bytes 1769480 | tf_op jit(solution)/shard_map/ppermute | solution.py:34
  68.7 21.1 %copy-start.11 = (f32[1,1,512]{2,1,0:T(1,128)S(1)}, f32[1,1,512]{2,1,0:T(1,128)}, u32[]{:S(2)}) copy-start(f32[1,1,512]{2,1,0:T(1,128)} %param.19) | copy-start | bytes 6148
  68.7 21.1 %copy-start.10 = (f32[1,1,512]{2,1,0:T(1,128)S(1)}, f32[1,1,512]{2,1,0:T(1,128)}, u32[]{:S(2)}) copy-start(f32[1,1,512]{2,1,0:T(1,128)} %param.20) | copy-start | bytes 6148
  68.8 39.7 %copy-start.9 = (f32[1,1,512]{2,1,0:T(1,128)S(1)}, f32[1,1,512]{2,1,0:T(1,128)}, u32[]{:S(2)}) copy-start(f32[1,1,512]{2,1,0:T(1,128)} %param.18) | copy-start | bytes 6148
  68.8 39.7 %copy-start.6 = (f32[1,128,64]{1,2,0:T(8,128)S(1)}, f32[1,128,64]{1,2,0:T(8,128)}, u32[]{:S(2)}) copy-start(f32[1,128,64]{1,2,0:T(8,128)} %param.15) | copy-start | bytes 98308
  68.8 39.7 %copy-start.7 = (f32[1,128,64]{1,2,0:T(8,128)S(1)}, f32[1,128,64]{1,2,0:T(8,128)}, u32[]{:S(2)}) copy-start(f32[1,128,64]{1,2,0:T(8,128)} %param.17) | copy-start | bytes 98308
  68.8 39.7 %copy-start.8 = (f32[1,128,64]{1,2,0:T(8,128)S(1)}, f32[1,128,64]{1,2,0:T(8,128)}, u32[]{:S(2)}) copy-start(f32[1,128,64]{1,2,0:T(8,128)} %param.16) | copy-start | bytes 98308
  68.8 10.4 %collective-permute-start.5 = (bf16[16,72,128]{2,1,0:T(8,128)(2,1)S(1)}, bf16[16,72,128]{2,1,0:T(8,128)(2,1)S(1)}, u32[]{:S(2)}, u32[]{:S(2)}) collective-permute-start(bf16[16,72,128]{2,1,0:T(8,128)(2,1)S(1)} %fusion.2), channel_id=1, source_target_pairs={{0,2},{2,0},{1,3},{3,1},{4,6},{6,4},{5,7},{7,5},{8,10},{10,8},{9,1... | collective-permute-start | bytes 884744 | tf_op jit(solution)/shard_map/ppermute | solution.py:34
  79.9 28.4 %all-to-all-start.1 = ((bf16[16,72,128]{2,1,0:T(8,128)(2,1)}), bf16[16,72,128]{2,1,0:T(8,128)(2,1)S(1)}, u32[]{:S(2)}, u32[]{:S(2)}) async-start(bf16[16,72,128]{2,1,0:T(8,128)(2,1)} %fusion.1), calls=%async_computation.1 | async-start | bytes 589824 | tf_op jit(solution)/shard_map/all_to_all | solution.py:229
  89.8 72.3 %copy-start.5 = (bf16[136,576]{1,0:T(8,128)(2,1)S(1)}, bf16[136,576]{1,0:T(8,128)(2,1)}, u32[]{:S(2)}) copy-start(bf16[136,576]{1,0:T(8,128)(2,1)} %copy-done.4) | copy-start | bytes 470020
  141.4 32.3 %collective-permute-start.6 = (bf16[32,576,128]{2,1,0:T(8,128)(2,1)}, bf16[32,576,128]{2,1,0:T(8,128)(2,1)S(1)}, u32[]{:S(2)}, u32[]{:S(2)}) collective-permute-start(bf16[32,576,128]{2,1,0:T(8,128)(2,1)} %all-gather.5.cloned.1.call-done.mine), channel_id=1, source_target_pairs={{0,1},{1,0},{2,3},{3,2},{4,5},{5,4},{6,7},{7,6},{8,9},{9,8},{10,11... | collective-permute-start | bytes 14155784 | tf_op jit(solution)/shard_map/ppermute | solution.py:34
  159.6 5.9 %collective-permute-start.7 = (bf16[2,16,72,128]{3,2,1,0:T(8,128)(2,1)S(1)}, bf16[2,16,72,128]{3,2,1,0:T(8,128)(2,1)S(1)}, u32[]{:S(2)}, u32[]{:S(2)}) collective-permute-start(bf16[2,16,72,128]{3,2,1,0:T(8,128)(2,1)S(1)} %bitcast.70), channel_id=1, source_target_pairs={{0,1},{1,0},{2,3},{3,2},{4,5},{5,4},{6,7},{7,6},{8,9},{9,8},{10,11... | collective-permute-start | bytes 1769480 | tf_op jit(solution)/shard_map/ppermute | solution.py:34
  162.1 11.5 %collective-permute-start.3 = (bf16[136,576]{1,0:T(8,128)(2,1)S(1)}, bf16[136,576]{1,0:T(8,128)(2,1)S(1)}, u32[]{:S(2)}, u32[]{:S(2)}) collective-permute-start(bf16[136,576]{1,0:T(8,128)(2,1)S(1)} %copy-done.5), channel_id=1, source_target_pairs={{64,0},{128,64},{192,128},{256,192},{320,256},{384,320},{448,384},... | collective-permute-start | bytes 470024 | tf_op jit(solution)/shard_map/ppermute | solution.py:225
  173.7 2.3 %copy-start.1 = (bf16[32,576,128]{2,1,0:T(8,128)(2,1)S(1)}, bf16[32,576,128]{2,1,0:T(8,128)(2,1)}, u32[]{:S(2)}) copy-start(bf16[32,576,128]{2,1,0:T(8,128)(2,1)} %all-gather.5.cloned.1.call-done.mine) | copy-start | bytes 14155780
Sparse Core Ops, SparseCore 0:
  44.5 96.9 all-gather.4

commit v3 on v2

v3 whole, which is shorter than its diff:
```python
import jax
import jax.numpy as jnp
from jax import lax
from jax.experimental import pallas as pl
from jax.experimental.pallas import tpu as pltpu
from jax.sharding import Mesh, PartitionSpec as P

adapter_scale = 2.0
beta_one = 0.9
beta_two = 0.999
learn_rate = 0.05
adam_eps = 1e-08

LANES = 128
EXTRA = 8
bf16 = jnp.bfloat16
f32 = jnp.float32
VMEM_BYTES = 20 * 1024 * 1024


def adam_update(master, first, second, grad, count):
    first_new = beta_one * first + (1.0 - beta_one) * grad
    second_new = beta_two * second + (1.0 - beta_two) * grad * grad
    fix_first = 1.0 - jnp.power(jnp.float32(beta_one), count)
    fix_second = 1.0 - jnp.power(jnp.float32(beta_two), count)
    master_new = master - learn_rate * (first_new / fix_first) / (
        jnp.sqrt(second_new / fix_second) + adam_eps
    )
    return (master_new, first_new, second_new)


def swap(array, axis):
    return lax.ppermute(array, axis, [(0, 1), (1, 0)])


def quarters(got, beside=None):
    got_yl = swap(got, "yl")
    got_yl, beside = after(got_yl, beside)
    return (got, got_yl, swap(got, "core"), swap(got_yl, "core")), beside


def after(value, *others):
    return lax.optimization_barrier((value,) + others)


def spread(copies):
    return lax.all_to_all(copies, "z", 0, 0)


def pad_rows(parts, rows):
    have = sum(p.shape[0] for p in parts)
    if have < rows:
        parts = parts + [jnp.zeros((rows - have, LANES), parts[0].dtype)]
    return jnp.concatenate(parts, axis=0)


def nn(a, b):
    return jnp.dot(a, b, preferred_element_type=f32)


def nt(a, b):
    return lax.dot_general(a, b, (((1,), (1,)), ((), ())), preferred_element_type=f32)


def target_of(q, core, yl, z, rank, up_rows):
    j = q % EXTRA
    block = q // EXTRA
    of_core = jnp.where(block // (2 * z) == 0, core, 1 - core)
    of_yl = jnp.where((block // z) % 2 == 0, yl, 1 - yl)
    row = (block % z) * 4 + of_yl * 2 + of_core
    return jnp.where(j < up_rows, j * rank + row, jnp.where(j < up_rows + 2, up_rows * rank + j - up_rows, -1))


def unpack(core, yl, quarters, down, extra, rank):
    z = quarters[0].shape[0]
    for quarter, ref in enumerate(quarters):
        of_core = core if quarter < 2 else 1 - core
        of_yl = yl if quarter % 2 == 0 else 1 - yl
        offset = (of_yl * 2 + of_core) * LANES
        for i in range(z):
            at = pl.multiple_of(i * 4 * LANES + offset, LANES)
            down[:, pl.ds(at, LANES)] = ref[i, :rank, :]
            row = (quarter * z + i) * EXTRA
            extra[row : row + EXTRA, :] = ref[i, rank:, :]


def up_rows_of(core, yl, extra, z, rank, up_rows):
    places = up_rows * rank + 16
    shape = (places, extra.shape[0])
    q = lax.broadcasted_iota(jnp.int32, (1, shape[1]), 1)
    pick = lax.broadcasted_iota(jnp.int32, shape, 0) == target_of(q, core, yl, z, rank, up_rows)
    found = nn(pick.astype(f32).astype(bf16), extra[...])
    up = jnp.concatenate(
        [found[k * rank : (k + 1) * rank].astype(bf16) for k in range(up_rows)], axis=1
    )
    return up, found[up_rows * rank :]


def prepare_kernel(down_master, up_master, loss_weight, value_weight, copies, weights):
    rank = down_master.shape[0]
    features = up_master.shape[1]
    down = down_master[...].astype(bf16)
    count = jnp.sum(loss_weight[...].astype(f32), axis=1, keepdims=True)
    high = jnp.floor(count / 128.0)
    parts = [up_master[:, at : at + LANES] for at in range(0, features, LANES)]
    parts += [jnp.broadcast_to(c, (1, LANES)) for c in (high, count - 128.0 * high)]
    parts.append(jnp.zeros((EXTRA - len(parts), LANES), f32))
    extra = jnp.concatenate(parts, axis=0).astype(bf16)
    for i in range(copies.shape[0]):
        copies[i, :rank, :] = down
        copies[i, rank:, :] = extra
    weights[:features, :] = value_weight[...].astype(f32).T.astype(bf16)
    weights[features:, :] = down


def backward_kernel(
    place, q0, q1, q2, q3, acts, value_grad, loss_weight, keep, send, rows_out, down, extra
):
    core, yl = place[0], place[1]
    z = q0.shape[0]
    rank = down.shape[0]
    tokens, features = value_grad.shape
    up_rows = features // LANES
    unpack(core, yl, (q0, q1, q2, q3), down, extra, rank)
    up, counts = up_rows_of(core, yl, extra, z, rank, up_rows)
    total = counts[0:1, :1] * 128.0 + counts[1:2, :1]
    weight = jnp.broadcast_to(loss_weight[...].astype(f32), (tokens, tokens))
    square = (tokens, tokens)
    diagonal = lax.broadcasted_iota(jnp.int32, square, 0) == lax.broadcasted_iota(jnp.int32, square, 1)
    share = jnp.sum(jnp.where(diagonal, weight, 0.0), axis=1, keepdims=True) / total
    scaled = (value_grad[...].astype(f32) * share).astype(bf16)
    rows_out[:, :features] = scaled
    rows_out[:, features:] = (adapter_scale * nt(scaled, up)).astype(bf16)
    mid_t = (adapter_scale * nt(up, scaled)).astype(bf16)
    low_t = nt(down[...], acts[...]).astype(bf16)

    shape = (extra.shape[0], up_rows * rank)
    q = lax.broadcasted_iota(jnp.int32, (shape[0], 1), 0)
    put = lax.broadcasted_iota(jnp.int32, shape, 1) == target_of(q, core, yl, z, rank, up_rows)
    put = put.astype(f32).astype(bf16)
    up_grad = jnp.zeros((shape[0], LANES), f32)
    for k in range(up_rows):
        low_k = nn(put[:, k * rank : (k + 1) * rank], low_t).astype(bf16)
        up_grad = up_grad + nn(low_k, scaled[:, k * LANES : (k + 1) * LANES])
    up_grad = adapter_scale * up_grad

    for half in range(2):
        of_yl = yl if half == 0 else 1 - yl
        for i in range(z):
            at = pl.multiple_of(i * 4 * LANES + of_yl * 2 * LANES, 2 * LANES)
            grad = nn(mid_t, acts[:, pl.ds(at, 2 * LANES)])
            first, second = grad[:, :LANES], grad[:, LANES:]
            row = (half * z + i) * EXTRA
            keep[half, i, :rank, :] = jnp.where(core == 0, first, second)
            keep[half, i, rank:, :] = up_grad[row : row + EXTRA]
            row = ((2 + half) * z + i) * EXTRA
            send[half, i, :rank, :] = jnp.where(core == 0, second, first).astype(bf16)
            send[half, i, rank:, :] = up_grad[row : row + EXTRA].astype(bf16)


def refresh_kernel(place, q0, q1, q2, q3, acts, out, down, extra):
    core, yl = place[0], place[1]
    rank = down.shape[0]
    unpack(core, yl, (q0, q1, q2, q3), down, extra, rank)
    up, _ = up_rows_of(core, yl, extra, q0.shape[0], rank, out.shape[1] // LANES)
    low = nt(acts[...], down[...]).astype(bf16)
    out[...] = (adapter_scale * nn(low, up)).astype(bf16)


def side_by_side(blocks):
    return jnp.concatenate([blocks[i] for i in range(blocks.shape[0])], axis=1)


def own_columns_kernel(rows, weights, out):
    out[...] = nn(rows[...], side_by_side(weights)).astype(bf16)


def all_columns_kernel(place, rows, weights, mine, out):
    core = place[0]
    other = nn(rows[...], side_by_side(weights)).astype(bf16)
    for i in range(weights.shape[0]):
        at = i * 2 * LANES
        a, b = mine[:, i * LANES : (i + 1) * LANES], other[:, i * LANES : (i + 1) * LANES]
        out[:, at : at + LANES] = jnp.where(core == 0, a, b)
        out[:, at + LANES : at + 2 * LANES] = jnp.where(core == 0, b, a)


def whole(n):
    return [pl.BlockSpec(memory_space=pltpu.VMEM)] * n


SCALARS = pl.BlockSpec(memory_space=pltpu.SMEM)


def per_device(
    acts,
    value_grad,
    loss_weight,
    value_weight,
    down_master,
    down_first,
    down_second,
    up_master,
    up_first,
    up_second,
    step_count,
):
    tokens, width = acts.shape[1:]
    features = value_grad.shape[2]
    rank = down_master.shape[2]
    up_rows = features // LANES
    rows = rank + EXTRA
    z, sections = lax.axis_size("z"), lax.axis_size("section")
    place = jnp.stack([lax.axis_index("core"), lax.axis_index("yl")]).astype(jnp.int32)
    params = pltpu.CompilerParams(vmem_limit_bytes=VMEM_BYTES)
    acts = acts[0]
    copies, weights = pl.pallas_call(
        prepare_kernel,
        out_shape=(
            jax.ShapeDtypeStruct((z, rows, LANES), bf16),
            jax.ShapeDtypeStruct((features + rank, LANES), bf16),
        ),
        in_specs=whole(4),
        out_specs=tuple(whole(2)),
        compiler_params=params,
        name="prepare",
    )(down_master[0].T, up_master[0], loss_weight, value_weight[0])

    def from_next(flip):
        return [
            (s * 2 + (yl ^ flip), (s - 1) * 2 + yl) for s in range(1, sections) for yl in range(2)
        ]

    same = lax.ppermute(weights, ("section", "yl"), from_next(0))
    flipped = lax.ppermute(weights, ("section", "yl"), from_next(1))

    got = spread(copies)
    got, same, flipped = after(got, same, flipped)
    even = lax.axis_index("yl") == 0
    weights = jnp.stack([jnp.where(even, same, flipped), jnp.where(even, flipped, same)])
    weights_mine = lax.all_gather(weights, "z").reshape(2 * z, features + rank, LANES)

    blocks, _ = quarters(got)
    keep, send, next_rows = pl.pallas_call(
        backward_kernel,
        out_shape=(
            jax.ShapeDtypeStruct((2, z, rows, LANES), f32),
            jax.ShapeDtypeStruct((2, z, rows, LANES), bf16),
            jax.ShapeDtypeStruct((tokens, features + rank), bf16),
        ),
        in_specs=[SCALARS] + whole(7),
        out_specs=tuple(whole(3)),
        scratch_shapes=[
            pltpu.VMEM((rank, width), bf16),
            pltpu.VMEM((4 * z * EXTRA, LANES), bf16),
        ],
        compiler_params=params,
        name="backward",
    )(place, *blocks, acts, value_grad[0], loss_weight)
    next_rows = lax.ppermute(next_rows, "section", [(s, s - 1) for s in range(1, sections)])

    kept = keep + swap(send, "core").astype(f32)
    kept = kept[0] + swap(kept[1].astype(bf16), "yl").astype(f32)
    parts, next_rows = after(lax.all_to_all(kept.astype(bf16), "z", 0, 0), next_rows)
    grad = jnp.sum(parts.astype(f32), axis=0)

    count = step_count.astype(f32)[0]
    down_new, down_first_new, down_second_new = adam_update(
        down_master[0].T, down_first[0].T, down_second[0].T, grad[:rank], count
    )
    up_new, up_first_new, up_second_new = adam_update(
        up_master[0], up_first[0], up_second[0], grad[rank : rank + up_rows].reshape(1, features), count
    )
    block = pad_rows([down_new.astype(bf16), up_new.astype(bf16).reshape(up_rows, LANES)], rows)
    got = spread(jnp.broadcast_to(block[None], (z, rows, LANES)))
    got, weights_mine = after(got, weights_mine)
    weights_other = swap(weights_mine, "core")
    chunk = min(4, 2 * z)
    rows_spec = pl.BlockSpec((tokens, features + rank), lambda i: (0, 0))
    w_spec = pl.BlockSpec((chunk, features + rank, LANES), lambda i: (i, 0, 0))
    half_spec = pl.BlockSpec((tokens, chunk * LANES), lambda i: (0, i))
    own_columns = pl.pallas_call(
        own_columns_kernel,
        out_shape=jax.ShapeDtypeStruct((tokens, width // 2), bf16),
        grid=(2 * z // chunk,),
        in_specs=[rows_spec, w_spec],
        out_specs=half_spec,
        compiler_params=pltpu.CompilerParams(vmem_limit_bytes=56 * 1024 * 1024),
        cost_estimate=pl.CostEstimate(
            flops=tokens * (features + rank) * width,
            bytes_accessed=(features + rank) * width + tokens * width,
            transcendentals=0,
        ),
        name="own_columns",
    )(next_rows, weights_mine)
    blocks, own_columns = quarters(got, own_columns)
    refreshed = pl.pallas_call(
        refresh_kernel,
        out_shape=jax.ShapeDtypeStruct((tokens, features), bf16),
        in_specs=[SCALARS] + whole(5),
        out_specs=whole(1)[0],
        scratch_shapes=[
            pltpu.VMEM((rank, width), bf16),
            pltpu.VMEM((4 * z * EXTRA, LANES), bf16),
        ],
        compiler_params=params,
        name="refresh",
    )(place, *blocks, acts)

    upstream = pl.pallas_call(
        all_columns_kernel,
        out_shape=jax.ShapeDtypeStruct((tokens, width), bf16),
        grid=(2 * z // chunk,),
        in_specs=[SCALARS, rows_spec, w_spec, half_spec],
        out_specs=pl.BlockSpec((tokens, chunk * 2 * LANES), lambda i: (0, i)),
        compiler_params=params,
        name="all_columns",
    )(place, next_rows, weights_other, own_columns)
    return (
        upstream[None],
        refreshed[None],
        down_new.T[None],
        down_first_new.T[None],
        down_second_new.T[None],
        up_new[None],
        up_first_new[None],
        up_second_new[None],
    )


def solution(mesh):
    sections, dp = mesh.devices.shape
    staged = Mesh(mesh.devices.reshape(sections, dp // 4, 2, 2), ("section", "z", "yl", "core"))
    split = P("section", ("z", "yl", "core"))
    return jax.shard_map(
        per_device,
        mesh=staged,
        in_specs=(split,) * 10 + (P(),),
        out_specs=(split,) * 8,
        check_vma=False,
    )
```

time: 189 us -> 179 us (0.947)
  blocking collectives: 45.6 us -> 28.5 us
  starting transfers between devices: 57 us -> 69 us
  Pallas kernels: 12.1 us -> 19.5 us
  waiting for transfers between devices: 45.4 us -> 38 us
  other arithmetic: 6.07 us -> 3.18 us
  between operations: 17.7 us -> 15.1 us
    all_gather x2 -> x0, blocking collectives: 16.2 us -> none  [per_device(): got = lax.all_gather(got, 'yl')]
    ppermute x5 -> x9, starting transfers between devices: 24.6 us -> 38 us  [swap(): return lax.ppermute(array, axis, [(0, 1), (1, 0)])]
    all_to_all x2, waiting for transfers between devices: 18.5 us -> 8.86 us  [the longest x1 8.86 us: per_device(): lax.all_to_all(kept.astype(bf16), 'z', 0, 0)]
    pallas_call x1 -> x3, Pallas kernels: 5.43 us -> 12.8 us  [the longest x1 7.02 us: per_device(): pl.pallas_call(own_columns_kernel, out_shape=jax.ShapeDtypeStruct((tokens...]
    ppermute x1, waiting for transfers between devices: 5.71 us -> 7.72 us  [per_device(): lax.ppermute(next_rows, 'section', [(s, s - 1) for s in range(1, sections)])]
    unnamed x25 -> x36, local copies, waits for them, and re-layouts: 3.43 us -> 4.14 us
    ppermute x5 -> x9, waiting for transfers between devices: 10.1 us -> 10.4 us  [swap(): return lax.ppermute(array, axis, [(0, 1), (1, 0)])]
  transfers between devices with their start and end apart: 11 -> 15, of which waited for: 8 -> 9; matrix products, arithmetic and copies ran while one was open for 2% -> 1% of each run, Pallas kernels for 4% -> 8%
where the time goes in v3:
time: 179 us; the launch traced here: 178 us
  starting transfers between devices  69 us (39%)
  waiting for transfers between devices  38 us (21%)
  blocking collectives  28.5 us (16%)
  Pallas kernels  19.5 us (11%)
  between operations  15.1 us (8%)
  local copies, waits for them, and re-layouts  4.3 us (2%)
  other arithmetic  3.18 us (2%)
    ppermute x9, starting transfers between devices, swap(): return lax.ppermute(array, axis, [(0, 1), (1, 0)])  38 us
    all_to_all x1, blocking collectives, spread(): return lax.all_to_all(copies, 'z', 0, 0)  28.5 us
    all_to_all x1, starting transfers between devices, spread(): return lax.all_to_all(copies, 'z', 0, 0)  14.9 us
    ppermute x9, waiting for transfers between devices, swap(): return lax.ppermute(array, axis, [(0, 1), (1, 0)])  10.4 us
    all_to_all x1, waiting for transfers between devices, per_device(): lax.all_to_all(kept.astype(bf16), 'z', 0, 0)  8.86 us
    all_to_all x1, starting transfers between devices, per_device(): lax.all_to_all(kept.astype(bf16), 'z', 0, 0)  8.1 us
    ppermute x1, waiting for transfers between devices, per_device(): lax.ppermute(next_rows, 'section', [(s, s - 1) for s in range(1, sections)])  7.72 us
    pallas_call x1, Pallas kernels, per_device(): pl.pallas_call(own_columns_kernel, out_shape=jax.ShapeDtypeStruct((tokens...  7.02 us
  transfers between devices with their start and end apart: 15, of which 9 were waited for; matrix products, arithmetic and copies ran while one was open for 1% of the time, Pallas kernels for 8%

profile of v3, /device:TPU:7, one launch (start us, length us, event | category | flops | bytes accessed | tf_op | source)
XLA Modules:
  0.0 177.5 jit_solution(14378857882342176797)
XLA Ops:
  7.2 0.0 copy-start
  7.2 0.0 copy-start.5
  7.2 1.0 copy-done.5
  8.2 0.8 copy-done.6
  9.0 0.7 copy-done.8
  9.7 0.7 copy-done.10
  10.4 0.8 prepare.1
  11.2 14.9 %all-to-all-start = ((bf16[16,72,128]{2,1,0:T(8,128)(2,1)}), bf16[16,72,128]{2,1,0:T(8,128)(2,1)S(1)}, u32[]{:S(2)}, u32[]{:S(2)}) async-start(bf16[16,72,128]{2,1,0:T(8,128)(2,1)} %get-tuple-element.22), calls=%async_computation | async-start | bytes 589824 | tf_op jit(solution)/shard_map/all_to_all | solution.py:47
  26.1 0.0 all-gather.3.cloned.1.call-start
  26.1 2.5 %collective-permute-start = (bf16[576,128]{1,0:T(8,128)(2,1)S(1)}, bf16[576,128]{1,0:T(8,128)(2,1)S(1)}, u32[]{:S(2)}, u32[]{:S(2)}) collective-permute-start(bf16[576,128]{1,0:T(8,128)(2,1)S(1)} %get-tuple-element.23), channel_id=1, source_target_pairs={{64,0},{66,2},{128,64},{130,66},{192,128},{194,130},{256,192},{258... | collective-permute-start | bytes 442376 | tf_op jit(solution)/shard_map/ppermute | solution.py:234
  28.6 3.2 %collective-permute-start.1 = (bf16[576,128]{1,0:T(8,128)(2,1)S(1)}, bf16[576,128]{1,0:T(8,128)(2,1)S(1)}, u32[]{:S(2)}, u32[]{:S(2)}) collective-permute-start(bf16[576,128]{1,0:T(8,128)(2,1)S(1)} %get-tuple-element.23), channel_id=1, source_target_pairs={{66,0},{64,2},{130,64},{128,66},{194,128},{192,130},{258,192},{256... | collective-permute-start | bytes 442376 | tf_op jit(solution)/shard_map/ppermute | solution.py:235
  31.8 4.2 %collective-permute-done = bf16[576,128]{1,0:T(8,128)(2,1)S(1)} collective-permute-done((bf16[576,128]{1,0:T(8,128)(2,1)S(1)}, bf16[576,128]{1,0:T(8,128)(2,1)S(1)}, u32[]{:S(2)}, u32[]{:S(2)}) %collective-permute-start) | collective-permute-done | bytes 147488 | tf_op jit(solution)/shard_map/ppermute | solution.py:234
  36.0 4.0 %collective-permute-done.1 = bf16[576,128]{1,0:T(8,128)(2,1)S(1)} collective-permute-done((bf16[576,128]{1,0:T(8,128)(2,1)S(1)}, bf16[576,128]{1,0:T(8,128)(2,1)S(1)}, u32[]{:S(2)}, u32[]{:S(2)}) %collective-permute-start.1) | collective-permute-done | bytes 147488 | tf_op jit(solution)/shard_map/ppermute | solution.py:235
  40.1 0.0 all-to-all-done.q0
  40.1 0.7 pad_maximum_fusion
  40.9 0.0 all-gather.3.cloned.1.call-update
  40.9 3.0 %collective-permute-start.2 = (bf16[16,72,128]{2,1,0:T(8,128)(2,1)S(1)}, bf16[16,72,128]{2,1,0:T(8,128)(2,1)S(1)}, u32[]{:S(2)}, u32[]{:S(2)}) collective-permute-start(bf16[16,72,128]{2,1,0:T(8,128)(2,1)S(1)} %all-to-all-done.q0), channel_id=1, source_target_pairs={{0,2},{2,0},{1,3},{3,1},{4,6},{6,4},{5,7},{7,5},{8,10},{10,8},{9,1... | collective-permute-start | bytes 884744 | tf_op jit(solution)/shard_map/ppermute | solution.py:33
  43.8 8.7 %collective-permute-start.3 = (bf16[16,72,128]{2,1,0:T(8,128)(2,1)S(1)}, bf16[16,72,128]{2,1,0:T(8,128)(2,1)S(1)}, u32[]{:S(2)}, u32[]{:S(2)}) collective-permute-start(bf16[16,72,128]{2,1,0:T(8,128)(2,1)S(1)} %all-to-all-done.q0), channel_id=1, source_target_pairs={{0,1},{1,0},{2,3},{3,2},{4,5},{5,4},{6,7},{7,6},{8,9},{9,8},{10,11... | collective-permute-start | bytes 884744 | tf_op jit(solution)/shard_map/ppermute | solution.py:33
  52.5 0.0 collective-permute-done.2.q1
  52.5 5.1 %collective-permute-start.4 = (bf16[16,72,128]{2,1,0:T(8,128)(2,1)S(1)}, bf16[16,72,128]{2,1,0:T(8,128)(2,1)S(1)}, u32[]{:S(2)}, u32[]{:S(2)}) collective-permute-start(bf16[16,72,128]{2,1,0:T(8,128)(2,1)S(1)} %collective-permute-done.2.q1), channel_id=1, source_target_pairs={{0,1},{1,0},{2,3},{3,2},{4,5},{5,4},{6,7},{7,6},{8,9},{9,8},{10,11... | collective-permute-start | bytes 884744 | tf_op jit(solution)/shard_map/ppermute | solution.py:33
  57.6 0.1 pad_add_fusion.place
  57.7 0.0 collective-permute-done.3.q2
  57.7 1.1 collective-permute-done.4.q3
  58.8 0.0 copy-done.11
  58.8 0.9 copy-done.4
  59.7 4.2 %backward.1 = (f32[2,16,72,128]{3,2,1,0:T(8,128)S(1)}, bf16[2,16,72,128]{3,2,1,0:T(8,128)(2,1)S(1)}, bf16[136,576]{1,0:T(8,128)(2,1)S(1)}) custom-call(s32[2]{0:T(128)S(1)} %pad_add_fusion.place, bf16[16,72,128]{2,1,0:T(8,128)(2,1)S(1)} %all-to-all-done.q0, bf16[16,72,128]{2,1,0:T(8,128)(2,1)S(1)} %collective-permute-done.2.q1, ...), custom_call_target="tpu_custom_call" | custom-call | tf_op jit(solution)/shard_map/backward/pallas_call | solution.py:244
  64.0 0.0 copy-start.12
  64.0 2.3 %collective-permute-start.5 = (bf16[2,16,72,128]{3,2,1,0:T(8,128)(2,1)S(1)}, bf16[2,16,72,128]{3,2,1,0:T(8,128)(2,1)S(1)}, u32[]{:S(2)}, u32[]{:S(2)}) collective-permute-start(bf16[2,16,72,128]{3,2,1,0:T(8,128)(2,1)S(1)} %get-tuple-element.26), channel_id=1, source_target_pairs={{0,1},{1,0},{2,3},{3,2},{4,5},{5,4},{6,7},{7,6},{8,9},{9,8},{10,11... | collective-permute-start | bytes 1769480 | tf_op jit(solution)/shard_map/ppermute | solution.py:33
  66.3 1.6 collective-permute-done.5
  67.9 0.1 convert_add_fusion
  68.0 0.0 copy-done.12
  68.0 0.0 copy-start.17
  68.0 0.0 copy-start.16
  68.1 0.0 copy-start.9
  68.1 0.0 copy-start.7
  68.1 0.0 copy-start.14
  68.1 0.0 copy-start.15
  68.1 3.3 %collective-permute-start.6 = (bf16[16,72,128]{2,1,0:T(8,128)(2,1)S(1)}, bf16[16,72,128]{2,1,0:T(8,128)(2,1)S(1)}, u32[]{:S(2)}, u32[]{:S(2)}) collective-permute-start(bf16[16,72,128]{2,1,0:T(8,128)(2,1)S(1)} %fusion.2), channel_id=1, source_target_pairs={{0,2},{2,0},{1,3},{3,1},{4,6},{6,4},{5,7},{7,5},{8,10},{10,8},{9,1... | collective-permute-start | bytes 884744 | tf_op jit(solution)/shard_map/ppermute | solution.py:33
  71.5 6.9 %collective-permute-done.6 = bf16[16,72,128]{2,1,0:T(8,128)(2,1)S(1)} collective-permute-done((bf16[16,72,128]{2,1,0:T(8,128)(2,1)S(1)}, bf16[16,72,128]{2,1,0:T(8,128)(2,1)S(1)}, u32[]{:S(2)}, u32[]{:S(2)}) %collective-permute-start.6) | collective-permute-done | bytes 294944 | tf_op jit(solution)/shard_map/ppermute | solution.py:33
  78.4 0.8 fusion.1
  79.2 8.1 %all-to-all-start.1 = ((bf16[16,72,128]{2,1,0:T(8,128)(2,1)}), bf16[16,72,128]{2,1,0:T(8,128)(2,1)S(1)}, u32[]{:S(2)}, u32[]{:S(2)}) async-start(bf16[16,72,128]{2,1,0:T(8,128)(2,1)} %fusion.1), calls=%async_computation.1 | async-start | bytes 589824 | tf_op jit(solution)/shard_map/all_to_all | solution.py:264
  88.0 0.1 pad.4.clone
  88.1 0.0 copy-done.17
  88.1 2.3 %collective-permute-start.7 = (bf16[136,576]{1,0:T(8,128)(2,1)S(1)}, bf16[136,576]{1,0:T(8,128)(2,1)S(1)}, u32[]{:S(2)}, u32[]{:S(2)}) collective-permute-start(bf16[136,576]{1,0:T(8,128)(2,1)S(1)} %copy-done.13), channel_id=1, source_target_pairs={{64,0},{128,64},{192,128},{256,192},{320,256},{384,320},{448,384},... | collective-permute-start | bytes 470024 | tf_op jit(solution)/shard_map/ppermute | solution.py:260
  90.5 7.7 %collective-permute-done.7.rows = bf16[136,576]{1,0:T(8,128)(2,1)S(1)} collective-permute-done((bf16[136,576]{1,0:T(8,128)(2,1)S(1)}, bf16[136,576]{1,0:T(8,128)(2,1)S(1)}, u32[]{:S(2)}, u32[]{:S(2)}) %collective-permute-start.7) | collective-permute-done | bytes 156704 | tf_op jit(solution)/shard_map/ppermute | solution.py:260
  98.2 8.9 %all-to-all-done.1 = bf16[16,72,128]{2,1,0:T(8,128)(2,1)S(1)} async-done(((bf16[16,72,128]{2,1,0:T(8,128)(2,1)}), bf16[16,72,128]{2,1,0:T(8,128)(2,1)S(1)}, u32[]{:S(2)}, u32[]{:S(2)}) %all-to-all-start.1) | async-done | bytes 294944 | tf_op jit(solution)/shard_map/all_to_all | solution.py:264
  107.1 0.0 copy-done.7
  107.2 0.0 copy-done.14
  107.2 0.7 fusion.10
  107.8 0.1 maximum_maximum_fusion
  108.0 28.5 %all_to_all.15.q0 = bf16[16,72,128]{2,1,0:T(8,128)(2,1)S(1)} all-to-all(bf16[16,72,128]{2,1,0:T(8,128)(2,1)S(1)} %broadcast_in_dim.28), channel_id=1, replica_groups=mesh['section'=8,'z'=16,'yl'=2,'core'=2] {'z'}, dimensions={0} | all-to-all | bytes 589824 | tf_op jit(solution)/shard_map/all_to_all | solution.py:47
  136.4 2.8 %all-gather.3.cloned.1.call-done.weights = bf16[32,576,128]{2,1,0:T(8,128)(2,1)} async-done(((bf16[2,576,128]{2,1,0:T(8,128)(2,1)}), bf16[32,576,128]{2,1,0:T(8,128)(2,1)}) %all-gather.3.cloned.1.call-update) | async-done | bytes 4718608 | tf_op jit(solution)/shard_map/all_gather | solution.py:241
  139.2 8.3 %collective-permute-start.8 = (bf16[32,576,128]{2,1,0:T(8,128)(2,1)}, bf16[32,576,128]{2,1,0:T(8,128)(2,1)S(1)}, u32[]{:S(2)}, u32[]{:S(2)}) collective-permute-start(bf16[32,576,128]{2,1,0:T(8,128)(2,1)} %all-gather.3.cloned.1.call-done.weights), channel_id=1, source_target_pairs={{0,1},{1,0},{2,3},{3,2},{4,5},{5,4},{6,7},{7,6},{8,9},{9,8},{10,11... | collective-permute-start | bytes 14155784 | tf_op jit(solution)/shard_map/ppermute | solution.py:33
  147.4 3.1 %collective-permute-start.9 = (bf16[16,72,128]{2,1,0:T(8,128)(2,1)S(1)}, bf16[16,72,128]{2,1,0:T(8,128)(2,1)S(1)}, u32[]{:S(2)}, u32[]{:S(2)}) collective-permute-start(bf16[16,72,128]{2,1,0:T(8,128)(2,1)S(1)} %all_to_all.15.q0), channel_id=1, source_target_pairs={{0,2},{2,0},{1,3},{3,1},{4,6},{6,4},{5,7},{7,5},{8,10},{10,8},{9,1... | collective-permute-start | bytes 884744 | tf_op jit(solution)/shard_map/ppermute | solution.py:33
  150.5 2.2 %collective-permute-start.10 = (bf16[16,72,128]{2,1,0:T(8,128)(2,1)S(1)}, bf16[16,72,128]{2,1,0:T(8,128)(2,1)S(1)}, u32[]{:S(2)}, u32[]{:S(2)}) collective-permute-start(bf16[16,72,128]{2,1,0:T(8,128)(2,1)S(1)} %all_to_all.15.q0), channel_id=1, source_target_pairs={{0,1},{1,0},{2,3},{3,2},{4,5},{5,4},{6,7},{7,6},{8,9},{9,8},{10,11... | collective-permute-start | bytes 884744 | tf_op jit(solution)/shard_map/ppermute | solution.py:33
  152.7 7.0 %own_columns.1.mine = bf16[136,4096]{1,0:T(8,128)(2,1)} custom-call(bf16[136,576]{1,0:T(8,128)(2,1)} %copy-done.2, bf16[32,576,128]{2,1,0:T(8,128)(2,1)} %all-gather.3.cloned.1.call-done.weights), custom_call_target="tpu_custom_call" | custom-call | flops 641728512 | bytes 5832704 | tf_op jit(solution)/shard_map/own_columns/pallas_call | solution.py:282
  159.8 0.0 collective-permute-done.9.q1
  159.8 2.1 %collective-permute-start.11 = (bf16[16,72,128]{2,1,0:T(8,128)(2,1)S(1)}, bf16[16,72,128]{2,1,0:T(8,128)(2,1)S(1)}, u32[]{:S(2)}, u32[]{:S(2)}) collective-permute-start(bf16[16,72,128]{2,1,0:T(8,128)(2,1)S(1)} %collective-permute-done.9.q1), channel_id=1, source_target_pairs={{0,1},{1,0},{2,3},{3,2},{4,5},{5,4},{6,7},{7,6},{8,9},{9,8},{10,11... | collective-permute-start | bytes 884744 | tf_op jit(solution)/shard_map/ppermute | solution.py:33
  161.9 0.6 divide_subtract_fusion.1
  162.5 0.0 collective-permute-done.10.q2
  162.5 0.7 collective-permute-done.11.q3
  163.2 2.5 %refresh.1 = bf16[136,512]{1,0:T(8,128)(2,1)} custom-call(s32[2]{0:T(128)S(1)} %pad_add_fusion.place, bf16[16,72,128]{2,1,0:T(8,128)(2,1)S(1)} %all_to_all.15.q0, bf16[16,72,128]{2,1,0:T(8,128)(2,1)S(1)} %collective-permute-done.9.q1, bf16[16,72,128]{2,1,0:T(8,128)(2,1)S(1)} %collective-permute-done.10.q2, ...), custom_call_target="tpu_custom_call" | custom-call | tf_op jit(solution)/shard_map/refresh/pallas_call | solution.py:297
  165.7 0.0 collective-permute-done.8.weights
  165.7 5.0 %all_columns.1 = bf16[136,8192]{1,0:T(8,128)(2,1)} custom-call(s32[2]{0:T(128)S(1)} %pad_add_fusion.place, bf16[136,576]{1,0:T(8,128)(2,1)S(1)} %copy-done.3, bf16[32,576,128]{2,1,0:T(8,128)(2,1)S(1)} %collective-permute-done.8.weights, bf16[136,4096]{1,0:T(8,128)(2,1)S(1)} %copy-done.1), custom_call_target="tpu_custom_call" | custom-call | tf_op jit(solution)/shard_map/all_columns/pallas_call | solution.py:310
  (25 shorter events, 0.2 us)
Async XLA Ops:
  7.2 51.7 %copy-start = (bf16[1,136,8192]{2,1,0:T(8,128)(2,1)S(1)}, bf16[1,136,8192]{2,1,0:T(8,128)(2,1)}, u32[]{:S(2)}) copy-start(bf16[1,136,8192]{2,1,0:T(8,128)(2,1)} %param.11) | copy-start | bytes 6684676
  7.2 1.1 copy-start.5
  8.2 0.8 copy-start.6
  9.0 0.7 copy-start.8
  9.7 0.7 copy-start.10
  10.4 48.5 %copy-start.11 = (s32[1,136]{1,0:T(1,128)S(1)}, s32[1,136]{1,0:T(1,128)}, u32[]{:S(2)}) copy-start(s32[1,136]{1,0:T(1,128)} %loss_weight.3) | copy-start | bytes 1636
  11.2 28.9 %all-to-all-start = ((bf16[16,72,128]{2,1,0:T(8,128)(2,1)}), bf16[16,72,128]{2,1,0:T(8,128)(2,1)S(1)}, u32[]{:S(2)}, u32[]{:S(2)}) async-start(bf16[16,72,128]{2,1,0:T(8,128)(2,1)} %get-tuple-element.22), calls=%async_computation | async-start | bytes 589824 | tf_op jit(solution)/shard_map/all_to_all | solution.py:47
  26.1 113.1 %all-gather.3.cloned.1.call-start = ((), (), s32[]{:S(2)}) async-start(), calls=%async_computation.3 | async-start | bytes 5013504 | tf_op jit(solution)/shard_map/all_gather | solution.py:241
  26.1 9.9 %collective-permute-start = (bf16[576,128]{1,0:T(8,128)(2,1)S(1)}, bf16[576,128]{1,0:T(8,128)(2,1)S(1)}, u32[]{:S(2)}, u32[]{:S(2)}) collective-permute-start(bf16[576,128]{1,0:T(8,128)(2,1)S(1)} %get-tuple-element.23), channel_id=1, source_target_pairs={{64,0},{66,2},{128,64},{130,66},{192,128},{194,130},{256,192},{258... | collective-permute-start | bytes 442376 | tf_op jit(solution)/shard_map/ppermute | solution.py:234
  28.6 11.5 %collective-permute-start.1 = (bf16[576,128]{1,0:T(8,128)(2,1)S(1)}, bf16[576,128]{1,0:T(8,128)(2,1)S(1)}, u32[]{:S(2)}, u32[]{:S(2)}) collective-permute-start(bf16[576,128]{1,0:T(8,128)(2,1)S(1)} %get-tuple-element.23), channel_id=1, source_target_pairs={{66,0},{64,2},{130,64},{128,66},{194,128},{192,130},{258,192},{256... | collective-permute-start | bytes 442376 | tf_op jit(solution)/shard_map/ppermute | solution.py:235
  40.9 11.6 %collective-permute-start.2 = (bf16[16,72,128]{2,1,0:T(8,128)(2,1)S(1)}, bf16[16,72,128]{2,1,0:T(8,128)(2,1)S(1)}, u32[]{:S(2)}, u32[]{:S(2)}) collective-permute-start(bf16[16,72,128]{2,1,0:T(8,128)(2,1)S(1)} %all-to-all-done.q0), channel_id=1, source_target_pairs={{0,2},{2,0},{1,3},{3,1},{4,6},{6,4},{5,7},{7,5},{8,10},{10,8},{9,1... | collective-permute-start | bytes 884744 | tf_op jit(solution)/shard_map/ppermute | solution.py:33
  43.8 13.9 %collective-permute-start.3 = (bf16[16,72,128]{2,1,0:T(8,128)(2,1)S(1)}, bf16[16,72,128]{2,1,0:T(8,128)(2,1)S(1)}, u32[]{:S(2)}, u32[]{:S(2)}) collective-permute-start(bf16[16,72,128]{2,1,0:T(8,128)(2,1)S(1)} %all-to-all-done.q0), channel_id=1, source_target_pairs={{0,1},{1,0},{2,3},{3,2},{4,5},{5,4},{6,7},{7,6},{8,9},{9,8},{10,11... | collective-permute-start | bytes 884744 | tf_op jit(solution)/shard_map/ppermute | solution.py:33
  52.5 6.3 %collective-permute-start.4 = (bf16[16,72,128]{2,1,0:T(8,128)(2,1)S(1)}, bf16[16,72,128]{2,1,0:T(8,128)(2,1)S(1)}, u32[]{:S(2)}, u32[]{:S(2)}) collective-permute-start(bf16[16,72,128]{2,1,0:T(8,128)(2,1)S(1)} %collective-permute-done.2.q1), channel_id=1, source_target_pairs={{0,1},{1,0},{2,3},{3,2},{4,5},{5,4},{6,7},{7,6},{8,9},{9,8},{10,11... | collective-permute-start | bytes 884744 | tf_op jit(solution)/shard_map/ppermute | solution.py:33
  58.8 0.9 copy-start.4
  64.0 4.0 %copy-start.12 = (bf16[136,576]{1,0:T(8,128)(2,1)}, bf16[136,576]{1,0:T(8,128)(2,1)S(1)}, u32[]{:S(2)}) copy-start(bf16[136,576]{1,0:T(8,128)(2,1)S(1)} %get-tuple-element.27) | copy-start | bytes 470020
  64.0 3.9 %collective-permute-start.5 = (bf16[2,16,72,128]{3,2,1,0:T(8,128)(2,1)S(1)}, bf16[2,16,72,128]{3,2,1,0:T(8,128)(2,1)S(1)}, u32[]{:S(2)}, u32[]{:S(2)}) collective-permute-start(bf16[2,16,72,128]{3,2,1,0:T(8,128)(2,1)S(1)} %get-tuple-element.26), channel_id=1, source_target_pairs={{0,1},{1,0},{2,3},{3,2},{4,5},{5,4},{6,7},{7,6},{8,9},{9,8},{10,11... | collective-permute-start | bytes 1769480 | tf_op jit(solution)/shard_map/ppermute | solution.py:33
  68.0 20.1 %copy-start.17 = (f32[1,1,512]{2,1,0:T(1,128)S(1)}, f32[1,1,512]{2,1,0:T(1,128)}, u32[]{:S(2)}) copy-start(f32[1,1,512]{2,1,0:T(1,128)} %param.19) | copy-start | bytes 6148
  68.0 22.4 %copy-start.16 = (f32[1,1,512]{2,1,0:T(1,128)S(1)}, f32[1,1,512]{2,1,0:T(1,128)}, u32[]{:S(2)}) copy-start(f32[1,1,512]{2,1,0:T(1,128)} %param.20) | copy-start | bytes 6148
  68.1 20.0 %copy-start.13 = (bf16[136,576]{1,0:T(8,128)(2,1)S(1)}, bf16[136,576]{1,0:T(8,128)(2,1)}, u32[]{:S(2)}) copy-start(bf16[136,576]{1,0:T(8,128)(2,1)} %copy-done.12) | copy-start | bytes 470020
  68.1 39.0 %copy-start.9 = (f32[1,1,512]{2,1,0:T(1,128)S(1)}, f32[1,1,512]{2,1,0:T(1,128)}, u32[]{:S(2)}) copy-start(f32[1,1,512]{2,1,0:T(1,128)} %param.18) | copy-start | bytes 6148
  68.1 39.0 %copy-start.7 = (f32[1,128,64]{1,2,0:T(8,128)S(1)}, f32[1,128,64]{1,2,0:T(8,128)}, u32[]{:S(2)}) copy-start(f32[1,128,64]{1,2,0:T(8,128)} %param.15) | copy-start | bytes 98308
  68.1 39.0 %copy-start.14 = (f32[1,128,64]{1,2,0:T(8,128)S(1)}, f32[1,128,64]{1,2,0:T(8,128)}, u32[]{:S(2)}) copy-start(f32[1,128,64]{1,2,0:T(8,128)} %param.17) | copy-start | bytes 98308
  68.1 39.0 %copy-start.15 = (f32[1,128,64]{1,2,0:T(8,128)S(1)}, f32[1,128,64]{1,2,0:T(8,128)}, u32[]{:S(2)}) copy-start(f32[1,128,64]{1,2,0:T(8,128)} %param.16) | copy-start | bytes 98308
  68.1 10.2 %collective-permute-start.6 = (bf16[16,72,128]{2,1,0:T(8,128)(2,1)S(1)}, bf16[16,72,128]{2,1,0:T(8,128)(2,1)S(1)}, u32[]{:S(2)}, u32[]{:S(2)}) collective-permute-start(bf16[16,72,128]{2,1,0:T(8,128)(2,1)S(1)} %fusion.2), channel_id=1, source_target_pairs={{0,2},{2,0},{1,3},{3,1},{4,6},{6,4},{5,7},{7,5},{8,10},{10,8},{9,1... | collective-permute-start | bytes 884744 | tf_op jit(solution)/shard_map/ppermute | solution.py:33
  79.2 27.9 %all-to-all-start.1 = ((bf16[16,72,128]{2,1,0:T(8,128)(2,1)}), bf16[16,72,128]{2,1,0:T(8,128)(2,1)S(1)}, u32[]{:S(2)}, u32[]{:S(2)}) async-start(bf16[16,72,128]{2,1,0:T(8,128)(2,1)} %fusion.1), calls=%async_computation.1 | async-start | bytes 589824 | tf_op jit(solution)/shard_map/all_to_all | solution.py:264
  88.1 10.1 %collective-permute-start.7 = (bf16[136,576]{1,0:T(8,128)(2,1)S(1)}, bf16[136,576]{1,0:T(8,128)(2,1)S(1)}, u32[]{:S(2)}, u32[]{:S(2)}) collective-permute-start(bf16[136,576]{1,0:T(8,128)(2,1)S(1)} %copy-done.13), channel_id=1, source_target_pairs={{64,0},{128,64},{192,128},{256,192},{320,256},{384,320},{448,384},... | collective-permute-start | bytes 470024 | tf_op jit(solution)/shard_map/ppermute | solution.py:260
  98.2 54.5 %copy-start.2 = (bf16[136,576]{1,0:T(8,128)(2,1)}, bf16[136,576]{1,0:T(8,128)(2,1)S(1)}, u32[]{:S(2)}) copy-start(bf16[136,576]{1,0:T(8,128)(2,1)S(1)} %collective-permute-done.7.rows) | copy-start | bytes 470020
  139.2 26.5 %collective-permute-start.8 = (bf16[32,576,128]{2,1,0:T(8,128)(2,1)}, bf16[32,576,128]{2,1,0:T(8,128)(2,1)S(1)}, u32[]{:S(2)}, u32[]{:S(2)}) collective-permute-start(bf16[32,576,128]{2,1,0:T(8,128)(2,1)} %all-gather.3.cloned.1.call-done.weights), channel_id=1, source_target_pairs={{0,1},{1,0},{2,3},{3,2},{4,5},{5,4},{6,7},{7,6},{8,9},{9,8},{10,11... | collective-permute-start | bytes 14155784 | tf_op jit(solution)/shard_map/ppermute | solution.py:33
  147.4 12.3 %collective-permute-start.9 = (bf16[16,72,128]{2,1,0:T(8,128)(2,1)S(1)}, bf16[16,72,128]{2,1,0:T(8,128)(2,1)S(1)}, u32[]{:S(2)}, u32[]{:S(2)}) collective-permute-start(bf16[16,72,128]{2,1,0:T(8,128)(2,1)S(1)} %all_to_all.15.q0), channel_id=1, source_target_pairs={{0,2},{2,0},{1,3},{3,1},{4,6},{6,4},{5,7},{7,5},{8,10},{10,8},{9,1... | collective-permute-start | bytes 884744 | tf_op jit(solution)/shard_map/ppermute | solution.py:33
  150.5 12.0 %collective-permute-start.10 = (bf16[16,72,128]{2,1,0:T(8,128)(2,1)S(1)}, bf16[16,72,128]{2,1,0:T(8,128)(2,1)S(1)}, u32[]{:S(2)}, u32[]{:S(2)}) collective-permute-start(bf16[16,72,128]{2,1,0:T(8,128)(2,1)S(1)} %all_to_all.15.q0), channel_id=1, source_target_pairs={{0,1},{1,0},{2,3},{3,2},{4,5},{5,4},{6,7},{7,6},{8,9},{9,8},{10,11... | collective-permute-start | bytes 884744 | tf_op jit(solution)/shard_map/ppermute | solution.py:33
  159.8 3.5 %collective-permute-start.11 = (bf16[16,72,128]{2,1,0:T(8,128)(2,1)S(1)}, bf16[16,72,128]{2,1,0:T(8,128)(2,1)S(1)}, u32[]{:S(2)}, u32[]{:S(2)}) collective-permute-start(bf16[16,72,128]{2,1,0:T(8,128)(2,1)S(1)} %collective-permute-done.9.q1), channel_id=1, source_target_pairs={{0,1},{1,0},{2,3},{3,2},{4,5},{5,4},{6,7},{7,6},{8,9},{9,8},{10,11... | collective-permute-start | bytes 884744 | tf_op jit(solution)/shard_map/ppermute | solution.py:33
  162.5 3.2 %copy-start.1 = (bf16[136,4096]{1,0:T(8,128)(2,1)S(1)}, bf16[136,4096]{1,0:T(8,128)(2,1)}, u32[]{:S(2)}) copy-start(bf16[136,4096]{1,0:T(8,128)(2,1)} %own_columns.1.mine) | copy-start | bytes 3342340
  162.5 3.2 %copy-start.3 = (bf16[136,576]{1,0:T(8,128)(2,1)S(1)}, bf16[136,576]{1,0:T(8,128)(2,1)}, u32[]{:S(2)}) copy-start(bf16[136,576]{1,0:T(8,128)(2,1)} %copy-done.2) | copy-start | bytes 470020
Sparse Core Ops, SparseCore 0:
  41.0 98.1 all-gather.2

commit v4 on v3

--- a/solution.py
+++ b/solution.py
@@ -31,12 +31,6 @@
 
 def swap(array, axis):
     return lax.ppermute(array, axis, [(0, 1), (1, 0)])
-
-
-def quarters(got, beside=None):
-    got_yl = swap(got, "yl")
-    got_yl, beside = after(got_yl, beside)
-    return (got, got_yl, swap(got, "core"), swap(got_yl, "core")), beside
 
 
 def after(value, *others):
@@ -167,22 +161,25 @@
     out[...] = (adapter_scale * nn(low, up)).astype(bf16)
 
 
-def side_by_side(blocks):
-    return jnp.concatenate([blocks[i] for i in range(blocks.shape[0])], axis=1)
+def pair_product(rows, weights, i):
+    return nn(rows[...], jnp.concatenate([weights[i], weights[i + 1]], axis=1)).astype(bf16)
 
 
 def own_columns_kernel(rows, weights, out):
-    out[...] = nn(rows[...], side_by_side(weights)).astype(bf16)
+    for i in range(0, weights.shape[0], 2):
+        out[:, i * LANES : (i + 2) * LANES] = pair_product(rows, weights, i)
 
 
 def all_columns_kernel(place, rows, weights, mine, out):
     core = place[0]
-    other = nn(rows[...], side_by_side(weights)).astype(bf16)
-    for i in range(weights.shape[0]):
-        at = i * 2 * LANES
-        a, b = mine[:, i * LANES : (i + 1) * LANES], other[:, i * LANES : (i + 1) * LANES]
-        out[:, at : at + LANES] = jnp.where(core == 0, a, b)
-        out[:, at + LANES : at + 2 * LANES] = jnp.where(core == 0, b, a)
+    for i in range(0, weights.shape[0], 2):
+        other = pair_product(rows, weights, i)
+        for j in range(2):
+            a = mine[:, (i + j) * LANES : (i + j + 1) * LANES]
+            b = other[:, j * LANES : (j + 1) * LANES]
+            at = (i + j) * 2 * LANES
+            out[:, at : at + LANES] = jnp.where(core == 0, a, b)
+            out[:, at + LANES : at + 2 * LANES] = jnp.where(core == 0, b, a)
 
 
 def whole(n):
@@ -222,7 +219,7 @@
         ),
         in_specs=whole(4),
         out_specs=tuple(whole(2)),
-        compiler_params=params,
+        compiler_params=pltpu.CompilerParams(vmem_limit_bytes=60 * 1024 * 1024),
         name="prepare",
     )(down_master[0].T, up_master[0], loss_weight, value_weight[0])
 
@@ -234,13 +231,12 @@
     same = lax.ppermute(weights, ("section", "yl"), from_next(0))
     flipped = lax.ppermute(weights, ("section", "yl"), from_next(1))
 
-    got = spread(copies)
-    got, same, flipped = after(got, same, flipped)
     even = lax.axis_index("yl") == 0
     weights = jnp.stack([jnp.where(even, same, flipped), jnp.where(even, flipped, same)])
+    copies, weights = after(copies, weights)
     weights_mine = lax.all_gather(weights, "z").reshape(2 * z, features + rank, LANES)
-
-    blocks, _ = quarters(got)
+    got = spread(copies)
+    got_yl = swap(got, "yl")
     keep, send, next_rows = pl.pallas_call(
         backward_kernel,
         out_shape=(
@@ -256,7 +252,7 @@
         ],
         compiler_params=params,
         name="backward",
-    )(place, *blocks, acts, value_grad[0], loss_weight)
+    )(place, got, got_yl, swap(got, "core"), swap(got_yl, "core"), acts, value_grad[0], loss_weight)
     next_rows = lax.ppermute(next_rows, "section", [(s, s - 1) for s in range(1, sections)])
 
     kept = keep + swap(send, "core").astype(f32)
@@ -276,6 +272,11 @@
     got, weights_mine = after(got, weights_mine)
     weights_other = swap(weights_mine, "core")
     chunk = min(4, 2 * z)
+    product_cost = pl.CostEstimate(
+        flops=tokens * (features + rank) * width,
+        bytes_accessed=(features + rank) * width + tokens * width,
+        transcendentals=0,
+    )
     rows_spec = pl.BlockSpec((tokens, features + rank), lambda i: (0, 0))
     w_spec = pl.BlockSpec((chunk, features + rank, LANES), lambda i: (i, 0, 0))
     half_spec = pl.BlockSpec((tokens, chunk * LANES), lambda i: (0, i))
@@ -286,14 +287,22 @@
         in_specs=[rows_spec, w_spec],
         out_specs=half_spec,
         compiler_params=pltpu.CompilerParams(vmem_limit_bytes=56 * 1024 * 1024),
-        cost_estimate=pl.CostEstimate(
-            flops=tokens * (features + rank) * width,
-            bytes_accessed=(features + rank) * width + tokens * width,
-            transcendentals=0,
-        ),
+        cost_estimate=product_cost,
         name="own_columns",
     )(next_rows, weights_mine)
-    blocks, own_columns = quarters(got, own_columns)
+    got_yl, own_columns = after(swap(got, "yl"), own_columns)
+    upstream = pl.pallas_call(
+        all_columns_kernel,
+        out_shape=jax.ShapeDtypeStruct((tokens, width), bf16),
+        grid=(2 * z // chunk,),
+        in_specs=[SCALARS, rows_spec, w_spec, half_spec],
+        out_specs=pl.BlockSpec((tokens, chunk * 2 * LANES), lambda i: (0, i)),
+        compiler_params=params,
+        cost_estimate=product_cost,
+        name="all_columns",
+    )(place, next_rows, weights_other, own_columns)
+    got_core, got_last = swap(got, "core"), swap(got_yl, "core")
+    got_last, upstream = after(got_last, upstream)
     refreshed = pl.pallas_call(
         refresh_kernel,
         out_shape=jax.ShapeDtypeStruct((tokens, features), bf16),
@@ -305,17 +314,8 @@
         ],
         compiler_params=params,
         name="refresh",
-    )(place, *blocks, acts)
-
-    upstream = pl.pallas_call(
-        all_columns_kernel,
-        out_shape=jax.ShapeDtypeStruct((tokens, width), bf16),
-        grid=(2 * z // chunk,),
-        in_specs=[SCALARS, rows_spec, w_spec, half_spec],
-        out_specs=pl.BlockSpec((tokens, chunk * 2 * LANES), lambda i: (0, i)),
-        compiler_params=params,
-        name="all_columns",
-    )(place, next_rows, weights_other, own_columns)
+    )(place, got, got_yl, got_core, got_last, acts)
+
     return (
         upstream[None],
         refreshed[None],

time: 179 us -> 184 us (1.028)
  blocking collectives: 28.5 us -> 52 us
  starting transfers between devices: 69 us -> 54.8 us
  waiting for transfers between devices: 38 us -> 34.7 us
    all_to_all x1 -> x2, blocking collectives: 28.5 us -> 52 us  [spread(): return lax.all_to_all(copies, 'z', 0, 0)]
    all_to_all x1 -> x0, starting transfers between devices: 14.9 us -> none  [spread(): return lax.all_to_all(copies, 'z', 0, 0)]
    all_to_all x1, waiting for transfers between devices: 8.86 us -> 5.63 us  [per_device(): lax.all_to_all(kept.astype(bf16), 'z', 0, 0)]
    all_gather x1, waiting for transfers between devices: 2.75 us -> 0.01 us  [per_device(): lax.all_gather(weights, 'z').reshape(2 * z, features + rank, LANES)]
    ppermute x9, starting transfers between devices: 38 us -> 40.6 us  [swap(): return lax.ppermute(array, axis, [(0, 1), (1, 0)])]
    ppermute x9, waiting for transfers between devices: 10.4 us -> 12.3 us  [swap(): return lax.ppermute(array, axis, [(0, 1), (1, 0)])]
    unnamed x36 -> x28, local copies, waits for them, and re-layouts: 4.14 us -> 3.14 us
  transfers between devices with their start and end apart: 15 -> 14, of which waited for: 9 -> 8; matrix products, arithmetic and copies ran while one was open for 1% -> 1% of each run, Pallas kernels for 8% -> 9%
where the time goes in v4:
time: 184 us
  starting transfers between devices  54.8 us (30%)
  blocking collectives  52 us (28%)
  waiting for transfers between devices  34.7 us (19%)
  Pallas kernels  20.6 us (11%)
  between operations  15.1 us (8%)
  local copies, waits for them, and re-layouts  3.3 us (2%)
  other arithmetic  3.12 us (2%)
    all_to_all x2, blocking collectives, spread(): return lax.all_to_all(copies, 'z', 0, 0)  52 us
    ppermute x9, starting transfers between devices, swap(): return lax.ppermute(array, axis, [(0, 1), (1, 0)])  40.6 us
    ppermute x9, waiting for transfers between devices, swap(): return lax.ppermute(array, axis, [(0, 1), (1, 0)])  12.3 us
    ppermute x1, waiting for transfers between devices, per_device(): lax.ppermute(next_rows, 'section', [(s, s - 1) for s in range(1, sections)])  8.13 us
    pallas_call x1, Pallas kernels, per_device(): pl.pallas_call(own_columns_kernel, out_shape=jax.ShapeDtypeStruct((tokens...  7.01 us
    all_to_all x1, starting transfers between devices, per_device(): lax.all_to_all(kept.astype(bf16), 'z', 0, 0)  6.58 us
    all_to_all x1, waiting for transfers between devices, per_device(): lax.all_to_all(kept.astype(bf16), 'z', 0, 0)  5.63 us
    pallas_call x1, Pallas kernels, per_device(): pl.pallas_call(all_columns_kernel, out_shape=jax.ShapeDtypeStruct((tokens...  4.98 us
  transfers between devices with their start and end apart: 14, of which 8 were waited for; matrix products, arithmetic and copies ran while one was open for 1% of the time, Pallas kernels for 9%

profile of v4, /device:TPU:7, one launch (start us, length us, event | category | flops | bytes accessed | tf_op | source)
XLA Modules:
  0.0 183.6 jit_solution(13611689287176522785)
XLA Ops:
  7.2 0.0 copy-start.5
  7.2 0.0 copy-start
  7.2 0.0 all-gather.3.cloned.1.call-start
  7.2 1.9 %prepare.1 = (bf16[16,72,128]{2,1,0:T(8,128)(2,1)}, bf16[576,128]{1,0:T(8,128)(2,1)}) custom-call(f32[64,128]{1,0:T(8,128)} %bitcast.66, f32[1,512]{1,0:T(1,128)} %bitcast.68, s32[1,136]{1,0:T(1,128)} %loss_weight.3, bf16[128,512]{1,0:T(8,128)(2,1)} %bitcast.65), custom_call_target="tpu_custom_call" | custom-call | tf_op jit(solution)/shard_map/prepare/pallas_call | solution.py:214
  9.2 2.4 %collective-permute-start = (bf16[576,128]{1,0:T(8,128)(2,1)}, bf16[576,128]{1,0:T(8,128)(2,1)S(1)}, u32[]{:S(2)}, u32[]{:S(2)}) collective-permute-start(bf16[576,128]{1,0:T(8,128)(2,1)} %get-tuple-element.24), channel_id=1, source_target_pairs={{64,0},{66,2},{128,64},{130,66},{192,128},{194,130},{256,192},{258... | collective-permute-start | bytes 442376 | tf_op jit(solution)/shard_map/ppermute | solution.py:231
  11.6 3.2 %collective-permute-start.1 = (bf16[576,128]{1,0:T(8,128)(2,1)}, bf16[576,128]{1,0:T(8,128)(2,1)S(1)}, u32[]{:S(2)}, u32[]{:S(2)}) collective-permute-start(bf16[576,128]{1,0:T(8,128)(2,1)} %get-tuple-element.24), channel_id=1, source_target_pairs={{66,0},{64,2},{130,64},{128,66},{194,128},{192,130},{258,192},{256... | collective-permute-start | bytes 442376 | tf_op jit(solution)/shard_map/ppermute | solution.py:232
  14.8 4.8 %collective-permute-done = bf16[576,128]{1,0:T(8,128)(2,1)S(1)} collective-permute-done((bf16[576,128]{1,0:T(8,128)(2,1)}, bf16[576,128]{1,0:T(8,128)(2,1)S(1)}, u32[]{:S(2)}, u32[]{:S(2)}) %collective-permute-start) | collective-permute-done | bytes 147488 | tf_op jit(solution)/shard_map/ppermute | solution.py:231
  19.6 3.9 %collective-permute-done.1 = bf16[576,128]{1,0:T(8,128)(2,1)S(1)} collective-permute-done((bf16[576,128]{1,0:T(8,128)(2,1)}, bf16[576,128]{1,0:T(8,128)(2,1)S(1)}, u32[]{:S(2)}, u32[]{:S(2)}) %collective-permute-start.1) | collective-permute-done | bytes 147488 | tf_op jit(solution)/shard_map/ppermute | solution.py:232
  23.5 0.7 pad_maximum_fusion
  24.2 0.0 all-gather.3.cloned.1.call-update
  24.3 28.0 %all_to_all.15.q0 = bf16[16,72,128]{2,1,0:T(8,128)(2,1)S(1)} all-to-all(bf16[16,72,128]{2,1,0:T(8,128)(2,1)} %get-tuple-element.25), channel_id=1, replica_groups=mesh['section'=8,'z'=16,'yl'=2,'core'=2] {'z'}, dimensions={0} | all-to-all | bytes 589824 | tf_op jit(solution)/shard_map/all_to_all | solution.py:41
  52.3 2.2 %collective-permute-start.2 = (bf16[16,72,128]{2,1,0:T(8,128)(2,1)S(1)}, bf16[16,72,128]{2,1,0:T(8,128)(2,1)S(1)}, u32[]{:S(2)}, u32[]{:S(2)}) collective-permute-start(bf16[16,72,128]{2,1,0:T(8,128)(2,1)S(1)} %all_to_all.15.q0), channel_id=1, source_target_pairs={{0,2},{2,0},{1,3},{3,1},{4,6},{6,4},{5,7},{7,5},{8,10},{10,8},{9,1... | collective-permute-start | bytes 884744 | tf_op jit(solution)/shard_map/ppermute | solution.py:33
  54.5 11.7 %collective-permute-start.3 = (bf16[16,72,128]{2,1,0:T(8,128)(2,1)S(1)}, bf16[16,72,128]{2,1,0:T(8,128)(2,1)S(1)}, u32[]{:S(2)}, u32[]{:S(2)}) collective-permute-start(bf16[16,72,128]{2,1,0:T(8,128)(2,1)S(1)} %all_to_all.15.q0), channel_id=1, source_target_pairs={{0,1},{1,0},{2,3},{3,2},{4,5},{5,4},{6,7},{7,6},{8,9},{9,8},{10,11... | collective-permute-start | bytes 884744 | tf_op jit(solution)/shard_map/ppermute | solution.py:33
  66.2 0.0 collective-permute-done.2.q1
  66.2 6.7 %collective-permute-start.4 = (bf16[16,72,128]{2,1,0:T(8,128)(2,1)S(1)}, bf16[16,72,128]{2,1,0:T(8,128)(2,1)S(1)}, u32[]{:S(2)}, u32[]{:S(2)}) collective-permute-start(bf16[16,72,128]{2,1,0:T(8,128)(2,1)S(1)} %collective-permute-done.2.q1), channel_id=1, source_target_pairs={{0,1},{1,0},{2,3},{3,2},{4,5},{5,4},{6,7},{7,6},{8,9},{9,8},{10,11... | collective-permute-start | bytes 884744 | tf_op jit(solution)/shard_map/ppermute | solution.py:33
  72.9 0.1 pad_add_fusion.place
  73.0 0.0 collective-permute-done.3.q2
  73.0 1.1 collective-permute-done.4.q3
  74.1 0.0 copy-done.5
  74.1 0.0 copy-done
  74.1 0.9 copy-done.4
  75.0 4.2 %backward.1 = (f32[2,16,72,128]{3,2,1,0:T(8,128)S(1)}, bf16[2,16,72,128]{3,2,1,0:T(8,128)(2,1)S(1)}, bf16[136,576]{1,0:T(8,128)(2,1)S(1)}) custom-call(s32[2]{0:T(128)S(1)} %pad_add_fusion.place, bf16[16,72,128]{2,1,0:T(8,128)(2,1)S(1)} %all_to_all.15.q0, bf16[16,72,128]{2,1,0:T(8,128)(2,1)S(1)} %collective-permute-done.2.q1, ...), custom_call_target="tpu_custom_call" | custom-call | tf_op jit(solution)/shard_map/backward/pallas_call | solution.py:240
  79.2 0.0 copy-start.6
  79.2 2.3 %collective-permute-start.5 = (bf16[2,16,72,128]{3,2,1,0:T(8,128)(2,1)S(1)}, bf16[2,16,72,128]{3,2,1,0:T(8,128)(2,1)S(1)}, u32[]{:S(2)}, u32[]{:S(2)}) collective-permute-start(bf16[2,16,72,128]{3,2,1,0:T(8,128)(2,1)S(1)} %get-tuple-element.27), channel_id=1, source_target_pairs={{0,1},{1,0},{2,3},{3,2},{4,5},{5,4},{6,7},{7,6},{8,9},{9,8},{10,11... | collective-permute-start | bytes 1769480 | tf_op jit(solution)/shard_map/ppermute | solution.py:33
  81.5 1.6 collective-permute-done.5
  83.1 0.1 convert_add_fusion
  83.2 0.0 copy-done.6
  83.2 0.0 copy-start.13
  83.2 0.0 copy-start.12
  83.3 0.0 copy-start.7
  83.3 0.0 copy-start.11
  83.3 0.0 copy-start.8
  83.3 0.0 copy-start.9
  83.4 0.0 copy-start.10
  83.4 2.1 %collective-permute-start.6 = (bf16[16,72,128]{2,1,0:T(8,128)(2,1)S(1)}, bf16[16,72,128]{2,1,0:T(8,128)(2,1)S(1)}, u32[]{:S(2)}, u32[]{:S(2)}) collective-permute-start(bf16[16,72,128]{2,1,0:T(8,128)(2,1)S(1)} %fusion.2), channel_id=1, source_target_pairs={{0,2},{2,0},{1,3},{3,1},{4,6},{6,4},{5,7},{7,5},{8,10},{10,8},{9,1... | collective-permute-start | bytes 884744 | tf_op jit(solution)/shard_map/ppermute | solution.py:33
  85.4 8.3 %collective-permute-done.6 = bf16[16,72,128]{2,1,0:T(8,128)(2,1)S(1)} collective-permute-done((bf16[16,72,128]{2,1,0:T(8,128)(2,1)S(1)}, bf16[16,72,128]{2,1,0:T(8,128)(2,1)S(1)}, u32[]{:S(2)}, u32[]{:S(2)}) %collective-permute-start.6) | collective-permute-done | bytes 294944 | tf_op jit(solution)/shard_map/ppermute | solution.py:33
  93.7 0.8 fusion.1
  94.5 6.6 %all-to-all-start.1 = ((bf16[16,72,128]{2,1,0:T(8,128)(2,1)}), bf16[16,72,128]{2,1,0:T(8,128)(2,1)S(1)}, u32[]{:S(2)}, u32[]{:S(2)}) async-start(bf16[16,72,128]{2,1,0:T(8,128)(2,1)} %fusion.1), calls=%async_computation.1 | async-start | bytes 589824 | tf_op jit(solution)/shard_map/all_to_all | solution.py:260
  101.8 0.1 pad.2.clone
  101.9 0.0 copy-done.13
  101.9 0.0 copy-done.7
  101.9 1.9 %collective-permute-start.7 = (bf16[136,576]{1,0:T(8,128)(2,1)S(1)}, bf16[136,576]{1,0:T(8,128)(2,1)S(1)}, u32[]{:S(2)}, u32[]{:S(2)}) collective-permute-start(bf16[136,576]{1,0:T(8,128)(2,1)S(1)} %copy-done.7), channel_id=1, source_target_pairs={{64,0},{128,64},{192,128},{256,192},{320,256},{384,320},{448,384},... | collective-permute-start | bytes 470024 | tf_op jit(solution)/shard_map/ppermute | solution.py:256
  103.8 0.0 copy-done.12
  103.9 8.1 %collective-permute-done.7.rows = bf16[136,576]{1,0:T(8,128)(2,1)S(1)} collective-permute-done((bf16[136,576]{1,0:T(8,128)(2,1)S(1)}, bf16[136,576]{1,0:T(8,128)(2,1)S(1)}, u32[]{:S(2)}, u32[]{:S(2)}) %collective-permute-start.7) | collective-permute-done | bytes 156704 | tf_op jit(solution)/shard_map/ppermute | solution.py:256
  112.0 5.6 %all-to-all-done.1 = bf16[16,72,128]{2,1,0:T(8,128)(2,1)S(1)} async-done(((bf16[16,72,128]{2,1,0:T(8,128)(2,1)}), bf16[16,72,128]{2,1,0:T(8,128)(2,1)S(1)}, u32[]{:S(2)}, u32[]{:S(2)}) %all-to-all-start.1) | async-done | bytes 294944 | tf_op jit(solution)/shard_map/all_to_all | solution.py:260
  117.7 0.0 copy-done.11
  117.7 0.7 fusion.10
  118.4 0.1 maximum_maximum_fusion
  118.5 23.9 %all_to_all.16.q0 = bf16[16,72,128]{2,1,0:T(8,128)(2,1)S(1)} all-to-all(bf16[16,72,128]{2,1,0:T(8,128)(2,1)S(1)} %broadcast_in_dim.28), channel_id=1, replica_groups=mesh['section'=8,'z'=16,'yl'=2,'core'=2] {'z'}, dimensions={0} | all-to-all | bytes 589824 | tf_op jit(solution)/shard_map/all_to_all | solution.py:41
  142.4 8.9 %collective-permute-start.10 = (bf16[32,576,128]{2,1,0:T(8,128)(2,1)}, bf16[32,576,128]{2,1,0:T(8,128)(2,1)S(1)}, u32[]{:S(2)}, u32[]{:S(2)}) collective-permute-start(bf16[32,576,128]{2,1,0:T(8,128)(2,1)} %all-gather.3.cloned.1.call-done.weights), channel_id=1, source_target_pairs={{0,1},{1,0},{2,3},{3,2},{4,5},{5,4},{6,7},{7,6},{8,9},{9,8},{10,11... | collective-permute-start | bytes 14155784 | tf_op jit(solution)/shard_map/ppermute | solution.py:33
  151.3 2.2 %collective-permute-start.8 = (bf16[16,72,128]{2,1,0:T(8,128)(2,1)S(1)}, bf16[16,72,128]{2,1,0:T(8,128)(2,1)S(1)}, u32[]{:S(2)}, u32[]{:S(2)}) collective-permute-start(bf16[16,72,128]{2,1,0:T(8,128)(2,1)S(1)} %all_to_all.16.q0), channel_id=1, source_target_pairs={{0,2},{2,0},{1,3},{3,1},{4,6},{6,4},{5,7},{7,5},{8,10},{10,8},{9,1... | collective-permute-start | bytes 884744 | tf_op jit(solution)/shard_map/ppermute | solution.py:33
  153.6 0.0 copy-done.2
  153.6 7.0 %own_columns.1.mine = bf16[136,4096]{1,0:T(8,128)(2,1)} custom-call(bf16[136,576]{1,0:T(8,128)(2,1)} %copy-done.2, bf16[32,576,128]{2,1,0:T(8,128)(2,1)} %all-gather.3.cloned.1.call-done.weights), custom_call_target="tpu_custom_call" | custom-call | flops 641728512 | bytes 5832704 | tf_op jit(solution)/shard_map/own_columns/pallas_call | solution.py:283
  160.6 1.3 collective-permute-done.8.q1
  161.9 2.7 %collective-permute-start.9 = (bf16[16,72,128]{2,1,0:T(8,128)(2,1)S(1)}, bf16[16,72,128]{2,1,0:T(8,128)(2,1)S(1)}, u32[]{:S(2)}, u32[]{:S(2)}) collective-permute-start(bf16[16,72,128]{2,1,0:T(8,128)(2,1)S(1)} %collective-permute-done.8.q1), channel_id=1, source_target_pairs={{0,1},{1,0},{2,3},{3,2},{4,5},{5,4},{6,7},{7,6},{8,9},{9,8},{10,11... | collective-permute-start | bytes 884744 | tf_op jit(solution)/shard_map/ppermute | solution.py:33
  164.6 1.9 %collective-permute-start.11 = (bf16[16,72,128]{2,1,0:T(8,128)(2,1)S(1)}, bf16[16,72,128]{2,1,0:T(8,128)(2,1)S(1)}, u32[]{:S(2)}, u32[]{:S(2)}) collective-permute-start(bf16[16,72,128]{2,1,0:T(8,128)(2,1)S(1)} %all_to_all.16.q0), channel_id=1, source_target_pairs={{0,1},{1,0},{2,3},{3,2},{4,5},{5,4},{6,7},{7,6},{8,9},{9,8},{10,11... | collective-permute-start | bytes 884744 | tf_op jit(solution)/shard_map/ppermute | solution.py:33
  166.5 0.6 divide_subtract_fusion.1
  167.1 0.0 collective-permute-done.10.weights
  167.1 1.2 copy-done.1
  168.4 0.9 copy-done.3
  169.3 5.0 %all_columns.1 = bf16[136,8192]{1,0:T(8,128)(2,1)} custom-call(s32[2]{0:T(128)S(1)} %pad_add_fusion.place, bf16[136,576]{1,0:T(8,128)(2,1)S(1)} %copy-done.3, bf16[32,576,128]{2,1,0:T(8,128)(2,1)S(1)} %collective-permute-done.10.weights, bf16[136,4096]{1,0:T(8,128)(2,1)S(1)} %copy-done.1), custom_call_target="tpu_custom_call" | custom-call | flops 641728512 | bytes 5832704 | tf_op jit(solution)/shard_map/all_columns/pallas_call | solution.py:294
  174.3 0.0 collective-permute-done.9.q3
  174.3 0.0 collective-permute-done.11.q2
  174.3 2.5 %refresh.1 = bf16[136,512]{1,0:T(8,128)(2,1)} custom-call(s32[2]{0:T(128)S(1)} %pad_add_fusion.place, bf16[16,72,128]{2,1,0:T(8,128)(2,1)S(1)} %all_to_all.16.q0, bf16[16,72,128]{2,1,0:T(8,128)(2,1)S(1)} %collective-permute-done.8.q1, bf16[16,72,128]{2,1,0:T(8,128)(2,1)S(1)} %collective-permute-done.11.q2, ...), custom_call_target="tpu_custom_call" | custom-call | tf_op jit(solution)/shard_map/refresh/pallas_call | solution.py:306
  (16 shorter events, 0.2 us)
Async XLA Ops:
  7.2 66.9 %copy-start.5 = (s32[1,136]{1,0:T(1,128)S(1)}, s32[1,136]{1,0:T(1,128)}, u32[]{:S(2)}) copy-start(s32[1,136]{1,0:T(1,128)} %loss_weight.3) | copy-start | bytes 1636
  7.2 66.9 %copy-start = (bf16[1,136,8192]{2,1,0:T(8,128)(2,1)S(1)}, bf16[1,136,8192]{2,1,0:T(8,128)(2,1)}, u32[]{:S(2)}) copy-start(bf16[1,136,8192]{2,1,0:T(8,128)(2,1)} %param.11) | copy-start | bytes 6684676
  7.2 135.3 %all-gather.3.cloned.1.call-start = ((), (), s32[]{:S(2)}) async-start(), calls=%async_computation.3 | async-start | bytes 5013504 | tf_op jit(solution)/shard_map/all_gather | solution.py:237
  9.2 10.4 %collective-permute-start = (bf16[576,128]{1,0:T(8,128)(2,1)}, bf16[576,128]{1,0:T(8,128)(2,1)S(1)}, u32[]{:S(2)}, u32[]{:S(2)}) collective-permute-start(bf16[576,128]{1,0:T(8,128)(2,1)} %get-tuple-element.24), channel_id=1, source_target_pairs={{64,0},{66,2},{128,64},{130,66},{192,128},{194,130},{256,192},{258... | collective-permute-start | bytes 442376 | tf_op jit(solution)/shard_map/ppermute | solution.py:231
  11.6 11.8 %collective-permute-start.1 = (bf16[576,128]{1,0:T(8,128)(2,1)}, bf16[576,128]{1,0:T(8,128)(2,1)S(1)}, u32[]{:S(2)}, u32[]{:S(2)}) collective-permute-start(bf16[576,128]{1,0:T(8,128)(2,1)} %get-tuple-element.24), channel_id=1, source_target_pairs={{66,0},{64,2},{130,64},{128,66},{194,128},{192,130},{258,192},{256... | collective-permute-start | bytes 442376 | tf_op jit(solution)/shard_map/ppermute | solution.py:232
  52.3 13.9 %collective-permute-start.2 = (bf16[16,72,128]{2,1,0:T(8,128)(2,1)S(1)}, bf16[16,72,128]{2,1,0:T(8,128)(2,1)S(1)}, u32[]{:S(2)}, u32[]{:S(2)}) collective-permute-start(bf16[16,72,128]{2,1,0:T(8,128)(2,1)S(1)} %all_to_all.15.q0), channel_id=1, source_target_pairs={{0,2},{2,0},{1,3},{3,1},{4,6},{6,4},{5,7},{7,5},{8,10},{10,8},{9,1... | collective-permute-start | bytes 884744 | tf_op jit(solution)/shard_map/ppermute | solution.py:33
  54.5 18.4 %collective-permute-start.3 = (bf16[16,72,128]{2,1,0:T(8,128)(2,1)S(1)}, bf16[16,72,128]{2,1,0:T(8,128)(2,1)S(1)}, u32[]{:S(2)}, u32[]{:S(2)}) collective-permute-start(bf16[16,72,128]{2,1,0:T(8,128)(2,1)S(1)} %all_to_all.15.q0), channel_id=1, source_target_pairs={{0,1},{1,0},{2,3},{3,2},{4,5},{5,4},{6,7},{7,6},{8,9},{9,8},{10,11... | collective-permute-start | bytes 884744 | tf_op jit(solution)/shard_map/ppermute | solution.py:33
  66.2 7.9 %collective-permute-start.4 = (bf16[16,72,128]{2,1,0:T(8,128)(2,1)S(1)}, bf16[16,72,128]{2,1,0:T(8,128)(2,1)S(1)}, u32[]{:S(2)}, u32[]{:S(2)}) collective-permute-start(bf16[16,72,128]{2,1,0:T(8,128)(2,1)S(1)} %collective-permute-done.2.q1), channel_id=1, source_target_pairs={{0,1},{1,0},{2,3},{3,2},{4,5},{5,4},{6,7},{7,6},{8,9},{9,8},{10,11... | collective-permute-start | bytes 884744 | tf_op jit(solution)/shard_map/ppermute | solution.py:33
  74.1 0.9 copy-start.4
  79.2 4.0 %copy-start.6 = (bf16[136,576]{1,0:T(8,128)(2,1)}, bf16[136,576]{1,0:T(8,128)(2,1)S(1)}, u32[]{:S(2)}) copy-start(bf16[136,576]{1,0:T(8,128)(2,1)S(1)} %get-tuple-element.28) | copy-start | bytes 470020
  79.2 3.9 %collective-permute-start.5 = (bf16[2,16,72,128]{3,2,1,0:T(8,128)(2,1)S(1)}, bf16[2,16,72,128]{3,2,1,0:T(8,128)(2,1)S(1)}, u32[]{:S(2)}, u32[]{:S(2)}) collective-permute-start(bf16[2,16,72,128]{3,2,1,0:T(8,128)(2,1)S(1)} %get-tuple-element.27), channel_id=1, source_target_pairs={{0,1},{1,0},{2,3},{3,2},{4,5},{5,4},{6,7},{7,6},{8,9},{9,8},{10,11... | collective-permute-start | bytes 1769480 | tf_op jit(solution)/shard_map/ppermute | solution.py:33
  83.2 18.7 %copy-start.13 = (f32[1,1,512]{2,1,0:T(1,128)S(1)}, f32[1,1,512]{2,1,0:T(1,128)}, u32[]{:S(2)}) copy-start(f32[1,1,512]{2,1,0:T(1,128)} %param.19) | copy-start | bytes 6148
  83.2 20.6 %copy-start.12 = (f32[1,1,512]{2,1,0:T(1,128)S(1)}, f32[1,1,512]{2,1,0:T(1,128)}, u32[]{:S(2)}) copy-start(f32[1,1,512]{2,1,0:T(1,128)} %param.20) | copy-start | bytes 6148
  83.3 18.6 %copy-start.7 = (bf16[136,576]{1,0:T(8,128)(2,1)S(1)}, bf16[136,576]{1,0:T(8,128)(2,1)}, u32[]{:S(2)}) copy-start(bf16[136,576]{1,0:T(8,128)(2,1)} %copy-done.6) | copy-start | bytes 470020
  83.3 34.4 %copy-start.11 = (f32[1,1,512]{2,1,0:T(1,128)S(1)}, f32[1,1,512]{2,1,0:T(1,128)}, u32[]{:S(2)}) copy-start(f32[1,1,512]{2,1,0:T(1,128)} %param.18) | copy-start | bytes 6148
  83.3 34.4 %copy-start.8 = (f32[1,128,64]{1,2,0:T(8,128)S(1)}, f32[1,128,64]{1,2,0:T(8,128)}, u32[]{:S(2)}) copy-start(f32[1,128,64]{1,2,0:T(8,128)} %param.15) | copy-start | bytes 98308
  83.3 34.4 %copy-start.9 = (f32[1,128,64]{1,2,0:T(8,128)S(1)}, f32[1,128,64]{1,2,0:T(8,128)}, u32[]{:S(2)}) copy-start(f32[1,128,64]{1,2,0:T(8,128)} %param.17) | copy-start | bytes 98308
  83.4 34.4 %copy-start.10 = (f32[1,128,64]{1,2,0:T(8,128)S(1)}, f32[1,128,64]{1,2,0:T(8,128)}, u32[]{:S(2)}) copy-start(f32[1,128,64]{1,2,0:T(8,128)} %param.16) | copy-start | bytes 98308
  83.4 10.4 %collective-permute-start.6 = (bf16[16,72,128]{2,1,0:T(8,128)(2,1)S(1)}, bf16[16,72,128]{2,1,0:T(8,128)(2,1)S(1)}, u32[]{:S(2)}, u32[]{:S(2)}) collective-permute-start(bf16[16,72,128]{2,1,0:T(8,128)(2,1)S(1)} %fusion.2), channel_id=1, source_target_pairs={{0,2},{2,0},{1,3},{3,1},{4,6},{6,4},{5,7},{7,5},{8,10},{10,8},{9,1... | collective-permute-start | bytes 884744 | tf_op jit(solution)/shard_map/ppermute | solution.py:33
  94.5 23.1 %all-to-all-start.1 = ((bf16[16,72,128]{2,1,0:T(8,128)(2,1)}), bf16[16,72,128]{2,1,0:T(8,128)(2,1)S(1)}, u32[]{:S(2)}, u32[]{:S(2)}) async-start(bf16[16,72,128]{2,1,0:T(8,128)(2,1)} %fusion.1), calls=%async_computation.1 | async-start | bytes 589824 | tf_op jit(solution)/shard_map/all_to_all | solution.py:260
  101.9 10.1 %collective-permute-start.7 = (bf16[136,576]{1,0:T(8,128)(2,1)S(1)}, bf16[136,576]{1,0:T(8,128)(2,1)S(1)}, u32[]{:S(2)}, u32[]{:S(2)}) collective-permute-start(bf16[136,576]{1,0:T(8,128)(2,1)S(1)} %copy-done.7), channel_id=1, source_target_pairs={{64,0},{128,64},{192,128},{256,192},{320,256},{384,320},{448,384},... | collective-permute-start | bytes 470024 | tf_op jit(solution)/shard_map/ppermute | solution.py:256
  112.0 41.6 %copy-start.2 = (bf16[136,576]{1,0:T(8,128)(2,1)}, bf16[136,576]{1,0:T(8,128)(2,1)S(1)}, u32[]{:S(2)}) copy-start(bf16[136,576]{1,0:T(8,128)(2,1)S(1)} %collective-permute-done.7.rows) | copy-start | bytes 470020
  142.4 24.7 %collective-permute-start.10 = (bf16[32,576,128]{2,1,0:T(8,128)(2,1)}, bf16[32,576,128]{2,1,0:T(8,128)(2,1)S(1)}, u32[]{:S(2)}, u32[]{:S(2)}) collective-permute-start(bf16[32,576,128]{2,1,0:T(8,128)(2,1)} %all-gather.3.cloned.1.call-done.weights), channel_id=1, source_target_pairs={{0,1},{1,0},{2,3},{3,2},{4,5},{5,4},{6,7},{7,6},{8,9},{9,8},{10,11... | collective-permute-start | bytes 14155784 | tf_op jit(solution)/shard_map/ppermute | solution.py:33
  151.3 10.5 %collective-permute-start.8 = (bf16[16,72,128]{2,1,0:T(8,128)(2,1)S(1)}, bf16[16,72,128]{2,1,0:T(8,128)(2,1)S(1)}, u32[]{:S(2)}, u32[]{:S(2)}) collective-permute-start(bf16[16,72,128]{2,1,0:T(8,128)(2,1)S(1)} %all_to_all.16.q0), channel_id=1, source_target_pairs={{0,2},{2,0},{1,3},{3,1},{4,6},{6,4},{5,7},{7,5},{8,10},{10,8},{9,1... | collective-permute-start | bytes 884744 | tf_op jit(solution)/shard_map/ppermute | solution.py:33
  161.9 12.4 %collective-permute-start.9 = (bf16[16,72,128]{2,1,0:T(8,128)(2,1)S(1)}, bf16[16,72,128]{2,1,0:T(8,128)(2,1)S(1)}, u32[]{:S(2)}, u32[]{:S(2)}) collective-permute-start(bf16[16,72,128]{2,1,0:T(8,128)(2,1)S(1)} %collective-permute-done.8.q1), channel_id=1, source_target_pairs={{0,1},{1,0},{2,3},{3,2},{4,5},{5,4},{6,7},{7,6},{8,9},{9,8},{10,11... | collective-permute-start | bytes 884744 | tf_op jit(solution)/shard_map/ppermute | solution.py:33
  164.6 9.7 %collective-permute-start.11 = (bf16[16,72,128]{2,1,0:T(8,128)(2,1)S(1)}, bf16[16,72,128]{2,1,0:T(8,128)(2,1)S(1)}, u32[]{:S(2)}, u32[]{:S(2)}) collective-permute-start(bf16[16,72,128]{2,1,0:T(8,128)(2,1)S(1)} %all_to_all.16.q0), channel_id=1, source_target_pairs={{0,1},{1,0},{2,3},{3,2},{4,5},{5,4},{6,7},{7,6},{8,9},{9,8},{10,11... | collective-permute-start | bytes 884744 | tf_op jit(solution)/shard_map/ppermute | solution.py:33
  167.1 1.2 copy-start.1
  168.4 0.9 copy-start.3
Sparse Core Ops, SparseCore 0:
  24.4 92.5 all-gather.2

commit v5 on v3

--- a/solution.py
+++ b/solution.py
@@ -31,12 +31,6 @@
 
 def swap(array, axis):
     return lax.ppermute(array, axis, [(0, 1), (1, 0)])
-
-
-def quarters(got, beside=None):
-    got_yl = swap(got, "yl")
-    got_yl, beside = after(got_yl, beside)
-    return (got, got_yl, swap(got, "core"), swap(got_yl, "core")), beside
 
 
 def after(value, *others):
@@ -167,20 +161,29 @@
     out[...] = (adapter_scale * nn(low, up)).astype(bf16)
 
 
-def side_by_side(blocks):
-    return jnp.concatenate([blocks[i] for i in range(blocks.shape[0])], axis=1)
-
-
-def own_columns_kernel(rows, weights, out):
-    out[...] = nn(rows[...], side_by_side(weights)).astype(bf16)
-
-
-def all_columns_kernel(place, rows, weights, mine, out):
+def columns_kernel(rows_mine, rows_other, weights, mine, other, held, sems):
+    chunks = sems.shape[0]
+    size = held.shape[0] // chunks
+    parts = [pl.ds(k * size, size) for k in range(chunks)]
+    copies = [
+        pltpu.make_async_copy(weights.at[part], held.at[part], sems.at[k])
+        for k, part in enumerate(parts)
+    ]
+    for copy in copies:
+        copy.start()
+    for k in range(chunks):
+        copies[k].wait()
+        for i in range(k * size, (k + 1) * size, 2):
+            pair = jnp.concatenate([held[i], held[i + 1]], axis=1)
+            mine[:, i * LANES : (i + 2) * LANES] = nn(rows_mine[...], pair).astype(bf16)
+            other[:, i * LANES : (i + 2) * LANES] = nn(rows_other[...], pair).astype(bf16)
+
+
+def merge_kernel(place, mine, other, out):
     core = place[0]
-    other = nn(rows[...], side_by_side(weights)).astype(bf16)
-    for i in range(weights.shape[0]):
+    for i in range(mine.shape[1] // LANES):
+        a, b = mine[:, i * LANES : (i + 1) * LANES], other[:, i * LANES : (i + 1) * LANES]
         at = i * 2 * LANES
-        a, b = mine[:, i * LANES : (i + 1) * LANES], other[:, i * LANES : (i + 1) * LANES]
         out[:, at : at + LANES] = jnp.where(core == 0, a, b)
         out[:, at + LANES : at + 2 * LANES] = jnp.where(core == 0, b, a)
 
@@ -222,7 +225,7 @@
         ),
         in_specs=whole(4),
         out_specs=tuple(whole(2)),
-        compiler_params=params,
+        compiler_params=pltpu.CompilerParams(vmem_limit_bytes=60 * 1024 * 1024),
         name="prepare",
     )(down_master[0].T, up_master[0], loss_weight, value_weight[0])
 
@@ -235,12 +238,11 @@
     flipped = lax.ppermute(weights, ("section", "yl"), from_next(1))
 
     got = spread(copies)
-    got, same, flipped = after(got, same, flipped)
     even = lax.axis_index("yl") == 0
     weights = jnp.stack([jnp.where(even, same, flipped), jnp.where(even, flipped, same)])
-    weights_mine = lax.all_gather(weights, "z").reshape(2 * z, features + rank, LANES)
-
-    blocks, _ = quarters(got)
+    got_yl, weights = after(swap(got, "yl"), weights)
+    weights_all = lax.all_gather(weights, "z").reshape(2 * z, features + rank, LANES)
+
     keep, send, next_rows = pl.pallas_call(
         backward_kernel,
         out_shape=(
@@ -256,12 +258,20 @@
         ],
         compiler_params=params,
         name="backward",
-    )(place, *blocks, acts, value_grad[0], loss_weight)
-    next_rows = lax.ppermute(next_rows, "section", [(s, s - 1) for s in range(1, sections)])
+    )(place, got, got_yl, swap(got, "core"), swap(got_yl, "core"), acts, value_grad[0], loss_weight)
+    rows_mine, rows_other = [
+        lax.ppermute(
+            next_rows,
+            ("section", "core"),
+            [(s * 2 + (c ^ flip), (s - 1) * 2 + c) for s in range(1, sections) for c in range(2)],
+        )
+        for flip in range(2)
+    ]
 
     kept = keep + swap(send, "core").astype(f32)
     kept = kept[0] + swap(kept[1].astype(bf16), "yl").astype(f32)
-    parts, next_rows = after(lax.all_to_all(kept.astype(bf16), "z", 0, 0), next_rows)
+    parts = lax.all_to_all(kept.astype(bf16), "z", 0, 0)
+    parts, rows_mine, rows_other = after(parts, rows_mine, rows_other)
     grad = jnp.sum(parts.astype(f32), axis=0)
 
     count = step_count.astype(f32)[0]
@@ -273,27 +283,29 @@
     )
     block = pad_rows([down_new.astype(bf16), up_new.astype(bf16).reshape(up_rows, LANES)], rows)
     got = spread(jnp.broadcast_to(block[None], (z, rows, LANES)))
-    got, weights_mine = after(got, weights_mine)
-    weights_other = swap(weights_mine, "core")
-    chunk = min(4, 2 * z)
-    rows_spec = pl.BlockSpec((tokens, features + rank), lambda i: (0, 0))
-    w_spec = pl.BlockSpec((chunk, features + rank, LANES), lambda i: (i, 0, 0))
-    half_spec = pl.BlockSpec((tokens, chunk * LANES), lambda i: (0, i))
-    own_columns = pl.pallas_call(
-        own_columns_kernel,
-        out_shape=jax.ShapeDtypeStruct((tokens, width // 2), bf16),
-        grid=(2 * z // chunk,),
-        in_specs=[rows_spec, w_spec],
-        out_specs=half_spec,
-        compiler_params=pltpu.CompilerParams(vmem_limit_bytes=56 * 1024 * 1024),
+    got_yl = swap(got, "yl")
+    got_core, got_last = swap(got, "core"), swap(got_yl, "core")
+    weights_all, _, _ = after(weights_all, got_last, got_core)
+    chunks = 4
+    half = jax.ShapeDtypeStruct((tokens, width // 2), bf16)
+    mine, other = pl.pallas_call(
+        columns_kernel,
+        out_shape=(half, half),
+        in_specs=whole(2) + [pl.BlockSpec(memory_space=pl.ANY)],
+        out_specs=tuple(whole(2)),
+        scratch_shapes=[
+            pltpu.VMEM((2 * z, features + rank, LANES), bf16),
+            pltpu.SemaphoreType.DMA((min(chunks, z),)),
+        ],
+        compiler_params=pltpu.CompilerParams(vmem_limit_bytes=52 * 1024 * 1024),
         cost_estimate=pl.CostEstimate(
-            flops=tokens * (features + rank) * width,
-            bytes_accessed=(features + rank) * width + tokens * width,
+            flops=2 * tokens * (features + rank) * width,
+            bytes_accessed=(features + rank) * width,
             transcendentals=0,
         ),
-        name="own_columns",
-    )(next_rows, weights_mine)
-    blocks, own_columns = quarters(got, own_columns)
+        name="columns",
+    )(rows_mine, rows_other, weights_all)
+    other = swap(other, "core")
     refreshed = pl.pallas_call(
         refresh_kernel,
         out_shape=jax.ShapeDtypeStruct((tokens, features), bf16),
@@ -305,17 +317,20 @@
         ],
         compiler_params=params,
         name="refresh",
-    )(place, *blocks, acts)
-
+    )(place, got, got_yl, got_core, got_last, acts)
+
+    other, refreshed = after(other, refreshed)
+    steps = 2
+    half_spec = pl.BlockSpec((tokens, width // 2 // steps), lambda i: (0, i))
     upstream = pl.pallas_call(
-        all_columns_kernel,
+        merge_kernel,
         out_shape=jax.ShapeDtypeStruct((tokens, width), bf16),
-        grid=(2 * z // chunk,),
-        in_specs=[SCALARS, rows_spec, w_spec, half_spec],
-        out_specs=pl.BlockSpec((tokens, chunk * 2 * LANES), lambda i: (0, i)),
+        grid=(steps,),
+        in_specs=[SCALARS, half_spec, half_spec],
+        out_specs=pl.BlockSpec((tokens, width // steps), lambda i: (0, i)),
         compiler_params=params,
-        name="all_columns",
-    )(place, next_rows, weights_other, own_columns)
+        name="merge",
+    )(place, mine, other)
     return (
         upstream[None],
         refreshed[None],

time: 179 us -> 176 us (0.983)
  Pallas kernels: 19.5 us -> 15.7 us
  starting transfers between devices: 69 us -> 72.1 us
  waiting for transfers between devices: 38 us -> 35.8 us
    all_to_all x1, waiting for transfers between devices: 0.01 us -> 8.05 us  [spread(): return lax.all_to_all(copies, 'z', 0, 0)]
    all_to_all x1, waiting for transfers between devices: 8.86 us -> 3.62 us  [per_device(): parts = lax.all_to_all(kept.astype(bf16), 'z', 0, 0)]
    pallas_call x2, Pallas kernels: 12 us -> 7.05 us  [the longest x1 4.85 us: per_device(): pl.pallas_call(columns_kernel, out_shape=(half, half), in_specs=whole(2)...]
    ppermute x9, waiting for transfers between devices: 10.4 us -> 15.2 us  [swap(): return lax.ppermute(array, axis, [(0, 1), (1, 0)])]
    ppermute x1, waiting for transfers between devices: 4.25 us -> 0.01 us  [per_device(): same = lax.ppermute(weights, ('section', 'yl'), from_next(0))]
    ppermute x1, waiting for transfers between devices: 4.04 us -> 0.01 us  [per_device(): flipped = lax.ppermute(weights, ('section', 'yl'), from_next(1))]
    ppermute x1 -> x2, starting transfers between devices: 2.33 us -> 5.92 us  [per_device(): lax.ppermute(next_rows, ('section', 'core'), [(s * 2 + (c ^ flip), (s - 1...]
    all_gather x1, waiting for transfers between devices: 2.75 us -> 0.01 us  [per_device(): lax.all_gather(weights, 'z').reshape(2 * z, features + rank, LANES)]
  transfers between devices with their start and end apart: 15 -> 16, of which waited for: 9 -> 9; matrix products, arithmetic and copies ran while one was open for 1% -> 2% of each run, Pallas kernels for 8% -> 4%
where the time goes in v5:
time: 176 us; the launch traced here: 174 us
  starting transfers between devices  72.1 us (41%)
  waiting for transfers between devices  35.8 us (20%)
  blocking collectives  27.8 us (16%)
  Pallas kernels  15.7 us (9%)
  between operations  15.1 us (9%)
  local copies, waits for them, and re-layouts  4.31 us (2%)
  other arithmetic  3.19 us (2%)
    ppermute x9, starting transfers between devices, swap(): return lax.ppermute(array, axis, [(0, 1), (1, 0)])  37.6 us
    all_to_all x1, blocking collectives, spread(): return lax.all_to_all(copies, 'z', 0, 0)  27.8 us
    ppermute x9, waiting for transfers between devices, swap(): return lax.ppermute(array, axis, [(0, 1), (1, 0)])  15.2 us
    all_to_all x1, starting transfers between devices, spread(): return lax.all_to_all(copies, 'z', 0, 0)  14.9 us
    ppermute x2, waiting for transfers between devices, per_device(): lax.ppermute(next_rows, ('section', 'core'), [(s * 2 + (c ^ flip), (s - 1...  8.95 us
    all_to_all x1, waiting for transfers between devices, spread(): return lax.all_to_all(copies, 'z', 0, 0)  8.05 us
    all_to_all x1, starting transfers between devices, per_device(): parts = lax.all_to_all(kept.astype(bf16), 'z', 0, 0)  7.96 us
    ppermute x2, starting transfers between devices, per_device(): lax.ppermute(next_rows, ('section', 'core'), [(s * 2 + (c ^ flip), (s - 1...  5.92 us
  transfers between devices with their start and end apart: 16, of which 9 were waited for; matrix products, arithmetic and copies ran while one was open for 2% of the time, Pallas kernels for 4%

profile of v5, /device:TPU:7, one launch (start us, length us, event | category | flops | bytes accessed | tf_op | source)
XLA Modules:
  0.0 174.0 jit_solution(12407099334264706876)
XLA Ops:
  7.2 0.0 copy-start.6
  7.2 0.0 copy-start
  7.2 1.9 %prepare.1 = (bf16[16,72,128]{2,1,0:T(8,128)(2,1)}, bf16[576,128]{1,0:T(8,128)(2,1)}) custom-call(f32[64,128]{1,0:T(8,128)} %bitcast.66, f32[1,512]{1,0:T(1,128)} %bitcast.68, s32[1,136]{1,0:T(1,128)} %loss_weight.3, bf16[128,512]{1,0:T(8,128)(2,1)} %bitcast.65), custom_call_target="tpu_custom_call" | custom-call | tf_op jit(solution)/shard_map/prepare/pallas_call | solution.py:220
  9.1 14.9 %all-to-all-start = ((bf16[16,72,128]{2,1,0:T(8,128)(2,1)}), bf16[16,72,128]{2,1,0:T(8,128)(2,1)S(1)}, u32[]{:S(2)}, u32[]{:S(2)}) async-start(bf16[16,72,128]{2,1,0:T(8,128)(2,1)} %get-tuple-element.23), calls=%async_computation | async-start | bytes 589824 | tf_op jit(solution)/shard_map/all_to_all | solution.py:41
  24.1 0.0 all-gather.3.cloned.1.call-start
  24.1 2.5 %collective-permute-start.1 = (bf16[576,128]{1,0:T(8,128)(2,1)}, bf16[576,128]{1,0:T(8,128)(2,1)S(1)}, u32[]{:S(2)}, u32[]{:S(2)}) collective-permute-start(bf16[576,128]{1,0:T(8,128)(2,1)} %get-tuple-element.24), channel_id=1, source_target_pairs={{64,0},{66,2},{128,64},{130,66},{192,128},{194,130},{256,192},{258... | collective-permute-start | bytes 442376 | tf_op jit(solution)/shard_map/ppermute | solution.py:237
  26.6 3.2 %collective-permute-start.2 = (bf16[576,128]{1,0:T(8,128)(2,1)}, bf16[576,128]{1,0:T(8,128)(2,1)S(1)}, u32[]{:S(2)}, u32[]{:S(2)}) collective-permute-start(bf16[576,128]{1,0:T(8,128)(2,1)} %get-tuple-element.24), channel_id=1, source_target_pairs={{66,0},{64,2},{130,64},{128,66},{194,128},{192,130},{258,192},{256... | collective-permute-start | bytes 442376 | tf_op jit(solution)/shard_map/ppermute | solution.py:238
  29.8 8.1 %all-to-all-done.q0 = bf16[16,72,128]{2,1,0:T(8,128)(2,1)S(1)} async-done(((bf16[16,72,128]{2,1,0:T(8,128)(2,1)}), bf16[16,72,128]{2,1,0:T(8,128)(2,1)S(1)}, u32[]{:S(2)}, u32[]{:S(2)}) %all-to-all-start) | async-done | bytes 294944 | tf_op jit(solution)/shard_map/all_to_all | solution.py:41
  37.8 3.2 %collective-permute-start = (bf16[16,72,128]{2,1,0:T(8,128)(2,1)S(1)}, bf16[16,72,128]{2,1,0:T(8,128)(2,1)S(1)}, u32[]{:S(2)}, u32[]{:S(2)}) collective-permute-start(bf16[16,72,128]{2,1,0:T(8,128)(2,1)S(1)} %all-to-all-done.q0), channel_id=1, source_target_pairs={{0,2},{2,0},{1,3},{3,1},{4,6},{6,4},{5,7},{7,5},{8,10},{10,8},{9,1... | collective-permute-start | bytes 884744 | tf_op jit(solution)/shard_map/ppermute | solution.py:33
  41.0 0.0 collective-permute-done.1
  41.0 0.0 collective-permute-done.2
  41.1 0.7 pad_maximum_fusion
  41.8 3.5 %collective-permute-done.q1 = bf16[16,72,128]{2,1,0:T(8,128)(2,1)S(1)} collective-permute-done((bf16[16,72,128]{2,1,0:T(8,128)(2,1)S(1)}, bf16[16,72,128]{2,1,0:T(8,128)(2,1)S(1)}, u32[]{:S(2)}, u32[]{:S(2)}) %collective-permute-start) | collective-permute-done | bytes 294944 | tf_op jit(solution)/shard_map/ppermute | solution.py:33
  45.3 0.0 all-gather.3.cloned.1.call-update
  45.3 9.5 %collective-permute-start.3 = (bf16[16,72,128]{2,1,0:T(8,128)(2,1)S(1)}, bf16[16,72,128]{2,1,0:T(8,128)(2,1)S(1)}, u32[]{:S(2)}, u32[]{:S(2)}) collective-permute-start(bf16[16,72,128]{2,1,0:T(8,128)(2,1)S(1)} %all-to-all-done.q0), channel_id=1, source_target_pairs={{0,1},{1,0},{2,3},{3,2},{4,5},{5,4},{6,7},{7,6},{8,9},{9,8},{10,11... | collective-permute-start | bytes 884744 | tf_op jit(solution)/shard_map/ppermute | solution.py:33
  54.8 1.9 %collective-permute-start.4 = (bf16[16,72,128]{2,1,0:T(8,128)(2,1)S(1)}, bf16[16,72,128]{2,1,0:T(8,128)(2,1)S(1)}, u32[]{:S(2)}, u32[]{:S(2)}) collective-permute-start(bf16[16,72,128]{2,1,0:T(8,128)(2,1)S(1)} %collective-permute-done.q1), channel_id=1, source_target_pairs={{0,1},{1,0},{2,3},{3,2},{4,5},{5,4},{6,7},{7,6},{8,9},{9,8},{10,11... | collective-permute-start | bytes 884744 | tf_op jit(solution)/shard_map/ppermute | solution.py:33
  56.8 0.1 pad_add_fusion.place
  56.8 0.0 collective-permute-done.3.q2
  56.9 1.5 collective-permute-done.4.q3
  58.3 0.0 copy-done.6
  58.3 0.0 copy-done
  58.3 0.9 copy-done.5
  59.2 4.2 %backward.1 = (f32[2,16,72,128]{3,2,1,0:T(8,128)S(1)}, bf16[2,16,72,128]{3,2,1,0:T(8,128)(2,1)S(1)}, bf16[136,576]{1,0:T(8,128)(2,1)S(1)}) custom-call(s32[2]{0:T(128)S(1)} %pad_add_fusion.place, bf16[16,72,128]{2,1,0:T(8,128)(2,1)S(1)} %all-to-all-done.q0, bf16[16,72,128]{2,1,0:T(8,128)(2,1)S(1)} %collective-permute-done.q1, ...), custom_call_target="tpu_custom_call" | custom-call | tf_op jit(solution)/shard_map/backward/pallas_call | solution.py:246
  63.5 0.0 copy-start.7
  63.5 2.0 %collective-permute-start.5 = (bf16[2,16,72,128]{3,2,1,0:T(8,128)(2,1)S(1)}, bf16[2,16,72,128]{3,2,1,0:T(8,128)(2,1)S(1)}, u32[]{:S(2)}, u32[]{:S(2)}) collective-permute-start(bf16[2,16,72,128]{3,2,1,0:T(8,128)(2,1)S(1)} %get-tuple-element.27), channel_id=1, source_target_pairs={{0,1},{1,0},{2,3},{3,2},{4,5},{5,4},{6,7},{7,6},{8,9},{9,8},{10,11... | collective-permute-start | bytes 1769480 | tf_op jit(solution)/shard_map/ppermute | solution.py:33
  65.5 1.8 %collective-permute-done.5 = bf16[2,16,72,128]{3,2,1,0:T(8,128)(2,1)S(1)} collective-permute-done((bf16[2,16,72,128]{3,2,1,0:T(8,128)(2,1)S(1)}, bf16[2,16,72,128]{3,2,1,0:T(8,128)(2,1)S(1)}, u32[]{:S(2)}, u32[]{:S(2)}) %collective-permute-start.5) | collective-permute-done | bytes 589856 | tf_op jit(solution)/shard_map/ppermute | solution.py:33
  67.4 0.1 convert_add_fusion
  67.5 0.0 copy-done.7
  67.5 0.0 copy-start.14
  67.5 0.0 copy-start.13
  67.6 0.0 copy-start.8
  67.6 0.0 copy-start.12
  67.6 0.0 copy-start.9
  67.6 0.0 copy-start.10
  67.6 0.0 copy-start.11
  67.6 3.3 %collective-permute-start.6 = (bf16[16,72,128]{2,1,0:T(8,128)(2,1)S(1)}, bf16[16,72,128]{2,1,0:T(8,128)(2,1)S(1)}, u32[]{:S(2)}, u32[]{:S(2)}) collective-permute-start(bf16[16,72,128]{2,1,0:T(8,128)(2,1)S(1)} %fusion.2), channel_id=1, source_target_pairs={{0,2},{2,0},{1,3},{3,1},{4,6},{6,4},{5,7},{7,5},{8,10},{10,8},{9,1... | collective-permute-start | bytes 884744 | tf_op jit(solution)/shard_map/ppermute | solution.py:33
  71.0 7.2 %collective-permute-done.6 = bf16[16,72,128]{2,1,0:T(8,128)(2,1)S(1)} collective-permute-done((bf16[16,72,128]{2,1,0:T(8,128)(2,1)S(1)}, bf16[16,72,128]{2,1,0:T(8,128)(2,1)S(1)}, u32[]{:S(2)}, u32[]{:S(2)}) %collective-permute-start.6) | collective-permute-done | bytes 294944 | tf_op jit(solution)/shard_map/ppermute | solution.py:33
  78.2 0.8 fusion.1
  79.0 8.0 %all-to-all-start.1 = ((bf16[16,72,128]{2,1,0:T(8,128)(2,1)}), bf16[16,72,128]{2,1,0:T(8,128)(2,1)S(1)}, u32[]{:S(2)}, u32[]{:S(2)}) async-start(bf16[16,72,128]{2,1,0:T(8,128)(2,1)} %fusion.1), calls=%async_computation.1 | async-start | bytes 589824 | tf_op jit(solution)/shard_map/all_to_all | solution.py:273
  87.7 0.1 pad.2.clone
  87.8 2.5 %collective-permute-start.7 = (bf16[136,576]{1,0:T(8,128)(2,1)S(1)}, bf16[136,576]{1,0:T(8,128)(2,1)S(1)}, u32[]{:S(2)}, u32[]{:S(2)}) collective-permute-start(bf16[136,576]{1,0:T(8,128)(2,1)S(1)} %copy-done.8), channel_id=1, source_target_pairs={{64,0},{65,1},{128,64},{129,65},{192,128},{193,129},{256,192},{257... | collective-permute-start | bytes 470024 | tf_op jit(solution)/shard_map/ppermute | solution.py:263
  90.3 3.5 %collective-permute-start.8 = (bf16[136,576]{1,0:T(8,128)(2,1)S(1)}, bf16[136,576]{1,0:T(8,128)(2,1)S(1)}, u32[]{:S(2)}, u32[]{:S(2)}) collective-permute-start(bf16[136,576]{1,0:T(8,128)(2,1)S(1)} %copy-done.8), channel_id=1, source_target_pairs={{65,0},{64,1},{129,64},{128,65},{193,128},{192,129},{257,192},{256... | collective-permute-start | bytes 470024 | tf_op jit(solution)/shard_map/ppermute | solution.py:263
  93.7 4.3 %collective-permute-done.7.rows_mine = bf16[136,576]{1,0:T(8,128)(2,1)S(1)} collective-permute-done((bf16[136,576]{1,0:T(8,128)(2,1)S(1)}, bf16[136,576]{1,0:T(8,128)(2,1)S(1)}, u32[]{:S(2)}, u32[]{:S(2)}) %collective-permute-start.7) | collective-permute-done | bytes 156704 | tf_op jit(solution)/shard_map/ppermute | solution.py:263
  98.1 0.7 copy-done.1
  98.8 4.6 %collective-permute-done.8.rows_other = bf16[136,576]{1,0:T(8,128)(2,1)S(1)} collective-permute-done((bf16[136,576]{1,0:T(8,128)(2,1)S(1)}, bf16[136,576]{1,0:T(8,128)(2,1)S(1)}, u32[]{:S(2)}, u32[]{:S(2)}) %collective-permute-start.8) | collective-permute-done | bytes 156704 | tf_op jit(solution)/shard_map/ppermute | solution.py:263
  103.4 0.7 copy-done.3
  104.0 3.6 %all-to-all-done.1 = bf16[16,72,128]{2,1,0:T(8,128)(2,1)S(1)} async-done(((bf16[16,72,128]{2,1,0:T(8,128)(2,1)}), bf16[16,72,128]{2,1,0:T(8,128)(2,1)S(1)}, u32[]{:S(2)}, u32[]{:S(2)}) %all-to-all-start.1) | async-done | bytes 294944 | tf_op jit(solution)/shard_map/all_to_all | solution.py:273
  107.8 0.7 fusion.10
  108.4 0.1 maximum_maximum_fusion
  108.5 27.8 %all_to_all.15.q0 = bf16[16,72,128]{2,1,0:T(8,128)(2,1)S(1)} all-to-all(bf16[16,72,128]{2,1,0:T(8,128)(2,1)S(1)} %broadcast_in_dim.28), channel_id=1, replica_groups=mesh['section'=8,'z'=16,'yl'=2,'core'=2] {'z'}, dimensions={0} | all-to-all | bytes 589824 | tf_op jit(solution)/shard_map/all_to_all | solution.py:41
  136.4 3.3 %collective-permute-start.9 = (bf16[16,72,128]{2,1,0:T(8,128)(2,1)S(1)}, bf16[16,72,128]{2,1,0:T(8,128)(2,1)S(1)}, u32[]{:S(2)}, u32[]{:S(2)}) collective-permute-start(bf16[16,72,128]{2,1,0:T(8,128)(2,1)S(1)} %all_to_all.15.q0), channel_id=1, source_target_pairs={{0,2},{2,0},{1,3},{3,1},{4,6},{6,4},{5,7},{7,5},{8,10},{10,8},{9,1... | collective-permute-start | bytes 884744 | tf_op jit(solution)/shard_map/ppermute | solution.py:33
  139.7 6.8 %collective-permute-start.11 = (bf16[16,72,128]{2,1,0:T(8,128)(2,1)S(1)}, bf16[16,72,128]{2,1,0:T(8,128)(2,1)S(1)}, u32[]{:S(2)}, u32[]{:S(2)}) collective-permute-start(bf16[16,72,128]{2,1,0:T(8,128)(2,1)S(1)} %all_to_all.15.q0), channel_id=1, source_target_pairs={{0,1},{1,0},{2,3},{3,2},{4,5},{5,4},{6,7},{7,6},{8,9},{9,8},{10,11... | collective-permute-start | bytes 884744 | tf_op jit(solution)/shard_map/ppermute | solution.py:33
  146.5 0.0 collective-permute-done.9.q1
  146.5 5.2 %collective-permute-start.10 = (bf16[16,72,128]{2,1,0:T(8,128)(2,1)S(1)}, bf16[16,72,128]{2,1,0:T(8,128)(2,1)S(1)}, u32[]{:S(2)}, u32[]{:S(2)}) collective-permute-start(bf16[16,72,128]{2,1,0:T(8,128)(2,1)S(1)} %collective-permute-done.9.q1), channel_id=1, source_target_pairs={{0,1},{1,0},{2,3},{3,2},{4,5},{5,4},{6,7},{7,6},{8,9},{9,8},{10,11... | collective-permute-start | bytes 884744 | tf_op jit(solution)/shard_map/ppermute | solution.py:33
  151.7 0.0 collective-permute-done.11.q2
  151.7 1.2 collective-permute-done.10.q3
  152.9 0.9 copy-done.2
  153.8 0.9 copy-done.4
  154.8 4.8 %columns.1 = (bf16[136,4096]{1,0:T(8,128)(2,1)S(1)}, bf16[136,4096]{1,0:T(8,128)(2,1)}) custom-call(bf16[136,576]{1,0:T(8,128)(2,1)S(1)} %copy-done.2, bf16[136,576]{1,0:T(8,128)(2,1)S(1)} %copy-done.4, bf16[32,576,128]{2,1,0:T(8,128)(2,1)} %all-gather.3.cloned.1.call-done.weights), custom_call_target="tpu_custom_call" | custom-call | flops 1283457024 | bytes 4718592 | tf_op jit(solution)/shard_map/columns/pallas_call | solution.py:291
  159.6 2.3 %collective-permute-start.12 = (bf16[136,4096]{1,0:T(8,128)(2,1)}, bf16[136,4096]{1,0:T(8,128)(2,1)S(1)}, u32[]{:S(2)}, u32[]{:S(2)}) collective-permute-start(bf16[136,4096]{1,0:T(8,128)(2,1)} %get-tuple-element.35), channel_id=1, source_target_pairs={{0,1},{1,0},{2,3},{3,2},{4,5},{5,4},{6,7},{7,6},{8,9},{9,8},{10,11... | collective-permute-start | bytes 3342344 | tf_op jit(solution)/shard_map/ppermute | solution.py:33
  161.9 0.6 divide_subtract_fusion.1
  162.5 2.5 %refresh.1 = bf16[136,512]{1,0:T(8,128)(2,1)} custom-call(s32[2]{0:T(128)S(1)} %pad_add_fusion.place, bf16[16,72,128]{2,1,0:T(8,128)(2,1)S(1)} %all_to_all.15.q0, bf16[16,72,128]{2,1,0:T(8,128)(2,1)S(1)} %collective-permute-done.9.q1, bf16[16,72,128]{2,1,0:T(8,128)(2,1)S(1)} %collective-permute-done.11.q2, ...), custom_call_target="tpu_custom_call" | custom-call | tf_op jit(solution)/shard_map/refresh/pallas_call | solution.py:309
  165.0 0.0 collective-permute-done.12.other
  165.0 2.2 %merge.1 = bf16[136,8192]{1,0:T(8,128)(2,1)} custom-call(s32[2]{0:T(128)S(1)} %pad_add_fusion.place, bf16[136,4096]{1,0:T(8,128)(2,1)S(1)} %get-tuple-element.34.mine, bf16[136,4096]{1,0:T(8,128)(2,1)S(1)} %collective-permute-done.12.other), custom_call_target="tpu_custom_call" | custom-call | tf_op jit(solution)/shard_map/merge/pallas_call | solution.py:325
  (21 shorter events, 0.2 us)
Async XLA Ops:
  7.2 51.2 %copy-start.6 = (s32[1,136]{1,0:T(1,128)S(1)}, s32[1,136]{1,0:T(1,128)}, u32[]{:S(2)}) copy-start(s32[1,136]{1,0:T(1,128)} %loss_weight.3) | copy-start | bytes 1636
  7.2 51.1 %copy-start = (bf16[1,136,8192]{2,1,0:T(8,128)(2,1)S(1)}, bf16[1,136,8192]{2,1,0:T(8,128)(2,1)}, u32[]{:S(2)}) copy-start(bf16[1,136,8192]{2,1,0:T(8,128)(2,1)} %param.11) | copy-start | bytes 6684676
  9.1 28.7 %all-to-all-start = ((bf16[16,72,128]{2,1,0:T(8,128)(2,1)}), bf16[16,72,128]{2,1,0:T(8,128)(2,1)S(1)}, u32[]{:S(2)}, u32[]{:S(2)}) async-start(bf16[16,72,128]{2,1,0:T(8,128)(2,1)} %get-tuple-element.23), calls=%async_computation | async-start | bytes 589824 | tf_op jit(solution)/shard_map/all_to_all | solution.py:41
  24.1 128.9 %all-gather.3.cloned.1.call-start = ((), (), s32[]{:S(2)}) async-start(), calls=%async_computation.3 | async-start | bytes 5013504 | tf_op jit(solution)/shard_map/all_gather | solution.py:244
  24.1 16.9 %collective-permute-start.1 = (bf16[576,128]{1,0:T(8,128)(2,1)}, bf16[576,128]{1,0:T(8,128)(2,1)S(1)}, u32[]{:S(2)}, u32[]{:S(2)}) collective-permute-start(bf16[576,128]{1,0:T(8,128)(2,1)} %get-tuple-element.24), channel_id=1, source_target_pairs={{64,0},{66,2},{128,64},{130,66},{192,128},{194,130},{256,192},{258... | collective-permute-start | bytes 442376 | tf_op jit(solution)/shard_map/ppermute | solution.py:237
  26.6 14.5 %collective-permute-start.2 = (bf16[576,128]{1,0:T(8,128)(2,1)}, bf16[576,128]{1,0:T(8,128)(2,1)S(1)}, u32[]{:S(2)}, u32[]{:S(2)}) collective-permute-start(bf16[576,128]{1,0:T(8,128)(2,1)} %get-tuple-element.24), channel_id=1, source_target_pairs={{66,0},{64,2},{130,64},{128,66},{194,128},{192,130},{258,192},{256... | collective-permute-start | bytes 442376 | tf_op jit(solution)/shard_map/ppermute | solution.py:238
  37.8 7.5 %collective-permute-start = (bf16[16,72,128]{2,1,0:T(8,128)(2,1)S(1)}, bf16[16,72,128]{2,1,0:T(8,128)(2,1)S(1)}, u32[]{:S(2)}, u32[]{:S(2)}) collective-permute-start(bf16[16,72,128]{2,1,0:T(8,128)(2,1)S(1)} %all-to-all-done.q0), channel_id=1, source_target_pairs={{0,2},{2,0},{1,3},{3,1},{4,6},{6,4},{5,7},{7,5},{8,10},{10,8},{9,1... | collective-permute-start | bytes 884744 | tf_op jit(solution)/shard_map/ppermute | solution.py:33
  45.3 11.6 %collective-permute-start.3 = (bf16[16,72,128]{2,1,0:T(8,128)(2,1)S(1)}, bf16[16,72,128]{2,1,0:T(8,128)(2,1)S(1)}, u32[]{:S(2)}, u32[]{:S(2)}) collective-permute-start(bf16[16,72,128]{2,1,0:T(8,128)(2,1)S(1)} %all-to-all-done.q0), channel_id=1, source_target_pairs={{0,1},{1,0},{2,3},{3,2},{4,5},{5,4},{6,7},{7,6},{8,9},{9,8},{10,11... | collective-permute-start | bytes 884744 | tf_op jit(solution)/shard_map/ppermute | solution.py:33
  54.8 3.5 %collective-permute-start.4 = (bf16[16,72,128]{2,1,0:T(8,128)(2,1)S(1)}, bf16[16,72,128]{2,1,0:T(8,128)(2,1)S(1)}, u32[]{:S(2)}, u32[]{:S(2)}) collective-permute-start(bf16[16,72,128]{2,1,0:T(8,128)(2,1)S(1)} %collective-permute-done.q1), channel_id=1, source_target_pairs={{0,1},{1,0},{2,3},{3,2},{4,5},{5,4},{6,7},{7,6},{8,9},{9,8},{10,11... | collective-permute-start | bytes 884744 | tf_op jit(solution)/shard_map/ppermute | solution.py:33
  58.3 0.9 copy-start.5
  63.5 4.0 %copy-start.7 = (bf16[136,576]{1,0:T(8,128)(2,1)}, bf16[136,576]{1,0:T(8,128)(2,1)S(1)}, u32[]{:S(2)}) copy-start(bf16[136,576]{1,0:T(8,128)(2,1)S(1)} %get-tuple-element.28) | copy-start | bytes 470020
  63.5 3.9 %collective-permute-start.5 = (bf16[2,16,72,128]{3,2,1,0:T(8,128)(2,1)S(1)}, bf16[2,16,72,128]{3,2,1,0:T(8,128)(2,1)S(1)}, u32[]{:S(2)}, u32[]{:S(2)}) collective-permute-start(bf16[2,16,72,128]{3,2,1,0:T(8,128)(2,1)S(1)} %get-tuple-element.27), channel_id=1, source_target_pairs={{0,1},{1,0},{2,3},{3,2},{4,5},{5,4},{6,7},{7,6},{8,9},{9,8},{10,11... | collective-permute-start | bytes 1769480 | tf_op jit(solution)/shard_map/ppermute | solution.py:33
  67.5 20.3 %copy-start.14 = (f32[1,1,512]{2,1,0:T(1,128)S(1)}, f32[1,1,512]{2,1,0:T(1,128)}, u32[]{:S(2)}) copy-start(f32[1,1,512]{2,1,0:T(1,128)} %param.19) | copy-start | bytes 6148
  67.5 26.2 %copy-start.13 = (f32[1,1,512]{2,1,0:T(1,128)S(1)}, f32[1,1,512]{2,1,0:T(1,128)}, u32[]{:S(2)}) copy-start(f32[1,1,512]{2,1,0:T(1,128)} %param.20) | copy-start | bytes 6148
  67.6 20.2 %copy-start.8 = (bf16[136,576]{1,0:T(8,128)(2,1)S(1)}, bf16[136,576]{1,0:T(8,128)(2,1)}, u32[]{:S(2)}) copy-start(bf16[136,576]{1,0:T(8,128)(2,1)} %copy-done.7) | copy-start | bytes 470020
  67.6 40.1 %copy-start.12 = (f32[1,1,512]{2,1,0:T(1,128)S(1)}, f32[1,1,512]{2,1,0:T(1,128)}, u32[]{:S(2)}) copy-start(f32[1,1,512]{2,1,0:T(1,128)} %param.18) | copy-start | bytes 6148
  67.6 40.1 %copy-start.9 = (f32[1,128,64]{1,2,0:T(8,128)S(1)}, f32[1,128,64]{1,2,0:T(8,128)}, u32[]{:S(2)}) copy-start(f32[1,128,64]{1,2,0:T(8,128)} %param.15) | copy-start | bytes 98308
  67.6 40.1 %copy-start.10 = (f32[1,128,64]{1,2,0:T(8,128)S(1)}, f32[1,128,64]{1,2,0:T(8,128)}, u32[]{:S(2)}) copy-start(f32[1,128,64]{1,2,0:T(8,128)} %param.17) | copy-start | bytes 98308
  67.6 40.1 %copy-start.11 = (f32[1,128,64]{1,2,0:T(8,128)S(1)}, f32[1,128,64]{1,2,0:T(8,128)}, u32[]{:S(2)}) copy-start(f32[1,128,64]{1,2,0:T(8,128)} %param.16) | copy-start | bytes 98308
  67.6 10.6 %collective-permute-start.6 = (bf16[16,72,128]{2,1,0:T(8,128)(2,1)S(1)}, bf16[16,72,128]{2,1,0:T(8,128)(2,1)S(1)}, u32[]{:S(2)}, u32[]{:S(2)}) collective-permute-start(bf16[16,72,128]{2,1,0:T(8,128)(2,1)S(1)} %fusion.2), channel_id=1, source_target_pairs={{0,2},{2,0},{1,3},{3,1},{4,6},{6,4},{5,7},{7,5},{8,10},{10,8},{9,1... | collective-permute-start | bytes 884744 | tf_op jit(solution)/shard_map/ppermute | solution.py:33
  79.0 28.7 %all-to-all-start.1 = ((bf16[16,72,128]{2,1,0:T(8,128)(2,1)}), bf16[16,72,128]{2,1,0:T(8,128)(2,1)S(1)}, u32[]{:S(2)}, u32[]{:S(2)}) async-start(bf16[16,72,128]{2,1,0:T(8,128)(2,1)} %fusion.1), calls=%async_computation.1 | async-start | bytes 589824 | tf_op jit(solution)/shard_map/all_to_all | solution.py:273
  87.8 10.3 %collective-permute-start.7 = (bf16[136,576]{1,0:T(8,128)(2,1)S(1)}, bf16[136,576]{1,0:T(8,128)(2,1)S(1)}, u32[]{:S(2)}, u32[]{:S(2)}) collective-permute-start(bf16[136,576]{1,0:T(8,128)(2,1)S(1)} %copy-done.8), channel_id=1, source_target_pairs={{64,0},{65,1},{128,64},{129,65},{192,128},{193,129},{256,192},{257... | collective-permute-start | bytes 470024 | tf_op jit(solution)/shard_map/ppermute | solution.py:263
  90.3 13.1 %collective-permute-start.8 = (bf16[136,576]{1,0:T(8,128)(2,1)S(1)}, bf16[136,576]{1,0:T(8,128)(2,1)S(1)}, u32[]{:S(2)}, u32[]{:S(2)}) collective-permute-start(bf16[136,576]{1,0:T(8,128)(2,1)S(1)} %copy-done.8), channel_id=1, source_target_pairs={{65,0},{64,1},{129,64},{128,65},{193,128},{192,129},{257,192},{256... | collective-permute-start | bytes 470024 | tf_op jit(solution)/shard_map/ppermute | solution.py:263
  98.1 0.7 copy-start.1
  103.4 0.7 copy-start.3
  136.4 10.2 %collective-permute-start.9 = (bf16[16,72,128]{2,1,0:T(8,128)(2,1)S(1)}, bf16[16,72,128]{2,1,0:T(8,128)(2,1)S(1)}, u32[]{:S(2)}, u32[]{:S(2)}) collective-permute-start(bf16[16,72,128]{2,1,0:T(8,128)(2,1)S(1)} %all_to_all.15.q0), channel_id=1, source_target_pairs={{0,2},{2,0},{1,3},{3,1},{4,6},{6,4},{5,7},{7,5},{8,10},{10,8},{9,1... | collective-permute-start | bytes 884744 | tf_op jit(solution)/shard_map/ppermute | solution.py:33
  139.7 12.1 %collective-permute-start.11 = (bf16[16,72,128]{2,1,0:T(8,128)(2,1)S(1)}, bf16[16,72,128]{2,1,0:T(8,128)(2,1)S(1)}, u32[]{:S(2)}, u32[]{:S(2)}) collective-permute-start(bf16[16,72,128]{2,1,0:T(8,128)(2,1)S(1)} %all_to_all.15.q0), channel_id=1, source_target_pairs={{0,1},{1,0},{2,3},{3,2},{4,5},{5,4},{6,7},{7,6},{8,9},{9,8},{10,11... | collective-permute-start | bytes 884744 | tf_op jit(solution)/shard_map/ppermute | solution.py:33
  146.5 6.4 %collective-permute-start.10 = (bf16[16,72,128]{2,1,0:T(8,128)(2,1)S(1)}, bf16[16,72,128]{2,1,0:T(8,128)(2,1)S(1)}, u32[]{:S(2)}, u32[]{:S(2)}) collective-permute-start(bf16[16,72,128]{2,1,0:T(8,128)(2,1)S(1)} %collective-permute-done.9.q1), channel_id=1, source_target_pairs={{0,1},{1,0},{2,3},{3,2},{4,5},{5,4},{6,7},{7,6},{8,9},{9,8},{10,11... | collective-permute-start | bytes 884744 | tf_op jit(solution)/shard_map/ppermute | solution.py:33
  152.9 0.9 copy-start.2
  153.8 0.9 copy-start.4
  159.6 5.4 %collective-permute-start.12 = (bf16[136,4096]{1,0:T(8,128)(2,1)}, bf16[136,4096]{1,0:T(8,128)(2,1)S(1)}, u32[]{:S(2)}, u32[]{:S(2)}) collective-permute-start(bf16[136,4096]{1,0:T(8,128)(2,1)} %get-tuple-element.35), channel_id=1, source_target_pairs={{0,1},{1,0},{2,3},{3,2},{4,5},{5,4},{6,7},{7,6},{8,9},{9,8},{10,11... | collective-permute-start | bytes 3342344 | tf_op jit(solution)/shard_map/ppermute | solution.py:33
Sparse Core Ops, SparseCore 0:
  45.4 101.2 all-gather.2

commit v6 on v5

--- a/solution.py
+++ b/solution.py
@@ -123,8 +123,10 @@
     diagonal = lax.broadcasted_iota(jnp.int32, square, 0) == lax.broadcasted_iota(jnp.int32, square, 1)
     share = jnp.sum(jnp.where(diagonal, weight, 0.0), axis=1, keepdims=True) / total
     scaled = (value_grad[...].astype(f32) * share).astype(bf16)
-    rows_out[:, :features] = scaled
-    rows_out[:, features:] = (adapter_scale * nt(scaled, up)).astype(bf16)
+    rows_out[:tokens, :features] = scaled
+    rows_out[:tokens, features:] = (adapter_scale * nt(scaled, up)).astype(bf16)
+    if rows_out.shape[0] > tokens:
+        rows_out[tokens:, :] = jnp.zeros((rows_out.shape[0] - tokens, rows_out.shape[1]), bf16)
     mid_t = (adapter_scale * nt(up, scaled)).astype(bf16)
     low_t = nt(down[...], acts[...]).astype(bf16)
 
@@ -161,22 +163,27 @@
     out[...] = (adapter_scale * nn(low, up)).astype(bf16)
 
 
-def columns_kernel(rows_mine, rows_other, weights, mine, other, held, sems):
-    chunks = sems.shape[0]
+def columns_kernel(rows_mine, rows_other, weights, mine, other, rows, held, sems):
+    tokens, second = mine.shape[0], rows_mine.shape[0]
+    chunks = sems.shape[0] - 2
     size = held.shape[0] // chunks
-    parts = [pl.ds(k * size, size) for k in range(chunks)]
     copies = [
-        pltpu.make_async_copy(weights.at[part], held.at[part], sems.at[k])
-        for k, part in enumerate(parts)
+        pltpu.make_async_copy(rows_mine, rows.at[pl.ds(0, second)], sems.at[chunks]),
+        pltpu.make_async_copy(rows_other, rows.at[pl.ds(second, second)], sems.at[chunks + 1]),
     ]
+    for k in range(chunks):
+        part = pl.ds(k * size, size)
+        copies.append(pltpu.make_async_copy(weights.at[part], held.at[part], sems.at[k]))
     for copy in copies:
         copy.start()
+    copies[0].wait()
+    copies[1].wait()
     for k in range(chunks):
-        copies[k].wait()
+        copies[k + 2].wait()
         for i in range(k * size, (k + 1) * size, 2):
-            pair = jnp.concatenate([held[i], held[i + 1]], axis=1)
-            mine[:, i * LANES : (i + 2) * LANES] = nn(rows_mine[...], pair).astype(bf16)
-            other[:, i * LANES : (i + 2) * LANES] = nn(rows_other[...], pair).astype(bf16)
+            product = nn(rows[...], jnp.concatenate([held[i], held[i + 1]], axis=1))
+            mine[:, i * LANES : (i + 2) * LANES] = product[:tokens].astype(bf16)
+            other[:, i * LANES : (i + 2) * LANES] = product[second : second + tokens].astype(bf16)
 
 
 def merge_kernel(place, mine, other, out):
@@ -213,6 +220,7 @@
     rank = down_master.shape[2]
     up_rows = features // LANES
     rows = rank + EXTRA
+    padded = -(-tokens // 16) * 16
     z, sections = lax.axis_size("z"), lax.axis_size("section")
     place = jnp.stack([lax.axis_index("core"), lax.axis_index("yl")]).astype(jnp.int32)
     params = pltpu.CompilerParams(vmem_limit_bytes=VMEM_BYTES)
@@ -240,7 +248,8 @@
     got = spread(copies)
     even = lax.axis_index("yl") == 0
     weights = jnp.stack([jnp.where(even, same, flipped), jnp.where(even, flipped, same)])
-    got_yl, weights = after(swap(got, "yl"), weights)
+    got, weights = after(got, weights)
+    got_yl = swap(got, "yl")
     weights_all = lax.all_gather(weights, "z").reshape(2 * z, features + rank, LANES)
 
     keep, send, next_rows = pl.pallas_call(
@@ -248,7 +257,7 @@
         out_shape=(
             jax.ShapeDtypeStruct((2, z, rows, LANES), f32),
             jax.ShapeDtypeStruct((2, z, rows, LANES), bf16),
-            jax.ShapeDtypeStruct((tokens, features + rank), bf16),
+            jax.ShapeDtypeStruct((padded, features + rank), bf16),
         ),
         in_specs=[SCALARS] + whole(7),
         out_specs=tuple(whole(3)),
@@ -283,19 +292,18 @@
     )
     block = pad_rows([down_new.astype(bf16), up_new.astype(bf16).reshape(up_rows, LANES)], rows)
     got = spread(jnp.broadcast_to(block[None], (z, rows, LANES)))
-    got_yl = swap(got, "yl")
-    got_core, got_last = swap(got, "core"), swap(got_yl, "core")
-    weights_all, _, _ = after(weights_all, got_last, got_core)
-    chunks = 4
+    weights_all, _ = after(weights_all, got)
+    chunks = min(4, z)
     half = jax.ShapeDtypeStruct((tokens, width // 2), bf16)
     mine, other = pl.pallas_call(
         columns_kernel,
         out_shape=(half, half),
-        in_specs=whole(2) + [pl.BlockSpec(memory_space=pl.ANY)],
+        in_specs=[pl.BlockSpec(memory_space=pl.ANY)] * 3,
         out_specs=tuple(whole(2)),
         scratch_shapes=[
+            pltpu.VMEM((2 * padded, features + rank), bf16),
             pltpu.VMEM((2 * z, features + rank, LANES), bf16),
-            pltpu.SemaphoreType.DMA((min(chunks, z),)),
+            pltpu.SemaphoreType.DMA((chunks + 2,)),
         ],
         compiler_params=pltpu.CompilerParams(vmem_limit_bytes=52 * 1024 * 1024),
         cost_estimate=pl.CostEstimate(
@@ -305,7 +313,8 @@
         ),
         name="columns",
     )(rows_mine, rows_other, weights_all)
-    other = swap(other, "core")
+    got_yl, mine, other = after(swap(got, "yl"), mine, other)
+    got_last, got_core, other = swap(got_yl, "core"), swap(got, "core"), swap(other, "core")
     refreshed = pl.pallas_call(
         refresh_kernel,
         out_shape=jax.ShapeDtypeStruct((tokens, features), bf16),

time: 176 us -> 169 us (0.960)
  local copies, waits for them, and re-layouts: 4.31 us -> 1.12 us
  waiting for transfers between devices: 35.8 us -> 32.9 us
    all_to_all x1, waiting for transfers between devices: 8.05 us -> 0.01 us  [spread(): return lax.all_to_all(copies, 'z', 0, 0)]
    ppermute x9, waiting for transfers between devices: 15.2 us -> 10.3 us  [swap(): return lax.ppermute(array, axis, [(0, 1), (1, 0)])]
    ppermute x1, waiting for transfers between devices: 0.01 us -> 4.46 us  [per_device(): same = lax.ppermute(weights, ('section', 'yl'), from_next(0))]
    ppermute x1, waiting for transfers between devices: 0.01 us -> 4.04 us  [per_device(): flipped = lax.ppermute(weights, ('section', 'yl'), from_next(1))]
    unnamed x30 -> x22, local copies, waits for them, and re-layouts: 4.15 us -> 0.96 us
    ppermute x9, starting transfers between devices: 37.6 us -> 35.7 us  [swap(): return lax.ppermute(array, axis, [(0, 1), (1, 0)])]
  transfers between devices with their start and end apart: 16 -> 16, of which waited for: 9 -> 10; matrix products, arithmetic and copies ran while one was open for 2% -> 2% of each run, Pallas kernels for 4% -> 7%
where the time goes in v6:
time: 169 us; the launch traced here: 167 us
  starting transfers between devices  70.5 us (42%)
  waiting for transfers between devices  32.9 us (19%)
  blocking collectives  28.1 us (17%)
  Pallas kernels  16.1 us (10%)
  between operations  15.1 us (9%)
  other arithmetic  3.17 us (2%)
    ppermute x9, starting transfers between devices, swap(): return lax.ppermute(array, axis, [(0, 1), (1, 0)])  35.7 us
    all_to_all x1, blocking collectives, spread(): return lax.all_to_all(copies, 'z', 0, 0)  28.1 us
    all_to_all x1, starting transfers between devices, spread(): return lax.all_to_all(copies, 'z', 0, 0)  14.9 us
    ppermute x2, waiting for transfers between devices, per_device(): lax.ppermute(next_rows, ('section', 'core'), [(s * 2 + (c ^ flip), (s - 1...  10.7 us
    ppermute x9, waiting for transfers between devices, swap(): return lax.ppermute(array, axis, [(0, 1), (1, 0)])  10.3 us
    all_to_all x1, starting transfers between devices, per_device(): parts = lax.all_to_all(kept.astype(bf16), 'z', 0, 0)  9.08 us
    pallas_call x1, Pallas kernels, per_device(): pl.pallas_call(columns_kernel, out_shape=(half, half), in_specs=[pl.Block...  5.29 us
    ppermute x2, starting transfers between devices, per_device(): lax.ppermute(next_rows, ('section', 'core'), [(s * 2 + (c ^ flip), (s - 1...  5.1 us
  transfers between devices with their start and end apart: 16, of which 10 were waited for; matrix products, arithmetic and copies ran while one was open for 2% of the time, Pallas kernels for 7%

profile of v6, /device:TPU:7, one launch (start us, length us, event | category | flops | bytes accessed | tf_op | source)
XLA Modules:
  0.0 167.0 jit_solution(2611943950975133163)
XLA Ops:
  7.2 0.0 copy-start.2
  7.2 0.0 copy-start
  7.2 1.9 %prepare.1 = (bf16[16,72,128]{2,1,0:T(8,128)(2,1)}, bf16[576,128]{1,0:T(8,128)(2,1)}) custom-call(f32[64,128]{1,0:T(8,128)} %bitcast.66, f32[1,512]{1,0:T(1,128)} %bitcast.68, s32[1,136]{1,0:T(1,128)} %loss_weight.3, bf16[128,512]{1,0:T(8,128)(2,1)} %bitcast.65), custom_call_target="tpu_custom_call" | custom-call | tf_op jit(solution)/shard_map/prepare/pallas_call | solution.py:228
  9.1 14.9 %all-to-all-start = ((bf16[16,72,128]{2,1,0:T(8,128)(2,1)}), bf16[16,72,128]{2,1,0:T(8,128)(2,1)S(1)}, u32[]{:S(2)}, u32[]{:S(2)}) async-start(bf16[16,72,128]{2,1,0:T(8,128)(2,1)} %get-tuple-element.26), calls=%async_computation | async-start | bytes 589824 | tf_op jit(solution)/shard_map/all_to_all | solution.py:41
  24.1 0.0 all-gather.3.cloned.1.call-start
  24.1 2.5 %collective-permute-start = (bf16[576,128]{1,0:T(8,128)(2,1)}, bf16[576,128]{1,0:T(8,128)(2,1)S(1)}, u32[]{:S(2)}, u32[]{:S(2)}) collective-permute-start(bf16[576,128]{1,0:T(8,128)(2,1)} %get-tuple-element.27), channel_id=1, source_target_pairs={{64,0},{66,2},{128,64},{130,66},{192,128},{194,130},{256,192},{258... | collective-permute-start | bytes 442376 | tf_op jit(solution)/shard_map/ppermute | solution.py:245
  26.6 3.2 %collective-permute-start.1 = (bf16[576,128]{1,0:T(8,128)(2,1)}, bf16[576,128]{1,0:T(8,128)(2,1)S(1)}, u32[]{:S(2)}, u32[]{:S(2)}) collective-permute-start(bf16[576,128]{1,0:T(8,128)(2,1)} %get-tuple-element.27), channel_id=1, source_target_pairs={{66,0},{64,2},{130,64},{128,66},{194,128},{192,130},{258,192},{256... | collective-permute-start | bytes 442376 | tf_op jit(solution)/shard_map/ppermute | solution.py:246
  29.8 4.5 %collective-permute-done = bf16[576,128]{1,0:T(8,128)(2,1)S(1)} collective-permute-done((bf16[576,128]{1,0:T(8,128)(2,1)}, bf16[576,128]{1,0:T(8,128)(2,1)S(1)}, u32[]{:S(2)}, u32[]{:S(2)}) %collective-permute-start) | collective-permute-done | bytes 147488 | tf_op jit(solution)/shard_map/ppermute | solution.py:245
  34.2 4.0 %collective-permute-done.1 = bf16[576,128]{1,0:T(8,128)(2,1)S(1)} collective-permute-done((bf16[576,128]{1,0:T(8,128)(2,1)}, bf16[576,128]{1,0:T(8,128)(2,1)S(1)}, u32[]{:S(2)}, u32[]{:S(2)}) %collective-permute-start.1) | collective-permute-done | bytes 147488 | tf_op jit(solution)/shard_map/ppermute | solution.py:246
  38.3 0.7 pad_maximum_fusion
  39.0 0.0 all-to-all-done.q0
  39.0 0.0 all-gather.3.cloned.1.call-update
  39.1 2.0 %collective-permute-start.2 = (bf16[16,72,128]{2,1,0:T(8,128)(2,1)S(1)}, bf16[16,72,128]{2,1,0:T(8,128)(2,1)S(1)}, u32[]{:S(2)}, u32[]{:S(2)}) collective-permute-start(bf16[16,72,128]{2,1,0:T(8,128)(2,1)S(1)} %all-to-all-done.q0), channel_id=1, source_target_pairs={{0,2},{2,0},{1,3},{3,1},{4,6},{6,4},{5,7},{7,5},{8,10},{10,8},{9,1... | collective-permute-start | bytes 884744 | tf_op jit(solution)/shard_map/ppermute | solution.py:33
  41.0 8.7 %collective-permute-start.3 = (bf16[16,72,128]{2,1,0:T(8,128)(2,1)S(1)}, bf16[16,72,128]{2,1,0:T(8,128)(2,1)S(1)}, u32[]{:S(2)}, u32[]{:S(2)}) collective-permute-start(bf16[16,72,128]{2,1,0:T(8,128)(2,1)S(1)} %all-to-all-done.q0), channel_id=1, source_target_pairs={{0,1},{1,0},{2,3},{3,2},{4,5},{5,4},{6,7},{7,6},{8,9},{9,8},{10,11... | collective-permute-start | bytes 884744 | tf_op jit(solution)/shard_map/ppermute | solution.py:33
  49.7 0.0 collective-permute-done.2.q1
  49.7 5.1 %collective-permute-start.4 = (bf16[16,72,128]{2,1,0:T(8,128)(2,1)S(1)}, bf16[16,72,128]{2,1,0:T(8,128)(2,1)S(1)}, u32[]{:S(2)}, u32[]{:S(2)}) collective-permute-start(bf16[16,72,128]{2,1,0:T(8,128)(2,1)S(1)} %collective-permute-done.2.q1), channel_id=1, source_target_pairs={{0,1},{1,0},{2,3},{3,2},{4,5},{5,4},{6,7},{7,6},{8,9},{9,8},{10,11... | collective-permute-start | bytes 884744 | tf_op jit(solution)/shard_map/ppermute | solution.py:33
  54.8 0.1 pad_add_fusion.place
  54.9 0.0 collective-permute-done.3.q2
  54.9 1.1 collective-permute-done.4.q3
  56.0 0.0 copy-done.2
  56.0 0.0 copy-done
  56.0 0.9 copy-done.1
  56.9 4.2 %backward.1 = (f32[2,16,72,128]{3,2,1,0:T(8,128)S(1)}, bf16[2,16,72,128]{3,2,1,0:T(8,128)(2,1)S(1)}, bf16[144,576]{1,0:T(8,128)(2,1)S(1)}) custom-call(s32[2]{0:T(128)S(1)} %pad_add_fusion.place, bf16[16,72,128]{2,1,0:T(8,128)(2,1)S(1)} %all-to-all-done.q0, bf16[16,72,128]{2,1,0:T(8,128)(2,1)S(1)} %collective-permute-done.2.q1, ...), custom_call_target="tpu_custom_call" | custom-call | tf_op jit(solution)/shard_map/backward/pallas_call | solution.py:255
  61.2 0.0 copy-start.3
  61.2 2.3 %collective-permute-start.5 = (bf16[2,16,72,128]{3,2,1,0:T(8,128)(2,1)S(1)}, bf16[2,16,72,128]{3,2,1,0:T(8,128)(2,1)S(1)}, u32[]{:S(2)}, u32[]{:S(2)}) collective-permute-start(bf16[2,16,72,128]{3,2,1,0:T(8,128)(2,1)S(1)} %get-tuple-element.30), channel_id=1, source_target_pairs={{0,1},{1,0},{2,3},{3,2},{4,5},{5,4},{6,7},{7,6},{8,9},{9,8},{10,11... | collective-permute-start | bytes 1769480 | tf_op jit(solution)/shard_map/ppermute | solution.py:33
  63.5 1.6 collective-permute-done.5
  65.1 0.1 convert_add_fusion
  65.2 0.0 copy-done.3
  65.2 0.0 copy-start.10
  65.2 0.0 copy-start.9
  65.3 0.0 copy-start.4
  65.3 0.0 copy-start.8
  65.3 0.0 copy-start.5
  65.3 0.0 copy-start.6
  65.3 0.0 copy-start.7
  65.3 3.3 %collective-permute-start.6 = (bf16[16,72,128]{2,1,0:T(8,128)(2,1)S(1)}, bf16[16,72,128]{2,1,0:T(8,128)(2,1)S(1)}, u32[]{:S(2)}, u32[]{:S(2)}) collective-permute-start(bf16[16,72,128]{2,1,0:T(8,128)(2,1)S(1)} %fusion.2), channel_id=1, source_target_pairs={{0,2},{2,0},{1,3},{3,1},{4,6},{6,4},{5,7},{7,5},{8,10},{10,8},{9,1... | collective-permute-start | bytes 884744 | tf_op jit(solution)/shard_map/ppermute | solution.py:33
  68.7 6.9 %collective-permute-done.6 = bf16[16,72,128]{2,1,0:T(8,128)(2,1)S(1)} collective-permute-done((bf16[16,72,128]{2,1,0:T(8,128)(2,1)S(1)}, bf16[16,72,128]{2,1,0:T(8,128)(2,1)S(1)}, u32[]{:S(2)}, u32[]{:S(2)}) %collective-permute-start.6) | collective-permute-done | bytes 294944 | tf_op jit(solution)/shard_map/ppermute | solution.py:33
  75.6 0.8 fusion.1
  76.4 9.1 %all-to-all-start.1 = ((bf16[16,72,128]{2,1,0:T(8,128)(2,1)}), bf16[16,72,128]{2,1,0:T(8,128)(2,1)S(1)}, u32[]{:S(2)}, u32[]{:S(2)}) async-start(bf16[16,72,128]{2,1,0:T(8,128)(2,1)} %fusion.1), calls=%async_computation.1 | async-start | bytes 589824 | tf_op jit(solution)/shard_map/all_to_all | solution.py:282
  86.2 0.1 pad.2.clone
  86.3 0.0 copy-done.10
  86.3 0.0 copy-done.4
  86.3 1.9 %collective-permute-start.7 = (bf16[144,576]{1,0:T(8,128)(2,1)S(1)}, bf16[144,576]{1,0:T(8,128)(2,1)S(1)}, u32[]{:S(2)}, u32[]{:S(2)}) collective-permute-start(bf16[144,576]{1,0:T(8,128)(2,1)S(1)} %copy-done.4), channel_id=1, source_target_pairs={{64,0},{65,1},{128,64},{129,65},{192,128},{193,129},{256,192},{257... | collective-permute-start | bytes 497672 | tf_op jit(solution)/shard_map/ppermute | solution.py:272
  88.2 3.2 %collective-permute-start.8 = (bf16[144,576]{1,0:T(8,128)(2,1)S(1)}, bf16[144,576]{1,0:T(8,128)(2,1)S(1)}, u32[]{:S(2)}, u32[]{:S(2)}) collective-permute-start(bf16[144,576]{1,0:T(8,128)(2,1)S(1)} %copy-done.4), channel_id=1, source_target_pairs={{65,0},{64,1},{129,64},{128,65},{193,128},{192,129},{257,192},{256... | collective-permute-start | bytes 497672 | tf_op jit(solution)/shard_map/ppermute | solution.py:272
  91.4 0.0 copy-done.9
  91.4 5.1 %collective-permute-done.7.rows_mine = bf16[144,576]{1,0:T(8,128)(2,1)S(1)} collective-permute-done((bf16[144,576]{1,0:T(8,128)(2,1)S(1)}, bf16[144,576]{1,0:T(8,128)(2,1)S(1)}, u32[]{:S(2)}, u32[]{:S(2)}) %collective-permute-start.7) | collective-permute-done | bytes 165920 | tf_op jit(solution)/shard_map/ppermute | solution.py:272
  96.6 5.6 %collective-permute-done.8.rows_other = bf16[144,576]{1,0:T(8,128)(2,1)S(1)} collective-permute-done((bf16[144,576]{1,0:T(8,128)(2,1)S(1)}, bf16[144,576]{1,0:T(8,128)(2,1)S(1)}, u32[]{:S(2)}, u32[]{:S(2)}) %collective-permute-start.8) | collective-permute-done | bytes 165920 | tf_op jit(solution)/shard_map/ppermute | solution.py:272
  102.1 3.4 %all-to-all-done.1 = bf16[16,72,128]{2,1,0:T(8,128)(2,1)S(1)} async-done(((bf16[16,72,128]{2,1,0:T(8,128)(2,1)}), bf16[16,72,128]{2,1,0:T(8,128)(2,1)S(1)}, u32[]{:S(2)}, u32[]{:S(2)}) %all-to-all-start.1) | async-done | bytes 294944 | tf_op jit(solution)/shard_map/all_to_all | solution.py:282
  105.6 0.7 fusion.10
  106.3 0.1 maximum_maximum_fusion
  106.4 28.1 %all_to_all.15.q0 = bf16[16,72,128]{2,1,0:T(8,128)(2,1)S(1)} all-to-all(bf16[16,72,128]{2,1,0:T(8,128)(2,1)S(1)} %broadcast_in_dim.28), channel_id=1, replica_groups=mesh['section'=8,'z'=16,'yl'=2,'core'=2] {'z'}, dimensions={0} | all-to-all | bytes 589824 | tf_op jit(solution)/shard_map/all_to_all | solution.py:41
  134.5 2.0 %collective-permute-start.9 = (bf16[16,72,128]{2,1,0:T(8,128)(2,1)S(1)}, bf16[16,72,128]{2,1,0:T(8,128)(2,1)S(1)}, u32[]{:S(2)}, u32[]{:S(2)}) collective-permute-start(bf16[16,72,128]{2,1,0:T(8,128)(2,1)S(1)} %all_to_all.15.q0), channel_id=1, source_target_pairs={{0,2},{2,0},{1,3},{3,1},{4,6},{6,4},{5,7},{7,5},{8,10},{10,8},{9,1... | collective-permute-start | bytes 884744 | tf_op jit(solution)/shard_map/ppermute | solution.py:33
  136.5 0.0 all-gather.3.cloned.1.call-done.weights
  136.5 5.3 %columns.1 = (bf16[136,4096]{1,0:T(8,128)(2,1)S(1)}, bf16[136,4096]{1,0:T(8,128)(2,1)}) custom-call(bf16[144,576]{1,0:T(8,128)(2,1)S(1)} %collective-permute-done.7.rows_mine, bf16[144,576]{1,0:T(8,128)(2,1)S(1)} %collective-permute-done.8.rows_other, bf16[32,576,128]{2,1,0:T(8,128)(2,1)} %all-gather.3.cloned.1.call-done.weights), custom_call_target="tpu_custom_call" | custom-call | flops 1283457024 | bytes 4718592 | tf_op jit(solution)/shard_map/columns/pallas_call | solution.py:298
  141.8 0.1 collective-permute-done.9.q1
  141.9 8.0 %collective-permute-start.10 = (bf16[136,4096]{1,0:T(8,128)(2,1)}, bf16[136,4096]{1,0:T(8,128)(2,1)S(1)}, u32[]{:S(2)}, u32[]{:S(2)}) collective-permute-start(bf16[136,4096]{1,0:T(8,128)(2,1)} %get-tuple-element.40), channel_id=1, source_target_pairs={{0,1},{1,0},{2,3},{3,2},{4,5},{5,4},{6,7},{7,6},{8,9},{9,8},{10,11... | collective-permute-start | bytes 3342344 | tf_op jit(solution)/shard_map/ppermute | solution.py:33
  149.9 1.9 %collective-permute-start.11 = (bf16[16,72,128]{2,1,0:T(8,128)(2,1)S(1)}, bf16[16,72,128]{2,1,0:T(8,128)(2,1)S(1)}, u32[]{:S(2)}, u32[]{:S(2)}) collective-permute-start(bf16[16,72,128]{2,1,0:T(8,128)(2,1)S(1)} %all_to_all.15.q0), channel_id=1, source_target_pairs={{0,1},{1,0},{2,3},{3,2},{4,5},{5,4},{6,7},{7,6},{8,9},{9,8},{10,11... | collective-permute-start | bytes 884744 | tf_op jit(solution)/shard_map/ppermute | solution.py:33
  151.9 2.4 %collective-permute-start.12 = (bf16[16,72,128]{2,1,0:T(8,128)(2,1)S(1)}, bf16[16,72,128]{2,1,0:T(8,128)(2,1)S(1)}, u32[]{:S(2)}, u32[]{:S(2)}) collective-permute-start(bf16[16,72,128]{2,1,0:T(8,128)(2,1)S(1)} %collective-permute-done.9.q1), channel_id=1, source_target_pairs={{0,1},{1,0},{2,3},{3,2},{4,5},{5,4},{6,7},{7,6},{8,9},{9,8},{10,11... | collective-permute-start | bytes 884744 | tf_op jit(solution)/shard_map/ppermute | solution.py:33
  154.3 0.6 divide_subtract_fusion.1
  154.9 0.0 collective-permute-done.11.q2
  154.9 0.6 collective-permute-done.12.q3
  155.5 2.5 %refresh.1 = bf16[136,512]{1,0:T(8,128)(2,1)} custom-call(s32[2]{0:T(128)S(1)} %pad_add_fusion.place, bf16[16,72,128]{2,1,0:T(8,128)(2,1)S(1)} %all_to_all.15.q0, bf16[16,72,128]{2,1,0:T(8,128)(2,1)S(1)} %collective-permute-done.9.q1, bf16[16,72,128]{2,1,0:T(8,128)(2,1)S(1)} %collective-permute-done.11.q2, ...), custom_call_target="tpu_custom_call" | custom-call | tf_op jit(solution)/shard_map/refresh/pallas_call | solution.py:318
  158.0 0.0 collective-permute-done.10.other
  158.0 2.2 %merge.1 = bf16[136,8192]{1,0:T(8,128)(2,1)} custom-call(s32[2]{0:T(128)S(1)} %pad_add_fusion.place, bf16[136,4096]{1,0:T(8,128)(2,1)S(1)} %get-tuple-element.39.mine, bf16[136,4096]{1,0:T(8,128)(2,1)S(1)} %collective-permute-done.10.other), custom_call_target="tpu_custom_call" | custom-call | tf_op jit(solution)/shard_map/merge/pallas_call | solution.py:334
  (13 shorter events, 0.2 us)
Async XLA Ops:
  7.2 48.9 %copy-start.2 = (s32[1,136]{1,0:T(1,128)S(1)}, s32[1,136]{1,0:T(1,128)}, u32[]{:S(2)}) copy-start(s32[1,136]{1,0:T(1,128)} %loss_weight.3) | copy-start | bytes 1636
  7.2 48.9 %copy-start = (bf16[1,136,8192]{2,1,0:T(8,128)(2,1)S(1)}, bf16[1,136,8192]{2,1,0:T(8,128)(2,1)}, u32[]{:S(2)}) copy-start(bf16[1,136,8192]{2,1,0:T(8,128)(2,1)} %param.11) | copy-start | bytes 6684676
  9.1 29.9 %all-to-all-start = ((bf16[16,72,128]{2,1,0:T(8,128)(2,1)}), bf16[16,72,128]{2,1,0:T(8,128)(2,1)S(1)}, u32[]{:S(2)}, u32[]{:S(2)}) async-start(bf16[16,72,128]{2,1,0:T(8,128)(2,1)} %get-tuple-element.26), calls=%async_computation | async-start | bytes 589824 | tf_op jit(solution)/shard_map/all_to_all | solution.py:41
  24.1 112.5 %all-gather.3.cloned.1.call-start = ((), (), s32[]{:S(2)}) async-start(), calls=%async_computation.3 | async-start | bytes 5013504 | tf_op jit(solution)/shard_map/all_gather | solution.py:253
  24.1 10.1 %collective-permute-start = (bf16[576,128]{1,0:T(8,128)(2,1)}, bf16[576,128]{1,0:T(8,128)(2,1)S(1)}, u32[]{:S(2)}, u32[]{:S(2)}) collective-permute-start(bf16[576,128]{1,0:T(8,128)(2,1)} %get-tuple-element.27), channel_id=1, source_target_pairs={{64,0},{66,2},{128,64},{130,66},{192,128},{194,130},{256,192},{258... | collective-permute-start | bytes 442376 | tf_op jit(solution)/shard_map/ppermute | solution.py:245
  26.6 11.7 %collective-permute-start.1 = (bf16[576,128]{1,0:T(8,128)(2,1)}, bf16[576,128]{1,0:T(8,128)(2,1)S(1)}, u32[]{:S(2)}, u32[]{:S(2)}) collective-permute-start(bf16[576,128]{1,0:T(8,128)(2,1)} %get-tuple-element.27), channel_id=1, source_target_pairs={{66,0},{64,2},{130,64},{128,66},{194,128},{192,130},{258,192},{256... | collective-permute-start | bytes 442376 | tf_op jit(solution)/shard_map/ppermute | solution.py:246
  39.1 10.7 %collective-permute-start.2 = (bf16[16,72,128]{2,1,0:T(8,128)(2,1)S(1)}, bf16[16,72,128]{2,1,0:T(8,128)(2,1)S(1)}, u32[]{:S(2)}, u32[]{:S(2)}) collective-permute-start(bf16[16,72,128]{2,1,0:T(8,128)(2,1)S(1)} %all-to-all-done.q0), channel_id=1, source_target_pairs={{0,2},{2,0},{1,3},{3,1},{4,6},{6,4},{5,7},{7,5},{8,10},{10,8},{9,1... | collective-permute-start | bytes 884744 | tf_op jit(solution)/shard_map/ppermute | solution.py:33
  41.0 13.9 %collective-permute-start.3 = (bf16[16,72,128]{2,1,0:T(8,128)(2,1)S(1)}, bf16[16,72,128]{2,1,0:T(8,128)(2,1)S(1)}, u32[]{:S(2)}, u32[]{:S(2)}) collective-permute-start(bf16[16,72,128]{2,1,0:T(8,128)(2,1)S(1)} %all-to-all-done.q0), channel_id=1, source_target_pairs={{0,1},{1,0},{2,3},{3,2},{4,5},{5,4},{6,7},{7,6},{8,9},{9,8},{10,11... | collective-permute-start | bytes 884744 | tf_op jit(solution)/shard_map/ppermute | solution.py:33
  49.7 6.3 %collective-permute-start.4 = (bf16[16,72,128]{2,1,0:T(8,128)(2,1)S(1)}, bf16[16,72,128]{2,1,0:T(8,128)(2,1)S(1)}, u32[]{:S(2)}, u32[]{:S(2)}) collective-permute-start(bf16[16,72,128]{2,1,0:T(8,128)(2,1)S(1)} %collective-permute-done.2.q1), channel_id=1, source_target_pairs={{0,1},{1,0},{2,3},{3,2},{4,5},{5,4},{6,7},{7,6},{8,9},{9,8},{10,11... | collective-permute-start | bytes 884744 | tf_op jit(solution)/shard_map/ppermute | solution.py:33
  56.0 0.9 copy-start.1
  61.2 4.0 %copy-start.3 = (bf16[144,576]{1,0:T(8,128)(2,1)}, bf16[144,576]{1,0:T(8,128)(2,1)S(1)}, u32[]{:S(2)}) copy-start(bf16[144,576]{1,0:T(8,128)(2,1)S(1)} %get-tuple-element.31) | copy-start | bytes 497668
  61.2 3.9 %collective-permute-start.5 = (bf16[2,16,72,128]{3,2,1,0:T(8,128)(2,1)S(1)}, bf16[2,16,72,128]{3,2,1,0:T(8,128)(2,1)S(1)}, u32[]{:S(2)}, u32[]{:S(2)}) collective-permute-start(bf16[2,16,72,128]{3,2,1,0:T(8,128)(2,1)S(1)} %get-tuple-element.30), channel_id=1, source_target_pairs={{0,1},{1,0},{2,3},{3,2},{4,5},{5,4},{6,7},{7,6},{8,9},{9,8},{10,11... | collective-permute-start | bytes 1769480 | tf_op jit(solution)/shard_map/ppermute | solution.py:33
  65.2 21.1 %copy-start.10 = (f32[1,1,512]{2,1,0:T(1,128)S(1)}, f32[1,1,512]{2,1,0:T(1,128)}, u32[]{:S(2)}) copy-start(f32[1,1,512]{2,1,0:T(1,128)} %param.19) | copy-start | bytes 6148
  65.2 26.2 %copy-start.9 = (f32[1,1,512]{2,1,0:T(1,128)S(1)}, f32[1,1,512]{2,1,0:T(1,128)}, u32[]{:S(2)}) copy-start(f32[1,1,512]{2,1,0:T(1,128)} %param.20) | copy-start | bytes 6148
  65.3 21.0 %copy-start.4 = (bf16[144,576]{1,0:T(8,128)(2,1)S(1)}, bf16[144,576]{1,0:T(8,128)(2,1)}, u32[]{:S(2)}) copy-start(bf16[144,576]{1,0:T(8,128)(2,1)} %copy-done.3) | copy-start | bytes 497668
  65.3 40.3 %copy-start.8 = (f32[1,1,512]{2,1,0:T(1,128)S(1)}, f32[1,1,512]{2,1,0:T(1,128)}, u32[]{:S(2)}) copy-start(f32[1,1,512]{2,1,0:T(1,128)} %param.18) | copy-start | bytes 6148
  65.3 40.3 %copy-start.5 = (f32[1,128,64]{1,2,0:T(8,128)S(1)}, f32[1,128,64]{1,2,0:T(8,128)}, u32[]{:S(2)}) copy-start(f32[1,128,64]{1,2,0:T(8,128)} %param.15) | copy-start | bytes 98308
  65.3 40.3 %copy-start.6 = (f32[1,128,64]{1,2,0:T(8,128)S(1)}, f32[1,128,64]{1,2,0:T(8,128)}, u32[]{:S(2)}) copy-start(f32[1,128,64]{1,2,0:T(8,128)} %param.17) | copy-start | bytes 98308
  65.3 40.3 %copy-start.7 = (f32[1,128,64]{1,2,0:T(8,128)S(1)}, f32[1,128,64]{1,2,0:T(8,128)}, u32[]{:S(2)}) copy-start(f32[1,128,64]{1,2,0:T(8,128)} %param.16) | copy-start | bytes 98308
  65.3 10.2 %collective-permute-start.6 = (bf16[16,72,128]{2,1,0:T(8,128)(2,1)S(1)}, bf16[16,72,128]{2,1,0:T(8,128)(2,1)S(1)}, u32[]{:S(2)}, u32[]{:S(2)}) collective-permute-start(bf16[16,72,128]{2,1,0:T(8,128)(2,1)S(1)} %fusion.2), channel_id=1, source_target_pairs={{0,2},{2,0},{1,3},{3,1},{4,6},{6,4},{5,7},{7,5},{8,10},{10,8},{9,1... | collective-permute-start | bytes 884744 | tf_op jit(solution)/shard_map/ppermute | solution.py:33
  76.4 29.1 %all-to-all-start.1 = ((bf16[16,72,128]{2,1,0:T(8,128)(2,1)}), bf16[16,72,128]{2,1,0:T(8,128)(2,1)S(1)}, u32[]{:S(2)}, u32[]{:S(2)}) async-start(bf16[16,72,128]{2,1,0:T(8,128)(2,1)} %fusion.1), calls=%async_computation.1 | async-start | bytes 589824 | tf_op jit(solution)/shard_map/all_to_all | solution.py:282
  86.3 10.3 %collective-permute-start.7 = (bf16[144,576]{1,0:T(8,128)(2,1)S(1)}, bf16[144,576]{1,0:T(8,128)(2,1)S(1)}, u32[]{:S(2)}, u32[]{:S(2)}) collective-permute-start(bf16[144,576]{1,0:T(8,128)(2,1)S(1)} %copy-done.4), channel_id=1, source_target_pairs={{64,0},{65,1},{128,64},{129,65},{192,128},{193,129},{256,192},{257... | collective-permute-start | bytes 497672 | tf_op jit(solution)/shard_map/ppermute | solution.py:272
  88.2 13.9 %collective-permute-start.8 = (bf16[144,576]{1,0:T(8,128)(2,1)S(1)}, bf16[144,576]{1,0:T(8,128)(2,1)S(1)}, u32[]{:S(2)}, u32[]{:S(2)}) collective-permute-start(bf16[144,576]{1,0:T(8,128)(2,1)S(1)} %copy-done.4), channel_id=1, source_target_pairs={{65,0},{64,1},{129,64},{128,65},{193,128},{192,129},{257,192},{256... | collective-permute-start | bytes 497672 | tf_op jit(solution)/shard_map/ppermute | solution.py:272
  134.5 7.5 %collective-permute-start.9 = (bf16[16,72,128]{2,1,0:T(8,128)(2,1)S(1)}, bf16[16,72,128]{2,1,0:T(8,128)(2,1)S(1)}, u32[]{:S(2)}, u32[]{:S(2)}) collective-permute-start(bf16[16,72,128]{2,1,0:T(8,128)(2,1)S(1)} %all_to_all.15.q0), channel_id=1, source_target_pairs={{0,2},{2,0},{1,3},{3,1},{4,6},{6,4},{5,7},{7,5},{8,10},{10,8},{9,1... | collective-permute-start | bytes 884744 | tf_op jit(solution)/shard_map/ppermute | solution.py:33
  141.9 16.0 %collective-permute-start.10 = (bf16[136,4096]{1,0:T(8,128)(2,1)}, bf16[136,4096]{1,0:T(8,128)(2,1)S(1)}, u32[]{:S(2)}, u32[]{:S(2)}) collective-permute-start(bf16[136,4096]{1,0:T(8,128)(2,1)} %get-tuple-element.40), channel_id=1, source_target_pairs={{0,1},{1,0},{2,3},{3,2},{4,5},{5,4},{6,7},{7,6},{8,9},{9,8},{10,11... | collective-permute-start | bytes 3342344 | tf_op jit(solution)/shard_map/ppermute | solution.py:33
  149.9 5.0 %collective-permute-start.11 = (bf16[16,72,128]{2,1,0:T(8,128)(2,1)S(1)}, bf16[16,72,128]{2,1,0:T(8,128)(2,1)S(1)}, u32[]{:S(2)}, u32[]{:S(2)}) collective-permute-start(bf16[16,72,128]{2,1,0:T(8,128)(2,1)S(1)} %all_to_all.15.q0), channel_id=1, source_target_pairs={{0,1},{1,0},{2,3},{3,2},{4,5},{5,4},{6,7},{7,6},{8,9},{9,8},{10,11... | collective-permute-start | bytes 884744 | tf_op jit(solution)/shard_map/ppermute | solution.py:33
  151.9 3.6 %collective-permute-start.12 = (bf16[16,72,128]{2,1,0:T(8,128)(2,1)S(1)}, bf16[16,72,128]{2,1,0:T(8,128)(2,1)S(1)}, u32[]{:S(2)}, u32[]{:S(2)}) collective-permute-start(bf16[16,72,128]{2,1,0:T(8,128)(2,1)S(1)} %collective-permute-done.9.q1), channel_id=1, source_target_pairs={{0,1},{1,0},{2,3},{3,2},{4,5},{5,4},{6,7},{7,6},{8,9},{9,8},{10,11... | collective-permute-start | bytes 884744 | tf_op jit(solution)/shard_map/ppermute | solution.py:33
Sparse Core Ops, SparseCore 0:
  39.2 96.5 all-gather.2

commit v7 on v6

--- a/solution.py
+++ b/solution.py
@@ -174,12 +174,14 @@
     for k in range(chunks):
         part = pl.ds(k * size, size)
         copies.append(pltpu.make_async_copy(weights.at[part], held.at[part], sems.at[k]))
-    for copy in copies:
+    for copy in copies[:4]:
         copy.start()
     copies[0].wait()
     copies[1].wait()
     for k in range(chunks):
         copies[k + 2].wait()
+        if k + 2 < chunks:
+            copies[k + 4].start()
         for i in range(k * size, (k + 1) * size, 2):
             product = nn(rows[...], jnp.concatenate([held[i], held[i + 1]], axis=1))
             mine[:, i * LANES : (i + 2) * LANES] = product[:tokens].astype(bf16)
@@ -292,7 +294,8 @@
     )
     block = pad_rows([down_new.astype(bf16), up_new.astype(bf16).reshape(up_rows, LANES)], rows)
     got = spread(jnp.broadcast_to(block[None], (z, rows, LANES)))
-    weights_all, _ = after(weights_all, got)
+    got_core = swap(got, "core")
+    weights_all, _, _ = after(weights_all, got, got_core)
     chunks = min(4, z)
     half = jax.ShapeDtypeStruct((tokens, width // 2), bf16)
     mine, other = pl.pallas_call(
@@ -314,7 +317,9 @@
         name="columns",
     )(rows_mine, rows_other, weights_all)
     got_yl, mine, other = after(swap(got, "yl"), mine, other)
-    got_last, got_core, other = swap(got_yl, "core"), swap(got, "core"), swap(other, "core")
+    got_last = swap(got_yl, "core")
+    other, _ = after(other, got_last)
+    other = swap(other, "core")
     refreshed = pl.pallas_call(
         refresh_kernel,
         out_shape=jax.ShapeDtypeStruct((tokens, features), bf16),

time: 169 us -> 171 us (1.012)
  waiting for transfers between devices: 32.9 us -> 36.3 us
    ppermute x9, waiting for transfers between devices: 10.3 us -> 13.7 us  [swap(): return lax.ppermute(array, axis, [(0, 1), (1, 0)])]
where the time goes in v7:
time: 171 us; the launch traced here: 170 us
  starting transfers between devices  70.2 us (41%)
  waiting for transfers between devices  36.3 us (21%)
  blocking collectives  28.1 us (16%)
  Pallas kernels  16.2 us (9%)
  between operations  15.1 us (9%)
  other arithmetic  3.17 us (2%)
    ppermute x9, starting transfers between devices, swap(): return lax.ppermute(array, axis, [(0, 1), (1, 0)])  35.4 us
    all_to_all x1, blocking collectives, spread(): return lax.all_to_all(copies, 'z', 0, 0)  28.1 us
    all_to_all x1, starting transfers between devices, spread(): return lax.all_to_all(copies, 'z', 0, 0)  14.9 us
    ppermute x9, waiting for transfers between devices, swap(): return lax.ppermute(array, axis, [(0, 1), (1, 0)])  13.7 us
    ppermute x2, waiting for transfers between devices, per_device(): lax.ppermute(next_rows, ('section', 'core'), [(s * 2 + (c ^ flip), (s - 1...  10.7 us
    all_to_all x1, starting transfers between devices, per_device(): parts = lax.all_to_all(kept.astype(bf16), 'z', 0, 0)  9.08 us
    pallas_call x1, Pallas kernels, per_device(): pl.pallas_call(columns_kernel, out_shape=(half, half), in_specs=[pl.Block...  5.4 us
    ppermute x2, starting transfers between devices, per_device(): lax.ppermute(next_rows, ('section', 'core'), [(s * 2 + (c ^ flip), (s - 1...  5.1 us
  transfers between devices with their start and end apart: 16, of which 10 were waited for; matrix products, arithmetic and copies ran while one was open for 2% of the time, Pallas kernels for 7%

profile of v7, /device:TPU:7, one launch (start us, length us, event | category | flops | bytes accessed | tf_op | source)
XLA Modules:
  0.0 170.2 jit_solution(8525187918783148838)
XLA Ops:
  7.2 0.0 copy-start.2
  7.2 0.0 copy-start
  7.2 1.9 %prepare.1 = (bf16[16,72,128]{2,1,0:T(8,128)(2,1)}, bf16[576,128]{1,0:T(8,128)(2,1)}) custom-call(f32[64,128]{1,0:T(8,128)} %bitcast.66, f32[1,512]{1,0:T(1,128)} %bitcast.68, s32[1,136]{1,0:T(1,128)} %loss_weight.3, bf16[128,512]{1,0:T(8,128)(2,1)} %bitcast.65), custom_call_target="tpu_custom_call" | custom-call | tf_op jit(solution)/shard_map/prepare/pallas_call | solution.py:230
  9.1 14.9 %all-to-all-start = ((bf16[16,72,128]{2,1,0:T(8,128)(2,1)}), bf16[16,72,128]{2,1,0:T(8,128)(2,1)S(1)}, u32[]{:S(2)}, u32[]{:S(2)}) async-start(bf16[16,72,128]{2,1,0:T(8,128)(2,1)} %get-tuple-element.27), calls=%async_computation | async-start | bytes 589824 | tf_op jit(solution)/shard_map/all_to_all | solution.py:41
  24.1 0.0 all-gather.3.cloned.1.call-start
  24.1 2.5 %collective-permute-start = (bf16[576,128]{1,0:T(8,128)(2,1)}, bf16[576,128]{1,0:T(8,128)(2,1)S(1)}, u32[]{:S(2)}, u32[]{:S(2)}) collective-permute-start(bf16[576,128]{1,0:T(8,128)(2,1)} %get-tuple-element.28), channel_id=1, source_target_pairs={{64,0},{66,2},{128,64},{130,66},{192,128},{194,130},{256,192},{258... | collective-permute-start | bytes 442376 | tf_op jit(solution)/shard_map/ppermute | solution.py:247
  26.6 3.2 %collective-permute-start.1 = (bf16[576,128]{1,0:T(8,128)(2,1)}, bf16[576,128]{1,0:T(8,128)(2,1)S(1)}, u32[]{:S(2)}, u32[]{:S(2)}) collective-permute-start(bf16[576,128]{1,0:T(8,128)(2,1)} %get-tuple-element.28), channel_id=1, source_target_pairs={{66,0},{64,2},{130,64},{128,66},{194,128},{192,130},{258,192},{256... | collective-permute-start | bytes 442376 | tf_op jit(solution)/shard_map/ppermute | solution.py:248
  29.8 4.5 %collective-permute-done = bf16[576,128]{1,0:T(8,128)(2,1)S(1)} collective-permute-done((bf16[576,128]{1,0:T(8,128)(2,1)}, bf16[576,128]{1,0:T(8,128)(2,1)S(1)}, u32[]{:S(2)}, u32[]{:S(2)}) %collective-permute-start) | collective-permute-done | bytes 147488 | tf_op jit(solution)/shard_map/ppermute | solution.py:247
  34.2 4.0 %collective-permute-done.1 = bf16[576,128]{1,0:T(8,128)(2,1)S(1)} collective-permute-done((bf16[576,128]{1,0:T(8,128)(2,1)}, bf16[576,128]{1,0:T(8,128)(2,1)S(1)}, u32[]{:S(2)}, u32[]{:S(2)}) %collective-permute-start.1) | collective-permute-done | bytes 147488 | tf_op jit(solution)/shard_map/ppermute | solution.py:248
  38.3 0.7 pad_maximum_fusion
  39.0 0.0 all-to-all-done.q0
  39.0 0.0 all-gather.3.cloned.1.call-update
  39.1 2.0 %collective-permute-start.2 = (bf16[16,72,128]{2,1,0:T(8,128)(2,1)S(1)}, bf16[16,72,128]{2,1,0:T(8,128)(2,1)S(1)}, u32[]{:S(2)}, u32[]{:S(2)}) collective-permute-start(bf16[16,72,128]{2,1,0:T(8,128)(2,1)S(1)} %all-to-all-done.q0), channel_id=1, source_target_pairs={{0,2},{2,0},{1,3},{3,1},{4,6},{6,4},{5,7},{7,5},{8,10},{10,8},{9,1... | collective-permute-start | bytes 884744 | tf_op jit(solution)/shard_map/ppermute | solution.py:33
  41.0 8.7 %collective-permute-start.3 = (bf16[16,72,128]{2,1,0:T(8,128)(2,1)S(1)}, bf16[16,72,128]{2,1,0:T(8,128)(2,1)S(1)}, u32[]{:S(2)}, u32[]{:S(2)}) collective-permute-start(bf16[16,72,128]{2,1,0:T(8,128)(2,1)S(1)} %all-to-all-done.q0), channel_id=1, source_target_pairs={{0,1},{1,0},{2,3},{3,2},{4,5},{5,4},{6,7},{7,6},{8,9},{9,8},{10,11... | collective-permute-start | bytes 884744 | tf_op jit(solution)/shard_map/ppermute | solution.py:33
  49.7 0.0 collective-permute-done.2.q1
  49.7 5.1 %collective-permute-start.4 = (bf16[16,72,128]{2,1,0:T(8,128)(2,1)S(1)}, bf16[16,72,128]{2,1,0:T(8,128)(2,1)S(1)}, u32[]{:S(2)}, u32[]{:S(2)}) collective-permute-start(bf16[16,72,128]{2,1,0:T(8,128)(2,1)S(1)} %collective-permute-done.2.q1), channel_id=1, source_target_pairs={{0,1},{1,0},{2,3},{3,2},{4,5},{5,4},{6,7},{7,6},{8,9},{9,8},{10,11... | collective-permute-start | bytes 884744 | tf_op jit(solution)/shard_map/ppermute | solution.py:33
  54.8 0.1 pad_add_fusion.place
  54.9 0.0 collective-permute-done.3.q2
  54.9 1.1 collective-permute-done.4.q3
  56.0 0.0 copy-done.2
  56.0 0.0 copy-done
  56.0 0.9 copy-done.1
  56.9 4.2 %backward.1 = (f32[2,16,72,128]{3,2,1,0:T(8,128)S(1)}, bf16[2,16,72,128]{3,2,1,0:T(8,128)(2,1)S(1)}, bf16[144,576]{1,0:T(8,128)(2,1)S(1)}) custom-call(s32[2]{0:T(128)S(1)} %pad_add_fusion.place, bf16[16,72,128]{2,1,0:T(8,128)(2,1)S(1)} %all-to-all-done.q0, bf16[16,72,128]{2,1,0:T(8,128)(2,1)S(1)} %collective-permute-done.2.q1, ...), custom_call_target="tpu_custom_call" | custom-call | tf_op jit(solution)/shard_map/backward/pallas_call | solution.py:257
  61.2 0.0 copy-start.3
  61.2 2.3 %collective-permute-start.5 = (bf16[2,16,72,128]{3,2,1,0:T(8,128)(2,1)S(1)}, bf16[2,16,72,128]{3,2,1,0:T(8,128)(2,1)S(1)}, u32[]{:S(2)}, u32[]{:S(2)}) collective-permute-start(bf16[2,16,72,128]{3,2,1,0:T(8,128)(2,1)S(1)} %get-tuple-element.31), channel_id=1, source_target_pairs={{0,1},{1,0},{2,3},{3,2},{4,5},{5,4},{6,7},{7,6},{8,9},{9,8},{10,11... | collective-permute-start | bytes 1769480 | tf_op jit(solution)/shard_map/ppermute | solution.py:33
  63.5 1.6 collective-permute-done.5
  65.1 0.1 convert_add_fusion
  65.2 0.0 copy-done.3
  65.2 0.0 copy-start.10
  65.2 0.0 copy-start.9
  65.3 0.0 copy-start.4
  65.3 0.0 copy-start.8
  65.3 0.0 copy-start.5
  65.3 0.0 copy-start.6
  65.3 0.0 copy-start.7
  65.3 3.3 %collective-permute-start.6 = (bf16[16,72,128]{2,1,0:T(8,128)(2,1)S(1)}, bf16[16,72,128]{2,1,0:T(8,128)(2,1)S(1)}, u32[]{:S(2)}, u32[]{:S(2)}) collective-permute-start(bf16[16,72,128]{2,1,0:T(8,128)(2,1)S(1)} %fusion.2), channel_id=1, source_target_pairs={{0,2},{2,0},{1,3},{3,1},{4,6},{6,4},{5,7},{7,5},{8,10},{10,8},{9,1... | collective-permute-start | bytes 884744 | tf_op jit(solution)/shard_map/ppermute | solution.py:33
  68.7 6.9 %collective-permute-done.6 = bf16[16,72,128]{2,1,0:T(8,128)(2,1)S(1)} collective-permute-done((bf16[16,72,128]{2,1,0:T(8,128)(2,1)S(1)}, bf16[16,72,128]{2,1,0:T(8,128)(2,1)S(1)}, u32[]{:S(2)}, u32[]{:S(2)}) %collective-permute-start.6) | collective-permute-done | bytes 294944 | tf_op jit(solution)/shard_map/ppermute | solution.py:33
  75.6 0.8 fusion.1
  76.4 9.1 %all-to-all-start.1 = ((bf16[16,72,128]{2,1,0:T(8,128)(2,1)}), bf16[16,72,128]{2,1,0:T(8,128)(2,1)S(1)}, u32[]{:S(2)}, u32[]{:S(2)}) async-start(bf16[16,72,128]{2,1,0:T(8,128)(2,1)} %fusion.1), calls=%async_computation.1 | async-start | bytes 589824 | tf_op jit(solution)/shard_map/all_to_all | solution.py:284
  86.2 0.1 pad.2.clone
  86.3 0.0 copy-done.10
  86.3 0.0 copy-done.4
  86.3 1.9 %collective-permute-start.7 = (bf16[144,576]{1,0:T(8,128)(2,1)S(1)}, bf16[144,576]{1,0:T(8,128)(2,1)S(1)}, u32[]{:S(2)}, u32[]{:S(2)}) collective-permute-start(bf16[144,576]{1,0:T(8,128)(2,1)S(1)} %copy-done.4), channel_id=1, source_target_pairs={{64,0},{65,1},{128,64},{129,65},{192,128},{193,129},{256,192},{257... | collective-permute-start | bytes 497672 | tf_op jit(solution)/shard_map/ppermute | solution.py:274
  88.2 3.2 %collective-permute-start.8 = (bf16[144,576]{1,0:T(8,128)(2,1)S(1)}, bf16[144,576]{1,0:T(8,128)(2,1)S(1)}, u32[]{:S(2)}, u32[]{:S(2)}) collective-permute-start(bf16[144,576]{1,0:T(8,128)(2,1)S(1)} %copy-done.4), channel_id=1, source_target_pairs={{65,0},{64,1},{129,64},{128,65},{193,128},{192,129},{257,192},{256... | collective-permute-start | bytes 497672 | tf_op jit(solution)/shard_map/ppermute | solution.py:274
  91.4 0.0 copy-done.9
  91.4 5.1 %collective-permute-done.7.rows_mine = bf16[144,576]{1,0:T(8,128)(2,1)S(1)} collective-permute-done((bf16[144,576]{1,0:T(8,128)(2,1)S(1)}, bf16[144,576]{1,0:T(8,128)(2,1)S(1)}, u32[]{:S(2)}, u32[]{:S(2)}) %collective-permute-start.7) | collective-permute-done | bytes 165920 | tf_op jit(solution)/shard_map/ppermute | solution.py:274
  96.6 5.6 %collective-permute-done.8.rows_other = bf16[144,576]{1,0:T(8,128)(2,1)S(1)} collective-permute-done((bf16[144,576]{1,0:T(8,128)(2,1)S(1)}, bf16[144,576]{1,0:T(8,128)(2,1)S(1)}, u32[]{:S(2)}, u32[]{:S(2)}) %collective-permute-start.8) | collective-permute-done | bytes 165920 | tf_op jit(solution)/shard_map/ppermute | solution.py:274
  102.1 3.4 %all-to-all-done.1 = bf16[16,72,128]{2,1,0:T(8,128)(2,1)S(1)} async-done(((bf16[16,72,128]{2,1,0:T(8,128)(2,1)}), bf16[16,72,128]{2,1,0:T(8,128)(2,1)S(1)}, u32[]{:S(2)}, u32[]{:S(2)}) %all-to-all-start.1) | async-done | bytes 294944 | tf_op jit(solution)/shard_map/all_to_all | solution.py:284
  105.6 0.7 fusion.10
  106.3 0.1 maximum_maximum_fusion
  106.4 28.1 %all_to_all.15.q0 = bf16[16,72,128]{2,1,0:T(8,128)(2,1)S(1)} all-to-all(bf16[16,72,128]{2,1,0:T(8,128)(2,1)S(1)} %broadcast_in_dim.28), channel_id=1, replica_groups=mesh['section'=8,'z'=16,'yl'=2,'core'=2] {'z'}, dimensions={0} | all-to-all | bytes 589824 | tf_op jit(solution)/shard_map/all_to_all | solution.py:41
  134.5 6.9 %collective-permute-start.10 = (bf16[16,72,128]{2,1,0:T(8,128)(2,1)S(1)}, bf16[16,72,128]{2,1,0:T(8,128)(2,1)S(1)}, u32[]{:S(2)}, u32[]{:S(2)}) collective-permute-start(bf16[16,72,128]{2,1,0:T(8,128)(2,1)S(1)} %all_to_all.15.q0), channel_id=1, source_target_pairs={{0,1},{1,0},{2,3},{3,2},{4,5},{5,4},{6,7},{7,6},{8,9},{9,8},{10,11... | collective-permute-start | bytes 884744 | tf_op jit(solution)/shard_map/ppermute | solution.py:33
  141.3 2.2 %collective-permute-start.9 = (bf16[16,72,128]{2,1,0:T(8,128)(2,1)S(1)}, bf16[16,72,128]{2,1,0:T(8,128)(2,1)S(1)}, u32[]{:S(2)}, u32[]{:S(2)}) collective-permute-start(bf16[16,72,128]{2,1,0:T(8,128)(2,1)S(1)} %all_to_all.15.q0), channel_id=1, source_target_pairs={{0,2},{2,0},{1,3},{3,1},{4,6},{6,4},{5,7},{7,5},{8,10},{10,8},{9,1... | collective-permute-start | bytes 884744 | tf_op jit(solution)/shard_map/ppermute | solution.py:33
  143.6 0.0 collective-permute-done.10.q2
  143.6 0.0 all-gather.3.cloned.1.call-done.weights
  143.6 5.4 %columns.1 = (bf16[136,4096]{1,0:T(8,128)(2,1)S(1)}, bf16[136,4096]{1,0:T(8,128)(2,1)}) custom-call(bf16[144,576]{1,0:T(8,128)(2,1)S(1)} %collective-permute-done.7.rows_mine, bf16[144,576]{1,0:T(8,128)(2,1)S(1)} %collective-permute-done.8.rows_other, bf16[32,576,128]{2,1,0:T(8,128)(2,1)} %all-gather.3.cloned.1.call-done.weights), custom_call_target="tpu_custom_call" | custom-call | flops 1283457024 | bytes 4718592 | tf_op jit(solution)/shard_map/columns/pallas_call | solution.py:301
  149.0 2.8 %collective-permute-done.9.q1 = bf16[16,72,128]{2,1,0:T(8,128)(2,1)S(1)} collective-permute-done((bf16[16,72,128]{2,1,0:T(8,128)(2,1)S(1)}, bf16[16,72,128]{2,1,0:T(8,128)(2,1)S(1)}, u32[]{:S(2)}, u32[]{:S(2)}) %collective-permute-start.9) | collective-permute-done | bytes 294944 | tf_op jit(solution)/shard_map/ppermute | solution.py:33
  151.9 2.7 %collective-permute-start.11 = (bf16[16,72,128]{2,1,0:T(8,128)(2,1)S(1)}, bf16[16,72,128]{2,1,0:T(8,128)(2,1)S(1)}, u32[]{:S(2)}, u32[]{:S(2)}) collective-permute-start(bf16[16,72,128]{2,1,0:T(8,128)(2,1)S(1)} %collective-permute-done.9.q1), channel_id=1, source_target_pairs={{0,1},{1,0},{2,3},{3,2},{4,5},{5,4},{6,7},{7,6},{8,9},{9,8},{10,11... | collective-permute-start | bytes 884744 | tf_op jit(solution)/shard_map/ppermute | solution.py:33
  154.6 1.2 collective-permute-done.11.q3
  155.8 2.3 %collective-permute-start.12 = (bf16[136,4096]{1,0:T(8,128)(2,1)}, bf16[136,4096]{1,0:T(8,128)(2,1)S(1)}, u32[]{:S(2)}, u32[]{:S(2)}) collective-permute-start(bf16[136,4096]{1,0:T(8,128)(2,1)} %get-tuple-element.43), channel_id=1, source_target_pairs={{0,1},{1,0},{2,3},{3,2},{4,5},{5,4},{6,7},{7,6},{8,9},{9,8},{10,11... | collective-permute-start | bytes 3342344 | tf_op jit(solution)/shard_map/ppermute | solution.py:33
  158.0 0.6 divide_subtract_fusion.1
  158.6 2.5 %refresh.1 = bf16[136,512]{1,0:T(8,128)(2,1)} custom-call(s32[2]{0:T(128)S(1)} %pad_add_fusion.place, bf16[16,72,128]{2,1,0:T(8,128)(2,1)S(1)} %all_to_all.15.q0, bf16[16,72,128]{2,1,0:T(8,128)(2,1)S(1)} %collective-permute-done.9.q1, bf16[16,72,128]{2,1,0:T(8,128)(2,1)S(1)} %collective-permute-done.10.q2, ...), custom_call_target="tpu_custom_call" | custom-call | tf_op jit(solution)/shard_map/refresh/pallas_call | solution.py:323
  161.1 0.0 collective-permute-done.12.other
  161.1 2.2 %merge.1 = bf16[136,8192]{1,0:T(8,128)(2,1)} custom-call(s32[2]{0:T(128)S(1)} %pad_add_fusion.place, bf16[136,4096]{1,0:T(8,128)(2,1)S(1)} %get-tuple-element.40.mine, bf16[136,4096]{1,0:T(8,128)(2,1)S(1)} %collective-permute-done.12.other), custom_call_target="tpu_custom_call" | custom-call | tf_op jit(solution)/shard_map/merge/pallas_call | solution.py:339
  (13 shorter events, 0.2 us)
Async XLA Ops:
  7.2 48.9 %copy-start.2 = (s32[1,136]{1,0:T(1,128)S(1)}, s32[1,136]{1,0:T(1,128)}, u32[]{:S(2)}) copy-start(s32[1,136]{1,0:T(1,128)} %loss_weight.3) | copy-start | bytes 1636
  7.2 48.9 %copy-start = (bf16[1,136,8192]{2,1,0:T(8,128)(2,1)S(1)}, bf16[1,136,8192]{2,1,0:T(8,128)(2,1)}, u32[]{:S(2)}) copy-start(bf16[1,136,8192]{2,1,0:T(8,128)(2,1)} %param.11) | copy-start | bytes 6684676
  9.1 29.9 %all-to-all-start = ((bf16[16,72,128]{2,1,0:T(8,128)(2,1)}), bf16[16,72,128]{2,1,0:T(8,128)(2,1)S(1)}, u32[]{:S(2)}, u32[]{:S(2)}) async-start(bf16[16,72,128]{2,1,0:T(8,128)(2,1)} %get-tuple-element.27), calls=%async_computation | async-start | bytes 589824 | tf_op jit(solution)/shard_map/all_to_all | solution.py:41
  24.1 119.5 %all-gather.3.cloned.1.call-start = ((), (), s32[]{:S(2)}) async-start(), calls=%async_computation.3 | async-start | bytes 5013504 | tf_op jit(solution)/shard_map/all_gather | solution.py:255
  24.1 10.1 %collective-permute-start = (bf16[576,128]{1,0:T(8,128)(2,1)}, bf16[576,128]{1,0:T(8,128)(2,1)S(1)}, u32[]{:S(2)}, u32[]{:S(2)}) collective-permute-start(bf16[576,128]{1,0:T(8,128)(2,1)} %get-tuple-element.28), channel_id=1, source_target_pairs={{64,0},{66,2},{128,64},{130,66},{192,128},{194,130},{256,192},{258... | collective-permute-start | bytes 442376 | tf_op jit(solution)/shard_map/ppermute | solution.py:247
  26.6 11.7 %collective-permute-start.1 = (bf16[576,128]{1,0:T(8,128)(2,1)}, bf16[576,128]{1,0:T(8,128)(2,1)S(1)}, u32[]{:S(2)}, u32[]{:S(2)}) collective-permute-start(bf16[576,128]{1,0:T(8,128)(2,1)} %get-tuple-element.28), channel_id=1, source_target_pairs={{66,0},{64,2},{130,64},{128,66},{194,128},{192,130},{258,192},{256... | collective-permute-start | bytes 442376 | tf_op jit(solution)/shard_map/ppermute | solution.py:248
  39.1 10.7 %collective-permute-start.2 = (bf16[16,72,128]{2,1,0:T(8,128)(2,1)S(1)}, bf16[16,72,128]{2,1,0:T(8,128)(2,1)S(1)}, u32[]{:S(2)}, u32[]{:S(2)}) collective-permute-start(bf16[16,72,128]{2,1,0:T(8,128)(2,1)S(1)} %all-to-all-done.q0), channel_id=1, source_target_pairs={{0,2},{2,0},{1,3},{3,1},{4,6},{6,4},{5,7},{7,5},{8,10},{10,8},{9,1... | collective-permute-start | bytes 884744 | tf_op jit(solution)/shard_map/ppermute | solution.py:33
  41.0 13.9 %collective-permute-start.3 = (bf16[16,72,128]{2,1,0:T(8,128)(2,1)S(1)}, bf16[16,72,128]{2,1,0:T(8,128)(2,1)S(1)}, u32[]{:S(2)}, u32[]{:S(2)}) collective-permute-start(bf16[16,72,128]{2,1,0:T(8,128)(2,1)S(1)} %all-to-all-done.q0), channel_id=1, source_target_pairs={{0,1},{1,0},{2,3},{3,2},{4,5},{5,4},{6,7},{7,6},{8,9},{9,8},{10,11... | collective-permute-start | bytes 884744 | tf_op jit(solution)/shard_map/ppermute | solution.py:33
  49.7 6.3 %collective-permute-start.4 = (bf16[16,72,128]{2,1,0:T(8,128)(2,1)S(1)}, bf16[16,72,128]{2,1,0:T(8,128)(2,1)S(1)}, u32[]{:S(2)}, u32[]{:S(2)}) collective-permute-start(bf16[16,72,128]{2,1,0:T(8,128)(2,1)S(1)} %collective-permute-done.2.q1), channel_id=1, source_target_pairs={{0,1},{1,0},{2,3},{3,2},{4,5},{5,4},{6,7},{7,6},{8,9},{9,8},{10,11... | collective-permute-start | bytes 884744 | tf_op jit(solution)/shard_map/ppermute | solution.py:33
  56.0 0.9 copy-start.1
  61.2 4.0 %copy-start.3 = (bf16[144,576]{1,0:T(8,128)(2,1)}, bf16[144,576]{1,0:T(8,128)(2,1)S(1)}, u32[]{:S(2)}) copy-start(bf16[144,576]{1,0:T(8,128)(2,1)S(1)} %get-tuple-element.32) | copy-start | bytes 497668
  61.2 3.9 %collective-permute-start.5 = (bf16[2,16,72,128]{3,2,1,0:T(8,128)(2,1)S(1)}, bf16[2,16,72,128]{3,2,1,0:T(8,128)(2,1)S(1)}, u32[]{:S(2)}, u32[]{:S(2)}) collective-permute-start(bf16[2,16,72,128]{3,2,1,0:T(8,128)(2,1)S(1)} %get-tuple-element.31), channel_id=1, source_target_pairs={{0,1},{1,0},{2,3},{3,2},{4,5},{5,4},{6,7},{7,6},{8,9},{9,8},{10,11... | collective-permute-start | bytes 1769480 | tf_op jit(solution)/shard_map/ppermute | solution.py:33
  65.2 21.1 %copy-start.10 = (f32[1,1,512]{2,1,0:T(1,128)S(1)}, f32[1,1,512]{2,1,0:T(1,128)}, u32[]{:S(2)}) copy-start(f32[1,1,512]{2,1,0:T(1,128)} %param.19) | copy-start | bytes 6148
  65.2 26.2 %copy-start.9 = (f32[1,1,512]{2,1,0:T(1,128)S(1)}, f32[1,1,512]{2,1,0:T(1,128)}, u32[]{:S(2)}) copy-start(f32[1,1,512]{2,1,0:T(1,128)} %param.20) | copy-start | bytes 6148
  65.3 21.0 %copy-start.4 = (bf16[144,576]{1,0:T(8,128)(2,1)S(1)}, bf16[144,576]{1,0:T(8,128)(2,1)}, u32[]{:S(2)}) copy-start(bf16[144,576]{1,0:T(8,128)(2,1)} %copy-done.3) | copy-start | bytes 497668
  65.3 40.3 %copy-start.8 = (f32[1,1,512]{2,1,0:T(1,128)S(1)}, f32[1,1,512]{2,1,0:T(1,128)}, u32[]{:S(2)}) copy-start(f32[1,1,512]{2,1,0:T(1,128)} %param.18) | copy-start | bytes 6148
  65.3 40.3 %copy-start.5 = (f32[1,128,64]{1,2,0:T(8,128)S(1)}, f32[1,128,64]{1,2,0:T(8,128)}, u32[]{:S(2)}) copy-start(f32[1,128,64]{1,2,0:T(8,128)} %param.15) | copy-start | bytes 98308
  65.3 40.3 %copy-start.6 = (f32[1,128,64]{1,2,0:T(8,128)S(1)}, f32[1,128,64]{1,2,0:T(8,128)}, u32[]{:S(2)}) copy-start(f32[1,128,64]{1,2,0:T(8,128)} %param.17) | copy-start | bytes 98308
  65.3 40.3 %copy-start.7 = (f32[1,128,64]{1,2,0:T(8,128)S(1)}, f32[1,128,64]{1,2,0:T(8,128)}, u32[]{:S(2)}) copy-start(f32[1,128,64]{1,2,0:T(8,128)} %param.16) | copy-start | bytes 98308
  65.3 10.2 %collective-permute-start.6 = (bf16[16,72,128]{2,1,0:T(8,128)(2,1)S(1)}, bf16[16,72,128]{2,1,0:T(8,128)(2,1)S(1)}, u32[]{:S(2)}, u32[]{:S(2)}) collective-permute-start(bf16[16,72,128]{2,1,0:T(8,128)(2,1)S(1)} %fusion.2), channel_id=1, source_target_pairs={{0,2},{2,0},{1,3},{3,1},{4,6},{6,4},{5,7},{7,5},{8,10},{10,8},{9,1... | collective-permute-start | bytes 884744 | tf_op jit(solution)/shard_map/ppermute | solution.py:33
  76.4 29.1 %all-to-all-start.1 = ((bf16[16,72,128]{2,1,0:T(8,128)(2,1)}), bf16[16,72,128]{2,1,0:T(8,128)(2,1)S(1)}, u32[]{:S(2)}, u32[]{:S(2)}) async-start(bf16[16,72,128]{2,1,0:T(8,128)(2,1)} %fusion.1), calls=%async_computation.1 | async-start | bytes 589824 | tf_op jit(solution)/shard_map/all_to_all | solution.py:284
  86.3 10.3 %collective-permute-start.7 = (bf16[144,576]{1,0:T(8,128)(2,1)S(1)}, bf16[144,576]{1,0:T(8,128)(2,1)S(1)}, u32[]{:S(2)}, u32[]{:S(2)}) collective-permute-start(bf16[144,576]{1,0:T(8,128)(2,1)S(1)} %copy-done.4), channel_id=1, source_target_pairs={{64,0},{65,1},{128,64},{129,65},{192,128},{193,129},{256,192},{257... | collective-permute-start | bytes 497672 | tf_op jit(solution)/shard_map/ppermute | solution.py:274
  88.2 13.9 %collective-permute-start.8 = (bf16[144,576]{1,0:T(8,128)(2,1)S(1)}, bf16[144,576]{1,0:T(8,128)(2,1)S(1)}, u32[]{:S(2)}, u32[]{:S(2)}) collective-permute-start(bf16[144,576]{1,0:T(8,128)(2,1)S(1)} %copy-done.4), channel_id=1, source_target_pairs={{65,0},{64,1},{129,64},{128,65},{193,128},{192,129},{257,192},{256... | collective-permute-start | bytes 497672 | tf_op jit(solution)/shard_map/ppermute | solution.py:274
  134.5 9.1 %collective-permute-start.10 = (bf16[16,72,128]{2,1,0:T(8,128)(2,1)S(1)}, bf16[16,72,128]{2,1,0:T(8,128)(2,1)S(1)}, u32[]{:S(2)}, u32[]{:S(2)}) collective-permute-start(bf16[16,72,128]{2,1,0:T(8,128)(2,1)S(1)} %all_to_all.15.q0), channel_id=1, source_target_pairs={{0,1},{1,0},{2,3},{3,2},{4,5},{5,4},{6,7},{7,6},{8,9},{9,8},{10,11... | collective-permute-start | bytes 884744 | tf_op jit(solution)/shard_map/ppermute | solution.py:33
  141.3 10.5 %collective-permute-start.9 = (bf16[16,72,128]{2,1,0:T(8,128)(2,1)S(1)}, bf16[16,72,128]{2,1,0:T(8,128)(2,1)S(1)}, u32[]{:S(2)}, u32[]{:S(2)}) collective-permute-start(bf16[16,72,128]{2,1,0:T(8,128)(2,1)S(1)} %all_to_all.15.q0), channel_id=1, source_target_pairs={{0,2},{2,0},{1,3},{3,1},{4,6},{6,4},{5,7},{7,5},{8,10},{10,8},{9,1... | collective-permute-start | bytes 884744 | tf_op jit(solution)/shard_map/ppermute | solution.py:33
  151.9 3.9 %collective-permute-start.11 = (bf16[16,72,128]{2,1,0:T(8,128)(2,1)S(1)}, bf16[16,72,128]{2,1,0:T(8,128)(2,1)S(1)}, u32[]{:S(2)}, u32[]{:S(2)}) collective-permute-start(bf16[16,72,128]{2,1,0:T(8,128)(2,1)S(1)} %collective-permute-done.9.q1), channel_id=1, source_target_pairs={{0,1},{1,0},{2,3},{3,2},{4,5},{5,4},{6,7},{7,6},{8,9},{9,8},{10,11... | collective-permute-start | bytes 884744 | tf_op jit(solution)/shard_map/ppermute | solution.py:33
  155.8 5.4 %collective-permute-start.12 = (bf16[136,4096]{1,0:T(8,128)(2,1)}, bf16[136,4096]{1,0:T(8,128)(2,1)S(1)}, u32[]{:S(2)}, u32[]{:S(2)}) collective-permute-start(bf16[136,4096]{1,0:T(8,128)(2,1)} %get-tuple-element.43), channel_id=1, source_target_pairs={{0,1},{1,0},{2,3},{3,2},{4,5},{5,4},{6,7},{7,6},{8,9},{9,8},{10,11... | collective-permute-start | bytes 3342344 | tf_op jit(solution)/shard_map/ppermute | solution.py:33
Sparse Core Ops, SparseCore 0:
  39.2 96.5 all-gather.2

commit v8 on v6

--- a/solution.py
+++ b/solution.py
@@ -154,15 +154,6 @@
             send[half, i, rank:, :] = up_grad[row : row + EXTRA].astype(bf16)
 
 
-def refresh_kernel(place, q0, q1, q2, q3, acts, out, down, extra):
-    core, yl = place[0], place[1]
-    rank = down.shape[0]
-    unpack(core, yl, (q0, q1, q2, q3), down, extra, rank)
-    up, _ = up_rows_of(core, yl, extra, q0.shape[0], rank, out.shape[1] // LANES)
-    low = nt(acts[...], down[...]).astype(bf16)
-    out[...] = (adapter_scale * nn(low, up)).astype(bf16)
-
-
 def columns_kernel(rows_mine, rows_other, weights, mine, other, rows, held, sems):
     tokens, second = mine.shape[0], rows_mine.shape[0]
     chunks = sems.shape[0] - 2
@@ -186,13 +177,21 @@
             other[:, i * LANES : (i + 2) * LANES] = product[second : second + tokens].astype(bf16)
 
 
-def merge_kernel(place, mine, other, out):
-    core = place[0]
+def finish_kernel(place, q0, q1, q2, q3, acts, mine, other, out, upstream, down, extra, merged, sem):
+    core, yl = place[0], place[1]
+    rank = down.shape[0]
     for i in range(mine.shape[1] // LANES):
         a, b = mine[:, i * LANES : (i + 1) * LANES], other[:, i * LANES : (i + 1) * LANES]
         at = i * 2 * LANES
-        out[:, at : at + LANES] = jnp.where(core == 0, a, b)
-        out[:, at + LANES : at + 2 * LANES] = jnp.where(core == 0, b, a)
+        merged[:, at : at + LANES] = jnp.where(core == 0, a, b)
+        merged[:, at + LANES : at + 2 * LANES] = jnp.where(core == 0, b, a)
+    copy = pltpu.make_async_copy(merged, upstream, sem)
+    copy.start()
+    unpack(core, yl, (q0, q1, q2, q3), down, extra, rank)
+    up, _ = up_rows_of(core, yl, extra, q0.shape[0], rank, out.shape[1] // LANES)
+    low = nt(acts[...], down[...]).astype(bf16)
+    out[...] = (adapter_scale * nn(low, up)).astype(bf16)
+    copy.wait()
 
 
 def whole(n):
@@ -315,31 +314,23 @@
     )(rows_mine, rows_other, weights_all)
     got_yl, mine, other = after(swap(got, "yl"), mine, other)
     got_last, got_core, other = swap(got_yl, "core"), swap(got, "core"), swap(other, "core")
-    refreshed = pl.pallas_call(
-        refresh_kernel,
-        out_shape=jax.ShapeDtypeStruct((tokens, features), bf16),
-        in_specs=[SCALARS] + whole(5),
-        out_specs=whole(1)[0],
+    refreshed, upstream = pl.pallas_call(
+        finish_kernel,
+        out_shape=(
+            jax.ShapeDtypeStruct((tokens, features), bf16),
+            jax.ShapeDtypeStruct((tokens, width), bf16),
+        ),
+        in_specs=[SCALARS] + whole(7),
+        out_specs=(whole(1)[0], pl.BlockSpec(memory_space=pl.ANY)),
         scratch_shapes=[
             pltpu.VMEM((rank, width), bf16),
             pltpu.VMEM((4 * z * EXTRA, LANES), bf16),
+            pltpu.VMEM((tokens, width), bf16),
+            pltpu.SemaphoreType.DMA,
         ],
         compiler_params=params,
-        name="refresh",
-    )(place, got, got_yl, got_core, got_last, acts)
-
-    other, refreshed = after(other, refreshed)
-    steps = 2
-    half_spec = pl.BlockSpec((tokens, width // 2 // steps), lambda i: (0, i))
-    upstream = pl.pallas_call(
-        merge_kernel,
-        out_shape=jax.ShapeDtypeStruct((tokens, width), bf16),
-        grid=(steps,),
-        in_specs=[SCALARS, half_spec, half_spec],
-        out_specs=pl.BlockSpec((tokens, width // steps), lambda i: (0, i)),
-        compiler_params=params,
-        name="merge",
-    )(place, mine, other)
+        name="finish",
+    )(place, got, got_yl, got_core, got_last, acts, mine, other)
     return (
         upstream[None],
         refreshed[None],

time: 169 us -> 168 us (level)
    pallas_call x2 -> x1, Pallas kernels: 4.68 us -> 4.22 us  [per_device(): pl.pallas_call(finish_kernel, out_shape=(jax.ShapeDtypeStruct((tokens, fe...]
  transfers between devices with their start and end apart: 16 -> 16, of which waited for: 10 -> 9; matrix products, arithmetic and copies ran while one was open for 2% -> 2% of each run, Pallas kernels for 7% -> 6%
where the time goes in v8:
time: 168 us; the launch traced here: 166 us
  starting transfers between devices  70.4 us (42%)
  waiting for transfers between devices  32.6 us (19%)
  blocking collectives  28 us (17%)
  Pallas kernels  15.7 us (9%)
  between operations  15.1 us (9%)
  other arithmetic  3.18 us (2%)
    ppermute x9, starting transfers between devices, swap(): return lax.ppermute(array, axis, [(0, 1), (1, 0)])  35.6 us
    all_to_all x1, blocking collectives, spread(): return lax.all_to_all(copies, 'z', 0, 0)  28 us
    all_to_all x1, starting transfers between devices, spread(): return lax.all_to_all(copies, 'z', 0, 0)  14.9 us
    ppermute x2, waiting for transfers between devices, per_device(): lax.ppermute(next_rows, ('section', 'core'), [(s * 2 + (c ^ flip), (s - 1...  10.7 us
    ppermute x9, waiting for transfers between devices, swap(): return lax.ppermute(array, axis, [(0, 1), (1, 0)])  10.2 us
    all_to_all x1, starting transfers between devices, per_device(): parts = lax.all_to_all(kept.astype(bf16), 'z', 0, 0)  9.09 us
    pallas_call x1, Pallas kernels, per_device(): pl.pallas_call(columns_kernel, out_shape=(half, half), in_specs=[pl.Block...  5.29 us
    ppermute x2, starting transfers between devices, per_device(): lax.ppermute(next_rows, ('section', 'core'), [(s * 2 + (c ^ flip), (s - 1...  5.09 us
  transfers between devices with their start and end apart: 16, of which 9 were waited for; matrix products, arithmetic and copies ran while one was open for 2% of the time, Pallas kernels for 6%

profile of v8, /device:TPU:7, one launch (start us, length us, event | category | flops | bytes accessed | tf_op | source)
XLA Modules:
  0.0 166.1 jit_solution(13054550763744134450)
XLA Ops:
  7.2 0.0 copy-start.2
  7.2 0.0 copy-start
  7.2 1.9 %prepare.1 = (bf16[16,72,128]{2,1,0:T(8,128)(2,1)}, bf16[576,128]{1,0:T(8,128)(2,1)}) custom-call(f32[64,128]{1,0:T(8,128)} %bitcast.64, f32[1,512]{1,0:T(1,128)} %bitcast.66, s32[1,136]{1,0:T(1,128)} %loss_weight.3, bf16[128,512]{1,0:T(8,128)(2,1)} %bitcast.63), custom_call_target="tpu_custom_call" | custom-call | tf_op jit(solution)/shard_map/prepare/pallas_call | solution.py:227
  9.1 14.9 %all-to-all-start = ((bf16[16,72,128]{2,1,0:T(8,128)(2,1)}), bf16[16,72,128]{2,1,0:T(8,128)(2,1)S(1)}, u32[]{:S(2)}, u32[]{:S(2)}) async-start(bf16[16,72,128]{2,1,0:T(8,128)(2,1)} %get-tuple-element.26), calls=%async_computation | async-start | bytes 589824 | tf_op jit(solution)/shard_map/all_to_all | solution.py:41
  24.1 0.0 all-gather.3.cloned.1.call-start
  24.1 2.5 %collective-permute-start = (bf16[576,128]{1,0:T(8,128)(2,1)}, bf16[576,128]{1,0:T(8,128)(2,1)S(1)}, u32[]{:S(2)}, u32[]{:S(2)}) collective-permute-start(bf16[576,128]{1,0:T(8,128)(2,1)} %get-tuple-element.27), channel_id=1, source_target_pairs={{64,0},{66,2},{128,64},{130,66},{192,128},{194,130},{256,192},{258... | collective-permute-start | bytes 442376 | tf_op jit(solution)/shard_map/ppermute | solution.py:244
  26.6 3.2 %collective-permute-start.1 = (bf16[576,128]{1,0:T(8,128)(2,1)}, bf16[576,128]{1,0:T(8,128)(2,1)S(1)}, u32[]{:S(2)}, u32[]{:S(2)}) collective-permute-start(bf16[576,128]{1,0:T(8,128)(2,1)} %get-tuple-element.27), channel_id=1, source_target_pairs={{66,0},{64,2},{130,64},{128,66},{194,128},{192,130},{258,192},{256... | collective-permute-start | bytes 442376 | tf_op jit(solution)/shard_map/ppermute | solution.py:245
  29.8 4.5 %collective-permute-done = bf16[576,128]{1,0:T(8,128)(2,1)S(1)} collective-permute-done((bf16[576,128]{1,0:T(8,128)(2,1)}, bf16[576,128]{1,0:T(8,128)(2,1)S(1)}, u32[]{:S(2)}, u32[]{:S(2)}) %collective-permute-start) | collective-permute-done | bytes 147488 | tf_op jit(solution)/shard_map/ppermute | solution.py:244
  34.2 4.0 %collective-permute-done.1 = bf16[576,128]{1,0:T(8,128)(2,1)S(1)} collective-permute-done((bf16[576,128]{1,0:T(8,128)(2,1)}, bf16[576,128]{1,0:T(8,128)(2,1)S(1)}, u32[]{:S(2)}, u32[]{:S(2)}) %collective-permute-start.1) | collective-permute-done | bytes 147488 | tf_op jit(solution)/shard_map/ppermute | solution.py:245
  38.3 0.7 pad_maximum_fusion
  39.0 0.0 all-to-all-done.q0
  39.0 0.0 all-gather.3.cloned.1.call-update
  39.1 2.0 %collective-permute-start.2 = (bf16[16,72,128]{2,1,0:T(8,128)(2,1)S(1)}, bf16[16,72,128]{2,1,0:T(8,128)(2,1)S(1)}, u32[]{:S(2)}, u32[]{:S(2)}) collective-permute-start(bf16[16,72,128]{2,1,0:T(8,128)(2,1)S(1)} %all-to-all-done.q0), channel_id=1, source_target_pairs={{0,2},{2,0},{1,3},{3,1},{4,6},{6,4},{5,7},{7,5},{8,10},{10,8},{9,1... | collective-permute-start | bytes 884744 | tf_op jit(solution)/shard_map/ppermute | solution.py:33
  41.1 8.7 %collective-permute-start.3 = (bf16[16,72,128]{2,1,0:T(8,128)(2,1)S(1)}, bf16[16,72,128]{2,1,0:T(8,128)(2,1)S(1)}, u32[]{:S(2)}, u32[]{:S(2)}) collective-permute-start(bf16[16,72,128]{2,1,0:T(8,128)(2,1)S(1)} %all-to-all-done.q0), channel_id=1, source_target_pairs={{0,1},{1,0},{2,3},{3,2},{4,5},{5,4},{6,7},{7,6},{8,9},{9,8},{10,11... | collective-permute-start | bytes 884744 | tf_op jit(solution)/shard_map/ppermute | solution.py:33
  49.7 0.0 collective-permute-done.2.q1
  49.7 5.1 %collective-permute-start.4 = (bf16[16,72,128]{2,1,0:T(8,128)(2,1)S(1)}, bf16[16,72,128]{2,1,0:T(8,128)(2,1)S(1)}, u32[]{:S(2)}, u32[]{:S(2)}) collective-permute-start(bf16[16,72,128]{2,1,0:T(8,128)(2,1)S(1)} %collective-permute-done.2.q1), channel_id=1, source_target_pairs={{0,1},{1,0},{2,3},{3,2},{4,5},{5,4},{6,7},{7,6},{8,9},{9,8},{10,11... | collective-permute-start | bytes 884744 | tf_op jit(solution)/shard_map/ppermute | solution.py:33
  54.8 0.1 pad_add_fusion.place
  54.9 0.0 collective-permute-done.3.q2
  54.9 1.1 collective-permute-done.4.q3
  56.0 0.0 copy-done.2
  56.0 0.0 copy-done
  56.0 0.9 copy-done.1
  56.9 4.2 %backward.1 = (f32[2,16,72,128]{3,2,1,0:T(8,128)S(1)}, bf16[2,16,72,128]{3,2,1,0:T(8,128)(2,1)S(1)}, bf16[144,576]{1,0:T(8,128)(2,1)S(1)}) custom-call(s32[2]{0:T(128)S(1)} %pad_add_fusion.place, bf16[16,72,128]{2,1,0:T(8,128)(2,1)S(1)} %all-to-all-done.q0, bf16[16,72,128]{2,1,0:T(8,128)(2,1)S(1)} %collective-permute-done.2.q1, ...), custom_call_target="tpu_custom_call" | custom-call | tf_op jit(solution)/shard_map/backward/pallas_call | solution.py:254
  61.2 0.0 copy-start.3
  61.2 2.3 %collective-permute-start.5 = (bf16[2,16,72,128]{3,2,1,0:T(8,128)(2,1)S(1)}, bf16[2,16,72,128]{3,2,1,0:T(8,128)(2,1)S(1)}, u32[]{:S(2)}, u32[]{:S(2)}) collective-permute-start(bf16[2,16,72,128]{3,2,1,0:T(8,128)(2,1)S(1)} %get-tuple-element.30), channel_id=1, source_target_pairs={{0,1},{1,0},{2,3},{3,2},{4,5},{5,4},{6,7},{7,6},{8,9},{9,8},{10,11... | collective-permute-start | bytes 1769480 | tf_op jit(solution)/shard_map/ppermute | solution.py:33
  63.5 1.6 collective-permute-done.5
  65.1 0.1 convert_add_fusion
  65.2 0.0 copy-done.3
  65.2 0.0 copy-start.10
  65.2 0.0 copy-start.9
  65.3 0.0 copy-start.8
  65.3 0.0 copy-start.5
  65.3 0.0 copy-start.6
  65.3 0.0 copy-start.7
  65.3 3.3 %collective-permute-start.6 = (bf16[16,72,128]{2,1,0:T(8,128)(2,1)S(1)}, bf16[16,72,128]{2,1,0:T(8,128)(2,1)S(1)}, u32[]{:S(2)}, u32[]{:S(2)}) collective-permute-start(bf16[16,72,128]{2,1,0:T(8,128)(2,1)S(1)} %fusion.2), channel_id=1, source_target_pairs={{0,2},{2,0},{1,3},{3,1},{4,6},{6,4},{5,7},{7,5},{8,10},{10,8},{9,1... | collective-permute-start | bytes 884744 | tf_op jit(solution)/shard_map/ppermute | solution.py:33
  68.7 6.9 %collective-permute-done.6 = bf16[16,72,128]{2,1,0:T(8,128)(2,1)S(1)} collective-permute-done((bf16[16,72,128]{2,1,0:T(8,128)(2,1)S(1)}, bf16[16,72,128]{2,1,0:T(8,128)(2,1)S(1)}, u32[]{:S(2)}, u32[]{:S(2)}) %collective-permute-start.6) | collective-permute-done | bytes 294944 | tf_op jit(solution)/shard_map/ppermute | solution.py:33
  75.6 0.8 fusion.1
  76.4 9.1 %all-to-all-start.1 = ((bf16[16,72,128]{2,1,0:T(8,128)(2,1)}), bf16[16,72,128]{2,1,0:T(8,128)(2,1)S(1)}, u32[]{:S(2)}, u32[]{:S(2)}) async-start(bf16[16,72,128]{2,1,0:T(8,128)(2,1)} %fusion.1), calls=%async_computation.1 | async-start | bytes 589824 | tf_op jit(solution)/shard_map/all_to_all | solution.py:281
  86.2 0.1 pad.2.clone
  86.3 0.0 copy-done.10
  86.3 0.0 copy-done.4
  86.3 1.9 %collective-permute-start.7 = (bf16[144,576]{1,0:T(8,128)(2,1)S(1)}, bf16[144,576]{1,0:T(8,128)(2,1)S(1)}, u32[]{:S(2)}, u32[]{:S(2)}) collective-permute-start(bf16[144,576]{1,0:T(8,128)(2,1)S(1)} %copy-done.4), channel_id=1, source_target_pairs={{64,0},{65,1},{128,64},{129,65},{192,128},{193,129},{256,192},{257... | collective-permute-start | bytes 497672 | tf_op jit(solution)/shard_map/ppermute | solution.py:271
  88.2 3.2 %collective-permute-start.8 = (bf16[144,576]{1,0:T(8,128)(2,1)S(1)}, bf16[144,576]{1,0:T(8,128)(2,1)S(1)}, u32[]{:S(2)}, u32[]{:S(2)}) collective-permute-start(bf16[144,576]{1,0:T(8,128)(2,1)S(1)} %copy-done.4), channel_id=1, source_target_pairs={{65,0},{64,1},{129,64},{128,65},{193,128},{192,129},{257,192},{256... | collective-permute-start | bytes 497672 | tf_op jit(solution)/shard_map/ppermute | solution.py:271
  91.4 5.1 %collective-permute-done.7.rows_mine = bf16[144,576]{1,0:T(8,128)(2,1)S(1)} collective-permute-done((bf16[144,576]{1,0:T(8,128)(2,1)S(1)}, bf16[144,576]{1,0:T(8,128)(2,1)S(1)}, u32[]{:S(2)}, u32[]{:S(2)}) %collective-permute-start.7) | collective-permute-done | bytes 165920 | tf_op jit(solution)/shard_map/ppermute | solution.py:271
  96.6 5.6 %collective-permute-done.8.rows_other = bf16[144,576]{1,0:T(8,128)(2,1)S(1)} collective-permute-done((bf16[144,576]{1,0:T(8,128)(2,1)S(1)}, bf16[144,576]{1,0:T(8,128)(2,1)S(1)}, u32[]{:S(2)}, u32[]{:S(2)}) %collective-permute-start.8) | collective-permute-done | bytes 165920 | tf_op jit(solution)/shard_map/ppermute | solution.py:271
  102.1 3.2 %all-to-all-done.1 = bf16[16,72,128]{2,1,0:T(8,128)(2,1)S(1)} async-done(((bf16[16,72,128]{2,1,0:T(8,128)(2,1)}), bf16[16,72,128]{2,1,0:T(8,128)(2,1)S(1)}, u32[]{:S(2)}, u32[]{:S(2)}) %all-to-all-start.1) | async-done | bytes 294944 | tf_op jit(solution)/shard_map/all_to_all | solution.py:281
  105.4 0.0 copy-done.5
  105.4 0.0 copy-done.6
  105.4 0.0 copy-done.7
  105.4 0.7 fusion.10
  106.1 0.1 maximum_maximum_fusion
  106.2 28.0 %all_to_all.15.q0 = bf16[16,72,128]{2,1,0:T(8,128)(2,1)S(1)} all-to-all(bf16[16,72,128]{2,1,0:T(8,128)(2,1)S(1)} %broadcast_in_dim.28), channel_id=1, replica_groups=mesh['section'=8,'z'=16,'yl'=2,'core'=2] {'z'}, dimensions={0} | all-to-all | bytes 589824 | tf_op jit(solution)/shard_map/all_to_all | solution.py:41
  134.1 2.5 %collective-permute-start.9 = (bf16[16,72,128]{2,1,0:T(8,128)(2,1)S(1)}, bf16[16,72,128]{2,1,0:T(8,128)(2,1)S(1)}, u32[]{:S(2)}, u32[]{:S(2)}) collective-permute-start(bf16[16,72,128]{2,1,0:T(8,128)(2,1)S(1)} %all_to_all.15.q0), channel_id=1, source_target_pairs={{0,2},{2,0},{1,3},{3,1},{4,6},{6,4},{5,7},{7,5},{8,10},{10,8},{9,1... | collective-permute-start | bytes 884744 | tf_op jit(solution)/shard_map/ppermute | solution.py:33
  136.6 0.0 all-gather.3.cloned.1.call-done.weights
  136.7 5.3 %columns.1 = (bf16[136,4096]{1,0:T(8,128)(2,1)S(1)}, bf16[136,4096]{1,0:T(8,128)(2,1)}) custom-call(bf16[144,576]{1,0:T(8,128)(2,1)S(1)} %collective-permute-done.7.rows_mine, bf16[144,576]{1,0:T(8,128)(2,1)S(1)} %collective-permute-done.8.rows_other, bf16[32,576,128]{2,1,0:T(8,128)(2,1)} %all-gather.3.cloned.1.call-done.weights), custom_call_target="tpu_custom_call" | custom-call | flops 1283457024 | bytes 4718592 | tf_op jit(solution)/shard_map/columns/pallas_call | solution.py:297
  142.0 0.0 collective-permute-done.9.q1
  142.0 7.5 %collective-permute-start.12 = (bf16[136,4096]{1,0:T(8,128)(2,1)}, bf16[136,4096]{1,0:T(8,128)(2,1)S(1)}, u32[]{:S(2)}, u32[]{:S(2)}) collective-permute-start(bf16[136,4096]{1,0:T(8,128)(2,1)} %get-tuple-element.41), channel_id=1, source_target_pairs={{0,1},{1,0},{2,3},{3,2},{4,5},{5,4},{6,7},{7,6},{8,9},{9,8},{10,11... | collective-permute-start | bytes 3342344 | tf_op jit(solution)/shard_map/ppermute | solution.py:33
  149.4 1.9 %collective-permute-start.10 = (bf16[16,72,128]{2,1,0:T(8,128)(2,1)S(1)}, bf16[16,72,128]{2,1,0:T(8,128)(2,1)S(1)}, u32[]{:S(2)}, u32[]{:S(2)}) collective-permute-start(bf16[16,72,128]{2,1,0:T(8,128)(2,1)S(1)} %all_to_all.15.q0), channel_id=1, source_target_pairs={{0,1},{1,0},{2,3},{3,2},{4,5},{5,4},{6,7},{7,6},{8,9},{9,8},{10,11... | collective-permute-start | bytes 884744 | tf_op jit(solution)/shard_map/ppermute | solution.py:33
  151.4 2.4 %collective-permute-start.11 = (bf16[16,72,128]{2,1,0:T(8,128)(2,1)S(1)}, bf16[16,72,128]{2,1,0:T(8,128)(2,1)S(1)}, u32[]{:S(2)}, u32[]{:S(2)}) collective-permute-start(bf16[16,72,128]{2,1,0:T(8,128)(2,1)S(1)} %collective-permute-done.9.q1), channel_id=1, source_target_pairs={{0,1},{1,0},{2,3},{3,2},{4,5},{5,4},{6,7},{7,6},{8,9},{9,8},{10,11... | collective-permute-start | bytes 884744 | tf_op jit(solution)/shard_map/ppermute | solution.py:33
  153.8 0.6 divide_subtract_fusion.1
  154.4 0.0 collective-permute-done.10.q2
  154.4 0.6 collective-permute-done.11.q3
  155.0 0.0 collective-permute-done.12.other
  155.0 4.2 %finish.1 = (bf16[136,512]{1,0:T(8,128)(2,1)}, bf16[136,8192]{1,0:T(8,128)(2,1)}) custom-call(s32[2]{0:T(128)S(1)} %pad_add_fusion.place, bf16[16,72,128]{2,1,0:T(8,128)(2,1)S(1)} %all_to_all.15.q0, bf16[16,72,128]{2,1,0:T(8,128)(2,1)S(1)} %collective-permute-done.9.q1, bf16[16,72,128]{2,1,0:T(8,128)(2,1)S(1)} %collective-permute-done.10.q2, ...), custom_call_target="tpu_custom_call" | custom-call | tf_op jit(solution)/shard_map/finish/pallas_call | solution.py:317
  (12 shorter events, 0.2 us)
Async XLA Ops:
  7.2 48.9 %copy-start.2 = (s32[1,136]{1,0:T(1,128)S(1)}, s32[1,136]{1,0:T(1,128)}, u32[]{:S(2)}) copy-start(s32[1,136]{1,0:T(1,128)} %loss_weight.3) | copy-start | bytes 1636
  7.2 48.9 %copy-start = (bf16[1,136,8192]{2,1,0:T(8,128)(2,1)S(1)}, bf16[1,136,8192]{2,1,0:T(8,128)(2,1)}, u32[]{:S(2)}) copy-start(bf16[1,136,8192]{2,1,0:T(8,128)(2,1)} %param.11) | copy-start | bytes 6684676
  9.1 29.9 %all-to-all-start = ((bf16[16,72,128]{2,1,0:T(8,128)(2,1)}), bf16[16,72,128]{2,1,0:T(8,128)(2,1)S(1)}, u32[]{:S(2)}, u32[]{:S(2)}) async-start(bf16[16,72,128]{2,1,0:T(8,128)(2,1)} %get-tuple-element.26), calls=%async_computation | async-start | bytes 589824 | tf_op jit(solution)/shard_map/all_to_all | solution.py:41
  24.1 112.6 %all-gather.3.cloned.1.call-start = ((), (), s32[]{:S(2)}) async-start(), calls=%async_computation.3 | async-start | bytes 5013504 | tf_op jit(solution)/shard_map/all_gather | solution.py:252
  24.1 10.1 %collective-permute-start = (bf16[576,128]{1,0:T(8,128)(2,1)}, bf16[576,128]{1,0:T(8,128)(2,1)S(1)}, u32[]{:S(2)}, u32[]{:S(2)}) collective-permute-start(bf16[576,128]{1,0:T(8,128)(2,1)} %get-tuple-element.27), channel_id=1, source_target_pairs={{64,0},{66,2},{128,64},{130,66},{192,128},{194,130},{256,192},{258... | collective-permute-start | bytes 442376 | tf_op jit(solution)/shard_map/ppermute | solution.py:244
  26.6 11.7 %collective-permute-start.1 = (bf16[576,128]{1,0:T(8,128)(2,1)}, bf16[576,128]{1,0:T(8,128)(2,1)S(1)}, u32[]{:S(2)}, u32[]{:S(2)}) collective-permute-start(bf16[576,128]{1,0:T(8,128)(2,1)} %get-tuple-element.27), channel_id=1, source_target_pairs={{66,0},{64,2},{130,64},{128,66},{194,128},{192,130},{258,192},{256... | collective-permute-start | bytes 442376 | tf_op jit(solution)/shard_map/ppermute | solution.py:245
  39.1 10.7 %collective-permute-start.2 = (bf16[16,72,128]{2,1,0:T(8,128)(2,1)S(1)}, bf16[16,72,128]{2,1,0:T(8,128)(2,1)S(1)}, u32[]{:S(2)}, u32[]{:S(2)}) collective-permute-start(bf16[16,72,128]{2,1,0:T(8,128)(2,1)S(1)} %all-to-all-done.q0), channel_id=1, source_target_pairs={{0,2},{2,0},{1,3},{3,1},{4,6},{6,4},{5,7},{7,5},{8,10},{10,8},{9,1... | collective-permute-start | bytes 884744 | tf_op jit(solution)/shard_map/ppermute | solution.py:33
  41.1 13.9 %collective-permute-start.3 = (bf16[16,72,128]{2,1,0:T(8,128)(2,1)S(1)}, bf16[16,72,128]{2,1,0:T(8,128)(2,1)S(1)}, u32[]{:S(2)}, u32[]{:S(2)}) collective-permute-start(bf16[16,72,128]{2,1,0:T(8,128)(2,1)S(1)} %all-to-all-done.q0), channel_id=1, source_target_pairs={{0,1},{1,0},{2,3},{3,2},{4,5},{5,4},{6,7},{7,6},{8,9},{9,8},{10,11... | collective-permute-start | bytes 884744 | tf_op jit(solution)/shard_map/ppermute | solution.py:33
  49.7 6.3 %collective-permute-start.4 = (bf16[16,72,128]{2,1,0:T(8,128)(2,1)S(1)}, bf16[16,72,128]{2,1,0:T(8,128)(2,1)S(1)}, u32[]{:S(2)}, u32[]{:S(2)}) collective-permute-start(bf16[16,72,128]{2,1,0:T(8,128)(2,1)S(1)} %collective-permute-done.2.q1), channel_id=1, source_target_pairs={{0,1},{1,0},{2,3},{3,2},{4,5},{5,4},{6,7},{7,6},{8,9},{9,8},{10,11... | collective-permute-start | bytes 884744 | tf_op jit(solution)/shard_map/ppermute | solution.py:33
  56.0 0.9 copy-start.1
  61.2 4.0 %copy-start.3 = (bf16[144,576]{1,0:T(8,128)(2,1)}, bf16[144,576]{1,0:T(8,128)(2,1)S(1)}, u32[]{:S(2)}) copy-start(bf16[144,576]{1,0:T(8,128)(2,1)S(1)} %get-tuple-element.31) | copy-start | bytes 497668
  61.2 3.9 %collective-permute-start.5 = (bf16[2,16,72,128]{3,2,1,0:T(8,128)(2,1)S(1)}, bf16[2,16,72,128]{3,2,1,0:T(8,128)(2,1)S(1)}, u32[]{:S(2)}, u32[]{:S(2)}) collective-permute-start(bf16[2,16,72,128]{3,2,1,0:T(8,128)(2,1)S(1)} %get-tuple-element.30), channel_id=1, source_target_pairs={{0,1},{1,0},{2,3},{3,2},{4,5},{5,4},{6,7},{7,6},{8,9},{9,8},{10,11... | collective-permute-start | bytes 1769480 | tf_op jit(solution)/shard_map/ppermute | solution.py:33
  65.2 21.1 %copy-start.10 = (f32[1,1,512]{2,1,0:T(1,128)S(1)}, f32[1,1,512]{2,1,0:T(1,128)}, u32[]{:S(2)}) copy-start(f32[1,1,512]{2,1,0:T(1,128)} %param.19) | copy-start | bytes 6148
  65.2 26.2 %copy-start.9 = (f32[1,1,512]{2,1,0:T(1,128)S(1)}, f32[1,1,512]{2,1,0:T(1,128)}, u32[]{:S(2)}) copy-start(f32[1,1,512]{2,1,0:T(1,128)} %param.20) | copy-start | bytes 6148
  65.3 21.0 %copy-start.4 = (bf16[144,576]{1,0:T(8,128)(2,1)S(1)}, bf16[144,576]{1,0:T(8,128)(2,1)}, u32[]{:S(2)}) copy-start(bf16[144,576]{1,0:T(8,128)(2,1)} %copy-done.3) | copy-start | bytes 497668
  65.3 40.0 %copy-start.8 = (f32[1,1,512]{2,1,0:T(1,128)S(1)}, f32[1,1,512]{2,1,0:T(1,128)}, u32[]{:S(2)}) copy-start(f32[1,1,512]{2,1,0:T(1,128)} %param.18) | copy-start | bytes 6148
  65.3 40.1 %copy-start.5 = (f32[1,128,64]{1,2,0:T(8,128)S(1)}, f32[1,128,64]{1,2,0:T(8,128)}, u32[]{:S(2)}) copy-start(f32[1,128,64]{1,2,0:T(8,128)} %param.15) | copy-start | bytes 98308
  65.3 40.1 %copy-start.6 = (f32[1,128,64]{1,2,0:T(8,128)S(1)}, f32[1,128,64]{1,2,0:T(8,128)}, u32[]{:S(2)}) copy-start(f32[1,128,64]{1,2,0:T(8,128)} %param.17) | copy-start | bytes 98308
  65.3 40.1 %copy-start.7 = (f32[1,128,64]{1,2,0:T(8,128)S(1)}, f32[1,128,64]{1,2,0:T(8,128)}, u32[]{:S(2)}) copy-start(f32[1,128,64]{1,2,0:T(8,128)} %param.16) | copy-start | bytes 98308
  65.3 10.2 %collective-permute-start.6 = (bf16[16,72,128]{2,1,0:T(8,128)(2,1)S(1)}, bf16[16,72,128]{2,1,0:T(8,128)(2,1)S(1)}, u32[]{:S(2)}, u32[]{:S(2)}) collective-permute-start(bf16[16,72,128]{2,1,0:T(8,128)(2,1)S(1)} %fusion.2), channel_id=1, source_target_pairs={{0,2},{2,0},{1,3},{3,1},{4,6},{6,4},{5,7},{7,5},{8,10},{10,8},{9,1... | collective-permute-start | bytes 884744 | tf_op jit(solution)/shard_map/ppermute | solution.py:33
  76.4 28.9 %all-to-all-start.1 = ((bf16[16,72,128]{2,1,0:T(8,128)(2,1)}), bf16[16,72,128]{2,1,0:T(8,128)(2,1)S(1)}, u32[]{:S(2)}, u32[]{:S(2)}) async-start(bf16[16,72,128]{2,1,0:T(8,128)(2,1)} %fusion.1), calls=%async_computation.1 | async-start | bytes 589824 | tf_op jit(solution)/shard_map/all_to_all | solution.py:281
  86.3 10.3 %collective-permute-start.7 = (bf16[144,576]{1,0:T(8,128)(2,1)S(1)}, bf16[144,576]{1,0:T(8,128)(2,1)S(1)}, u32[]{:S(2)}, u32[]{:S(2)}) collective-permute-start(bf16[144,576]{1,0:T(8,128)(2,1)S(1)} %copy-done.4), channel_id=1, source_target_pairs={{64,0},{65,1},{128,64},{129,65},{192,128},{193,129},{256,192},{257... | collective-permute-start | bytes 497672 | tf_op jit(solution)/shard_map/ppermute | solution.py:271
  88.2 13.9 %collective-permute-start.8 = (bf16[144,576]{1,0:T(8,128)(2,1)S(1)}, bf16[144,576]{1,0:T(8,128)(2,1)S(1)}, u32[]{:S(2)}, u32[]{:S(2)}) collective-permute-start(bf16[144,576]{1,0:T(8,128)(2,1)S(1)} %copy-done.4), channel_id=1, source_target_pairs={{65,0},{64,1},{129,64},{128,65},{193,128},{192,129},{257,192},{256... | collective-permute-start | bytes 497672 | tf_op jit(solution)/shard_map/ppermute | solution.py:271
  134.1 7.8 %collective-permute-start.9 = (bf16[16,72,128]{2,1,0:T(8,128)(2,1)S(1)}, bf16[16,72,128]{2,1,0:T(8,128)(2,1)S(1)}, u32[]{:S(2)}, u32[]{:S(2)}) collective-permute-start(bf16[16,72,128]{2,1,0:T(8,128)(2,1)S(1)} %all_to_all.15.q0), channel_id=1, source_target_pairs={{0,2},{2,0},{1,3},{3,1},{4,6},{6,4},{5,7},{7,5},{8,10},{10,8},{9,1... | collective-permute-start | bytes 884744 | tf_op jit(solution)/shard_map/ppermute | solution.py:33
  142.0 13.0 %collective-permute-start.12 = (bf16[136,4096]{1,0:T(8,128)(2,1)}, bf16[136,4096]{1,0:T(8,128)(2,1)S(1)}, u32[]{:S(2)}, u32[]{:S(2)}) collective-permute-start(bf16[136,4096]{1,0:T(8,128)(2,1)} %get-tuple-element.41), channel_id=1, source_target_pairs={{0,1},{1,0},{2,3},{3,2},{4,5},{5,4},{6,7},{7,6},{8,9},{9,8},{10,11... | collective-permute-start | bytes 3342344 | tf_op jit(solution)/shard_map/ppermute | solution.py:33
  149.4 5.0 %collective-permute-start.10 = (bf16[16,72,128]{2,1,0:T(8,128)(2,1)S(1)}, bf16[16,72,128]{2,1,0:T(8,128)(2,1)S(1)}, u32[]{:S(2)}, u32[]{:S(2)}) collective-permute-start(bf16[16,72,128]{2,1,0:T(8,128)(2,1)S(1)} %all_to_all.15.q0), channel_id=1, source_target_pairs={{0,1},{1,0},{2,3},{3,2},{4,5},{5,4},{6,7},{7,6},{8,9},{9,8},{10,11... | collective-permute-start | bytes 884744 | tf_op jit(solution)/shard_map/ppermute | solution.py:33
  151.4 3.6 %collective-permute-start.11 = (bf16[16,72,128]{2,1,0:T(8,128)(2,1)S(1)}, bf16[16,72,128]{2,1,0:T(8,128)(2,1)S(1)}, u32[]{:S(2)}, u32[]{:S(2)}) collective-permute-start(bf16[16,72,128]{2,1,0:T(8,128)(2,1)S(1)} %collective-permute-done.9.q1), channel_id=1, source_target_pairs={{0,1},{1,0},{2,3},{3,2},{4,5},{5,4},{6,7},{7,6},{8,9},{9,8},{10,11... | collective-permute-start | bytes 884744 | tf_op jit(solution)/shard_map/ppermute | solution.py:33
Sparse Core Ops, SparseCore 0:
  39.2 96.8 all-gather.2

commit v9 on v8

--- a/solution.py
+++ b/solution.py
@@ -177,7 +177,7 @@
             other[:, i * LANES : (i + 2) * LANES] = product[second : second + tokens].astype(bf16)
 
 
-def finish_kernel(place, q0, q1, q2, q3, acts, mine, other, out, upstream, down, extra, merged, sem):
+def finish_kernel(place, q0, q1, q23, acts, mine, other, out, upstream, down, extra, merged, sem):
     core, yl = place[0], place[1]
     rank = down.shape[0]
     for i in range(mine.shape[1] // LANES):
@@ -187,7 +187,7 @@
         merged[:, at + LANES : at + 2 * LANES] = jnp.where(core == 0, b, a)
     copy = pltpu.make_async_copy(merged, upstream, sem)
     copy.start()
-    unpack(core, yl, (q0, q1, q2, q3), down, extra, rank)
+    unpack(core, yl, (q0, q1, q23.at[0], q23.at[1]), down, extra, rank)
     up, _ = up_rows_of(core, yl, extra, q0.shape[0], rank, out.shape[1] // LANES)
     low = nt(acts[...], down[...]).astype(bf16)
     out[...] = (adapter_scale * nn(low, up)).astype(bf16)
@@ -313,14 +313,14 @@
         name="columns",
     )(rows_mine, rows_other, weights_all)
     got_yl, mine, other = after(swap(got, "yl"), mine, other)
-    got_last, got_core, other = swap(got_yl, "core"), swap(got, "core"), swap(other, "core")
+    got_core, other = swap(jnp.stack([got, got_yl]), "core"), swap(other, "core")
     refreshed, upstream = pl.pallas_call(
         finish_kernel,
         out_shape=(
             jax.ShapeDtypeStruct((tokens, features), bf16),
             jax.ShapeDtypeStruct((tokens, width), bf16),
         ),
-        in_specs=[SCALARS] + whole(7),
+        in_specs=[SCALARS] + whole(6),
         out_specs=(whole(1)[0], pl.BlockSpec(memory_space=pl.ANY)),
         scratch_shapes=[
             pltpu.VMEM((rank, width), bf16),
@@ -330,7 +330,7 @@
         ],
         compiler_params=params,
         name="finish",
-    )(place, got, got_yl, got_core, got_last, acts, mine, other)
+    )(place, got, got_yl, got_core, acts, mine, other)
     return (
         upstream[None],
         refreshed[None],

time: 168 us -> 167 us (level)
  starting transfers between devices: 70.4 us -> 68.1 us
    ppermute x9 -> x8, starting transfers between devices: 35.6 us -> 33.3 us  [swap(): return lax.ppermute(array, axis, [(0, 1), (1, 0)])]
    ppermute x9 -> x8, waiting for transfers between devices: 10.2 us -> 11.1 us  [swap(): return lax.ppermute(array, axis, [(0, 1), (1, 0)])]
  transfers between devices with their start and end apart: 16 -> 15, of which waited for: 9 -> 10; matrix products, arithmetic and copies ran while one was open for 2% -> 2% of each run, Pallas kernels for 6% -> 6%
where the time goes in v9:
time: 167 us; the launch traced here: 165 us
  starting transfers between devices  68.1 us (41%)
  waiting for transfers between devices  33.7 us (20%)
  blocking collectives  28.1 us (17%)
  Pallas kernels  15.7 us (9%)
  between operations  15.1 us (9%)
  other arithmetic  3.22 us (2%)
    ppermute x8, starting transfers between devices, swap(): return lax.ppermute(array, axis, [(0, 1), (1, 0)])  33.3 us
    all_to_all x1, blocking collectives, spread(): return lax.all_to_all(copies, 'z', 0, 0)  28.1 us
    all_to_all x1, starting transfers between devices, spread(): return lax.all_to_all(copies, 'z', 0, 0)  14.9 us
    ppermute x8, waiting for transfers between devices, swap(): return lax.ppermute(array, axis, [(0, 1), (1, 0)])  11.1 us
    ppermute x2, waiting for transfers between devices, per_device(): lax.ppermute(next_rows, ('section', 'core'), [(s * 2 + (c ^ flip), (s - 1...  10.7 us
    all_to_all x1, starting transfers between devices, per_device(): parts = lax.all_to_all(kept.astype(bf16), 'z', 0, 0)  9.08 us
    pallas_call x1, Pallas kernels, per_device(): pl.pallas_call(columns_kernel, out_shape=(half, half), in_specs=[pl.Block...  5.29 us
    ppermute x2, starting transfers between devices, per_device(): lax.ppermute(next_rows, ('section', 'core'), [(s * 2 + (c ^ flip), (s - 1...  5.1 us
  transfers between devices with their start and end apart: 15, of which 10 were waited for; matrix products, arithmetic and copies ran while one was open for 2% of the time, Pallas kernels for 6%

profile of v9, /device:TPU:7, one launch (start us, length us, event | category | flops | bytes accessed | tf_op | source)
XLA Modules:
  0.0 165.0 jit_solution(6433564524300388707)
XLA Ops:
  7.2 0.0 copy-start.2
  7.2 0.0 copy-start
  7.2 1.9 %prepare.1 = (bf16[16,72,128]{2,1,0:T(8,128)(2,1)}, bf16[576,128]{1,0:T(8,128)(2,1)}) custom-call(f32[64,128]{1,0:T(8,128)} %bitcast.68, f32[1,512]{1,0:T(1,128)} %bitcast.70, s32[1,136]{1,0:T(1,128)} %loss_weight.3, bf16[128,512]{1,0:T(8,128)(2,1)} %bitcast.67), custom_call_target="tpu_custom_call" | custom-call | tf_op jit(solution)/shard_map/prepare/pallas_call | solution.py:227
  9.1 14.9 %all-to-all-start = ((bf16[16,72,128]{2,1,0:T(8,128)(2,1)}), bf16[16,72,128]{2,1,0:T(8,128)(2,1)S(1)}, u32[]{:S(2)}, u32[]{:S(2)}) async-start(bf16[16,72,128]{2,1,0:T(8,128)(2,1)} %get-tuple-element.26), calls=%async_computation | async-start | bytes 589824 | tf_op jit(solution)/shard_map/all_to_all | solution.py:41
  24.1 0.0 all-gather.3.cloned.1.call-start
  24.1 2.5 %collective-permute-start = (bf16[576,128]{1,0:T(8,128)(2,1)}, bf16[576,128]{1,0:T(8,128)(2,1)S(1)}, u32[]{:S(2)}, u32[]{:S(2)}) collective-permute-start(bf16[576,128]{1,0:T(8,128)(2,1)} %get-tuple-element.27), channel_id=1, source_target_pairs={{64,0},{66,2},{128,64},{130,66},{192,128},{194,130},{256,192},{258... | collective-permute-start | bytes 442376 | tf_op jit(solution)/shard_map/ppermute | solution.py:244
  26.6 3.2 %collective-permute-start.1 = (bf16[576,128]{1,0:T(8,128)(2,1)}, bf16[576,128]{1,0:T(8,128)(2,1)S(1)}, u32[]{:S(2)}, u32[]{:S(2)}) collective-permute-start(bf16[576,128]{1,0:T(8,128)(2,1)} %get-tuple-element.27), channel_id=1, source_target_pairs={{66,0},{64,2},{130,64},{128,66},{194,128},{192,130},{258,192},{256... | collective-permute-start | bytes 442376 | tf_op jit(solution)/shard_map/ppermute | solution.py:245
  29.8 4.5 %collective-permute-done = bf16[576,128]{1,0:T(8,128)(2,1)S(1)} collective-permute-done((bf16[576,128]{1,0:T(8,128)(2,1)}, bf16[576,128]{1,0:T(8,128)(2,1)S(1)}, u32[]{:S(2)}, u32[]{:S(2)}) %collective-permute-start) | collective-permute-done | bytes 147488 | tf_op jit(solution)/shard_map/ppermute | solution.py:244
  34.2 4.0 %collective-permute-done.1 = bf16[576,128]{1,0:T(8,128)(2,1)S(1)} collective-permute-done((bf16[576,128]{1,0:T(8,128)(2,1)}, bf16[576,128]{1,0:T(8,128)(2,1)S(1)}, u32[]{:S(2)}, u32[]{:S(2)}) %collective-permute-start.1) | collective-permute-done | bytes 147488 | tf_op jit(solution)/shard_map/ppermute | solution.py:245
  38.3 0.7 pad_maximum_fusion.1
  39.0 0.0 all-to-all-done.q0
  39.0 0.0 all-gather.3.cloned.1.call-update
  39.1 2.0 %collective-permute-start.2 = (bf16[16,72,128]{2,1,0:T(8,128)(2,1)S(1)}, bf16[16,72,128]{2,1,0:T(8,128)(2,1)S(1)}, u32[]{:S(2)}, u32[]{:S(2)}) collective-permute-start(bf16[16,72,128]{2,1,0:T(8,128)(2,1)S(1)} %all-to-all-done.q0), channel_id=1, source_target_pairs={{0,2},{2,0},{1,3},{3,1},{4,6},{6,4},{5,7},{7,5},{8,10},{10,8},{9,1... | collective-permute-start | bytes 884744 | tf_op jit(solution)/shard_map/ppermute | solution.py:33
  41.0 8.7 %collective-permute-start.3 = (bf16[16,72,128]{2,1,0:T(8,128)(2,1)S(1)}, bf16[16,72,128]{2,1,0:T(8,128)(2,1)S(1)}, u32[]{:S(2)}, u32[]{:S(2)}) collective-permute-start(bf16[16,72,128]{2,1,0:T(8,128)(2,1)S(1)} %all-to-all-done.q0), channel_id=1, source_target_pairs={{0,1},{1,0},{2,3},{3,2},{4,5},{5,4},{6,7},{7,6},{8,9},{9,8},{10,11... | collective-permute-start | bytes 884744 | tf_op jit(solution)/shard_map/ppermute | solution.py:33
  49.7 0.0 collective-permute-done.2.q1
  49.7 5.1 %collective-permute-start.4 = (bf16[16,72,128]{2,1,0:T(8,128)(2,1)S(1)}, bf16[16,72,128]{2,1,0:T(8,128)(2,1)S(1)}, u32[]{:S(2)}, u32[]{:S(2)}) collective-permute-start(bf16[16,72,128]{2,1,0:T(8,128)(2,1)S(1)} %collective-permute-done.2.q1), channel_id=1, source_target_pairs={{0,1},{1,0},{2,3},{3,2},{4,5},{5,4},{6,7},{7,6},{8,9},{9,8},{10,11... | collective-permute-start | bytes 884744 | tf_op jit(solution)/shard_map/ppermute | solution.py:33
  54.8 0.1 pad_add_fusion.place
  54.9 0.0 collective-permute-done.3.q2
  54.9 1.1 collective-permute-done.4.q3
  56.0 0.0 copy-done.2
  56.0 0.0 copy-done
  56.0 0.9 copy-done.1
  56.9 4.2 %backward.1 = (f32[2,16,72,128]{3,2,1,0:T(8,128)S(1)}, bf16[2,16,72,128]{3,2,1,0:T(8,128)(2,1)S(1)}, bf16[144,576]{1,0:T(8,128)(2,1)S(1)}) custom-call(s32[2]{0:T(128)S(1)} %pad_add_fusion.place, bf16[16,72,128]{2,1,0:T(8,128)(2,1)S(1)} %all-to-all-done.q0, bf16[16,72,128]{2,1,0:T(8,128)(2,1)S(1)} %collective-permute-done.2.q1, ...), custom_call_target="tpu_custom_call" | custom-call | tf_op jit(solution)/shard_map/backward/pallas_call | solution.py:254
  61.2 0.0 copy-start.3
  61.2 2.3 %collective-permute-start.5 = (bf16[2,16,72,128]{3,2,1,0:T(8,128)(2,1)S(1)}, bf16[2,16,72,128]{3,2,1,0:T(8,128)(2,1)S(1)}, u32[]{:S(2)}, u32[]{:S(2)}) collective-permute-start(bf16[2,16,72,128]{3,2,1,0:T(8,128)(2,1)S(1)} %get-tuple-element.30), channel_id=1, source_target_pairs={{0,1},{1,0},{2,3},{3,2},{4,5},{5,4},{6,7},{7,6},{8,9},{9,8},{10,11... | collective-permute-start | bytes 1769480 | tf_op jit(solution)/shard_map/ppermute | solution.py:33
  63.5 1.6 collective-permute-done.5
  65.1 0.1 convert_add_fusion
  65.2 0.0 copy-done.3
  65.2 0.0 copy-start.10
  65.2 0.0 copy-start.9
  65.3 0.0 copy-start.4
  65.3 0.0 copy-start.8
  65.3 0.0 copy-start.5
  65.3 0.0 copy-start.6
  65.3 0.0 copy-start.7
  65.3 3.3 %collective-permute-start.6 = (bf16[16,72,128]{2,1,0:T(8,128)(2,1)S(1)}, bf16[16,72,128]{2,1,0:T(8,128)(2,1)S(1)}, u32[]{:S(2)}, u32[]{:S(2)}) collective-permute-start(bf16[16,72,128]{2,1,0:T(8,128)(2,1)S(1)} %fusion.2), channel_id=1, source_target_pairs={{0,2},{2,0},{1,3},{3,1},{4,6},{6,4},{5,7},{7,5},{8,10},{10,8},{9,1... | collective-permute-start | bytes 884744 | tf_op jit(solution)/shard_map/ppermute | solution.py:33
  68.7 6.9 %collective-permute-done.6 = bf16[16,72,128]{2,1,0:T(8,128)(2,1)S(1)} collective-permute-done((bf16[16,72,128]{2,1,0:T(8,128)(2,1)S(1)}, bf16[16,72,128]{2,1,0:T(8,128)(2,1)S(1)}, u32[]{:S(2)}, u32[]{:S(2)}) %collective-permute-start.6) | collective-permute-done | bytes 294944 | tf_op jit(solution)/shard_map/ppermute | solution.py:33
  75.6 0.8 fusion.1
  76.4 9.1 %all-to-all-start.1 = ((bf16[16,72,128]{2,1,0:T(8,128)(2,1)}), bf16[16,72,128]{2,1,0:T(8,128)(2,1)S(1)}, u32[]{:S(2)}, u32[]{:S(2)}) async-start(bf16[16,72,128]{2,1,0:T(8,128)(2,1)} %fusion.1), calls=%async_computation.1 | async-start | bytes 589824 | tf_op jit(solution)/shard_map/all_to_all | solution.py:281
  86.2 0.1 pad.4.clone
  86.3 0.0 copy-done.10
  86.3 0.0 copy-done.4
  86.3 1.9 %collective-permute-start.7 = (bf16[144,576]{1,0:T(8,128)(2,1)S(1)}, bf16[144,576]{1,0:T(8,128)(2,1)S(1)}, u32[]{:S(2)}, u32[]{:S(2)}) collective-permute-start(bf16[144,576]{1,0:T(8,128)(2,1)S(1)} %copy-done.4), channel_id=1, source_target_pairs={{64,0},{65,1},{128,64},{129,65},{192,128},{193,129},{256,192},{257... | collective-permute-start | bytes 497672 | tf_op jit(solution)/shard_map/ppermute | solution.py:271
  88.2 3.2 %collective-permute-start.8 = (bf16[144,576]{1,0:T(8,128)(2,1)S(1)}, bf16[144,576]{1,0:T(8,128)(2,1)S(1)}, u32[]{:S(2)}, u32[]{:S(2)}) collective-permute-start(bf16[144,576]{1,0:T(8,128)(2,1)S(1)} %copy-done.4), channel_id=1, source_target_pairs={{65,0},{64,1},{129,64},{128,65},{193,128},{192,129},{257,192},{256... | collective-permute-start | bytes 497672 | tf_op jit(solution)/shard_map/ppermute | solution.py:271
  91.4 5.1 %collective-permute-done.7.rows_mine = bf16[144,576]{1,0:T(8,128)(2,1)S(1)} collective-permute-done((bf16[144,576]{1,0:T(8,128)(2,1)S(1)}, bf16[144,576]{1,0:T(8,128)(2,1)S(1)}, u32[]{:S(2)}, u32[]{:S(2)}) %collective-permute-start.7) | collective-permute-done | bytes 165920 | tf_op jit(solution)/shard_map/ppermute | solution.py:271
  96.6 5.6 %collective-permute-done.8.rows_other = bf16[144,576]{1,0:T(8,128)(2,1)S(1)} collective-permute-done((bf16[144,576]{1,0:T(8,128)(2,1)S(1)}, bf16[144,576]{1,0:T(8,128)(2,1)S(1)}, u32[]{:S(2)}, u32[]{:S(2)}) %collective-permute-start.8) | collective-permute-done | bytes 165920 | tf_op jit(solution)/shard_map/ppermute | solution.py:271
  102.1 3.4 %all-to-all-done.1 = bf16[16,72,128]{2,1,0:T(8,128)(2,1)S(1)} async-done(((bf16[16,72,128]{2,1,0:T(8,128)(2,1)}), bf16[16,72,128]{2,1,0:T(8,128)(2,1)S(1)}, u32[]{:S(2)}, u32[]{:S(2)}) %all-to-all-start.1) | async-done | bytes 294944 | tf_op jit(solution)/shard_map/all_to_all | solution.py:281
  105.6 0.0 copy-done.5
  105.6 0.0 copy-done.6
  105.6 0.0 copy-done.7
  105.6 0.7 fusion.10
  106.3 0.1 maximum_maximum_fusion
  106.4 28.1 %all_to_all.15.q0 = bf16[16,72,128]{2,1,0:T(8,128)(2,1)S(1)} all-to-all(bf16[16,72,128]{2,1,0:T(8,128)(2,1)S(1)} %broadcast_in_dim.28), channel_id=1, replica_groups=mesh['section'=8,'z'=16,'yl'=2,'core'=2] {'z'}, dimensions={0} | all-to-all | bytes 589824 | tf_op jit(solution)/shard_map/all_to_all | solution.py:41
  134.5 2.0 %collective-permute-start.9 = (bf16[16,72,128]{2,1,0:T(8,128)(2,1)S(1)}, bf16[16,72,128]{2,1,0:T(8,128)(2,1)S(1)}, u32[]{:S(2)}, u32[]{:S(2)}) collective-permute-start(bf16[16,72,128]{2,1,0:T(8,128)(2,1)S(1)} %all_to_all.15.q0), channel_id=1, source_target_pairs={{0,2},{2,0},{1,3},{3,1},{4,6},{6,4},{5,7},{7,5},{8,10},{10,8},{9,1... | collective-permute-start | bytes 884744 | tf_op jit(solution)/shard_map/ppermute | solution.py:33
  136.5 0.0 all-gather.3.cloned.1.call-done.weights
  136.5 5.3 %columns.1 = (bf16[136,4096]{1,0:T(8,128)(2,1)S(1)}, bf16[136,4096]{1,0:T(8,128)(2,1)}) custom-call(bf16[144,576]{1,0:T(8,128)(2,1)S(1)} %collective-permute-done.7.rows_mine, bf16[144,576]{1,0:T(8,128)(2,1)S(1)} %collective-permute-done.8.rows_other, bf16[32,576,128]{2,1,0:T(8,128)(2,1)} %all-gather.3.cloned.1.call-done.weights), custom_call_target="tpu_custom_call" | custom-call | flops 1283457024 | bytes 4718592 | tf_op jit(solution)/shard_map/columns/pallas_call | solution.py:297
  141.8 0.1 collective-permute-done.9.q1
  141.9 8.0 %collective-permute-start.11 = (bf16[136,4096]{1,0:T(8,128)(2,1)}, bf16[136,4096]{1,0:T(8,128)(2,1)S(1)}, u32[]{:S(2)}, u32[]{:S(2)}) collective-permute-start(bf16[136,4096]{1,0:T(8,128)(2,1)} %get-tuple-element.41), channel_id=1, source_target_pairs={{0,1},{1,0},{2,3},{3,2},{4,5},{5,4},{6,7},{7,6},{8,9},{9,8},{10,11... | collective-permute-start | bytes 3342344 | tf_op jit(solution)/shard_map/ppermute | solution.py:33
  149.9 0.1 pad_maximum_fusion
  150.0 1.9 %collective-permute-start.10 = (bf16[2,16,72,128]{3,2,1,0:T(8,128)(2,1)S(1)}, bf16[2,16,72,128]{3,2,1,0:T(8,128)(2,1)S(1)}, u32[]{:S(2)}, u32[]{:S(2)}) collective-permute-start(bf16[2,16,72,128]{3,2,1,0:T(8,128)(2,1)S(1)} %pad_maximum_fusion), channel_id=1, source_target_pairs={{0,1},{1,0},{2,3},{3,2},{4,5},{5,4},{6,7},{7,6},{8,9},{9,8},{10,11... | collective-permute-start | bytes 1769480 | tf_op jit(solution)/shard_map/ppermute | solution.py:33
  151.9 0.6 divide_subtract_fusion.1
  152.5 1.4 collective-permute-done.10.q23
  153.9 0.0 collective-permute-done.11.other
  153.9 4.2 %finish.1 = (bf16[136,512]{1,0:T(8,128)(2,1)}, bf16[136,8192]{1,0:T(8,128)(2,1)}) custom-call(s32[2]{0:T(128)S(1)} %pad_add_fusion.place, bf16[16,72,128]{2,1,0:T(8,128)(2,1)S(1)} %all_to_all.15.q0, bf16[16,72,128]{2,1,0:T(8,128)(2,1)S(1)} %collective-permute-done.9.q1, bf16[2,16,72,128]{3,2,1,0:T(8,128)(2,1)S(1)} %collective-permute-done.10.q23, ...), custom_call_target="tpu_custom_call" | custom-call | tf_op jit(solution)/shard_map/finish/pallas_call | solution.py:317
  (11 shorter events, 0.2 us)
Async XLA Ops:
  7.2 48.9 %copy-start.2 = (s32[1,136]{1,0:T(1,128)S(1)}, s32[1,136]{1,0:T(1,128)}, u32[]{:S(2)}) copy-start(s32[1,136]{1,0:T(1,128)} %loss_weight.3) | copy-start | bytes 1636
  7.2 48.9 %copy-start = (bf16[1,136,8192]{2,1,0:T(8,128)(2,1)S(1)}, bf16[1,136,8192]{2,1,0:T(8,128)(2,1)}, u32[]{:S(2)}) copy-start(bf16[1,136,8192]{2,1,0:T(8,128)(2,1)} %param.11) | copy-start | bytes 6684676
  9.1 29.9 %all-to-all-start = ((bf16[16,72,128]{2,1,0:T(8,128)(2,1)}), bf16[16,72,128]{2,1,0:T(8,128)(2,1)S(1)}, u32[]{:S(2)}, u32[]{:S(2)}) async-start(bf16[16,72,128]{2,1,0:T(8,128)(2,1)} %get-tuple-element.26), calls=%async_computation | async-start | bytes 589824 | tf_op jit(solution)/shard_map/all_to_all | solution.py:41
  24.1 112.5 %all-gather.3.cloned.1.call-start = ((), (), s32[]{:S(2)}) async-start(), calls=%async_computation.3 | async-start | bytes 5013504 | tf_op jit(solution)/shard_map/all_gather | solution.py:252
  24.1 10.1 %collective-permute-start = (bf16[576,128]{1,0:T(8,128)(2,1)}, bf16[576,128]{1,0:T(8,128)(2,1)S(1)}, u32[]{:S(2)}, u32[]{:S(2)}) collective-permute-start(bf16[576,128]{1,0:T(8,128)(2,1)} %get-tuple-element.27), channel_id=1, source_target_pairs={{64,0},{66,2},{128,64},{130,66},{192,128},{194,130},{256,192},{258... | collective-permute-start | bytes 442376 | tf_op jit(solution)/shard_map/ppermute | solution.py:244
  26.6 11.7 %collective-permute-start.1 = (bf16[576,128]{1,0:T(8,128)(2,1)}, bf16[576,128]{1,0:T(8,128)(2,1)S(1)}, u32[]{:S(2)}, u32[]{:S(2)}) collective-permute-start(bf16[576,128]{1,0:T(8,128)(2,1)} %get-tuple-element.27), channel_id=1, source_target_pairs={{66,0},{64,2},{130,64},{128,66},{194,128},{192,130},{258,192},{256... | collective-permute-start | bytes 442376 | tf_op jit(solution)/shard_map/ppermute | solution.py:245
  39.1 10.7 %collective-permute-start.2 = (bf16[16,72,128]{2,1,0:T(8,128)(2,1)S(1)}, bf16[16,72,128]{2,1,0:T(8,128)(2,1)S(1)}, u32[]{:S(2)}, u32[]{:S(2)}) collective-permute-start(bf16[16,72,128]{2,1,0:T(8,128)(2,1)S(1)} %all-to-all-done.q0), channel_id=1, source_target_pairs={{0,2},{2,0},{1,3},{3,1},{4,6},{6,4},{5,7},{7,5},{8,10},{10,8},{9,1... | collective-permute-start | bytes 884744 | tf_op jit(solution)/shard_map/ppermute | solution.py:33
  41.0 13.9 %collective-permute-start.3 = (bf16[16,72,128]{2,1,0:T(8,128)(2,1)S(1)}, bf16[16,72,128]{2,1,0:T(8,128)(2,1)S(1)}, u32[]{:S(2)}, u32[]{:S(2)}) collective-permute-start(bf16[16,72,128]{2,1,0:T(8,128)(2,1)S(1)} %all-to-all-done.q0), channel_id=1, source_target_pairs={{0,1},{1,0},{2,3},{3,2},{4,5},{5,4},{6,7},{7,6},{8,9},{9,8},{10,11... | collective-permute-start | bytes 884744 | tf_op jit(solution)/shard_map/ppermute | solution.py:33
  49.7 6.3 %collective-permute-start.4 = (bf16[16,72,128]{2,1,0:T(8,128)(2,1)S(1)}, bf16[16,72,128]{2,1,0:T(8,128)(2,1)S(1)}, u32[]{:S(2)}, u32[]{:S(2)}) collective-permute-start(bf16[16,72,128]{2,1,0:T(8,128)(2,1)S(1)} %collective-permute-done.2.q1), channel_id=1, source_target_pairs={{0,1},{1,0},{2,3},{3,2},{4,5},{5,4},{6,7},{7,6},{8,9},{9,8},{10,11... | collective-permute-start | bytes 884744 | tf_op jit(solution)/shard_map/ppermute | solution.py:33
  56.0 0.9 copy-start.1
  61.2 4.0 %copy-start.3 = (bf16[144,576]{1,0:T(8,128)(2,1)}, bf16[144,576]{1,0:T(8,128)(2,1)S(1)}, u32[]{:S(2)}) copy-start(bf16[144,576]{1,0:T(8,128)(2,1)S(1)} %get-tuple-element.31) | copy-start | bytes 497668
  61.2 3.9 %collective-permute-start.5 = (bf16[2,16,72,128]{3,2,1,0:T(8,128)(2,1)S(1)}, bf16[2,16,72,128]{3,2,1,0:T(8,128)(2,1)S(1)}, u32[]{:S(2)}, u32[]{:S(2)}) collective-permute-start(bf16[2,16,72,128]{3,2,1,0:T(8,128)(2,1)S(1)} %get-tuple-element.30), channel_id=1, source_target_pairs={{0,1},{1,0},{2,3},{3,2},{4,5},{5,4},{6,7},{7,6},{8,9},{9,8},{10,11... | collective-permute-start | bytes 1769480 | tf_op jit(solution)/shard_map/ppermute | solution.py:33
  65.2 21.1 %copy-start.10 = (f32[1,1,512]{2,1,0:T(1,128)S(1)}, f32[1,1,512]{2,1,0:T(1,128)}, u32[]{:S(2)}) copy-start(f32[1,1,512]{2,1,0:T(1,128)} %param.19) | copy-start | bytes 6148
  65.2 26.2 %copy-start.9 = (f32[1,1,512]{2,1,0:T(1,128)S(1)}, f32[1,1,512]{2,1,0:T(1,128)}, u32[]{:S(2)}) copy-start(f32[1,1,512]{2,1,0:T(1,128)} %param.20) | copy-start | bytes 6148
  65.3 21.0 %copy-start.4 = (bf16[144,576]{1,0:T(8,128)(2,1)S(1)}, bf16[144,576]{1,0:T(8,128)(2,1)}, u32[]{:S(2)}) copy-start(bf16[144,576]{1,0:T(8,128)(2,1)} %copy-done.3) | copy-start | bytes 497668
  65.3 40.3 %copy-start.8 = (f32[1,1,512]{2,1,0:T(1,128)S(1)}, f32[1,1,512]{2,1,0:T(1,128)}, u32[]{:S(2)}) copy-start(f32[1,1,512]{2,1,0:T(1,128)} %param.18) | copy-start | bytes 6148
  65.3 40.3 %copy-start.5 = (f32[1,128,64]{1,2,0:T(8,128)S(1)}, f32[1,128,64]{1,2,0:T(8,128)}, u32[]{:S(2)}) copy-start(f32[1,128,64]{1,2,0:T(8,128)} %param.15) | copy-start | bytes 98308
  65.3 40.3 %copy-start.6 = (f32[1,128,64]{1,2,0:T(8,128)S(1)}, f32[1,128,64]{1,2,0:T(8,128)}, u32[]{:S(2)}) copy-start(f32[1,128,64]{1,2,0:T(8,128)} %param.17) | copy-start | bytes 98308
  65.3 40.3 %copy-start.7 = (f32[1,128,64]{1,2,0:T(8,128)S(1)}, f32[1,128,64]{1,2,0:T(8,128)}, u32[]{:S(2)}) copy-start(f32[1,128,64]{1,2,0:T(8,128)} %param.16) | copy-start | bytes 98308
  65.3 10.2 %collective-permute-start.6 = (bf16[16,72,128]{2,1,0:T(8,128)(2,1)S(1)}, bf16[16,72,128]{2,1,0:T(8,128)(2,1)S(1)}, u32[]{:S(2)}, u32[]{:S(2)}) collective-permute-start(bf16[16,72,128]{2,1,0:T(8,128)(2,1)S(1)} %fusion.2), channel_id=1, source_target_pairs={{0,2},{2,0},{1,3},{3,1},{4,6},{6,4},{5,7},{7,5},{8,10},{10,8},{9,1... | collective-permute-start | bytes 884744 | tf_op jit(solution)/shard_map/ppermute | solution.py:33
  76.4 29.1 %all-to-all-start.1 = ((bf16[16,72,128]{2,1,0:T(8,128)(2,1)}), bf16[16,72,128]{2,1,0:T(8,128)(2,1)S(1)}, u32[]{:S(2)}, u32[]{:S(2)}) async-start(bf16[16,72,128]{2,1,0:T(8,128)(2,1)} %fusion.1), calls=%async_computation.1 | async-start | bytes 589824 | tf_op jit(solution)/shard_map/all_to_all | solution.py:281
  86.3 10.3 %collective-permute-start.7 = (bf16[144,576]{1,0:T(8,128)(2,1)S(1)}, bf16[144,576]{1,0:T(8,128)(2,1)S(1)}, u32[]{:S(2)}, u32[]{:S(2)}) collective-permute-start(bf16[144,576]{1,0:T(8,128)(2,1)S(1)} %copy-done.4), channel_id=1, source_target_pairs={{64,0},{65,1},{128,64},{129,65},{192,128},{193,129},{256,192},{257... | collective-permute-start | bytes 497672 | tf_op jit(solution)/shard_map/ppermute | solution.py:271
  88.2 13.9 %collective-permute-start.8 = (bf16[144,576]{1,0:T(8,128)(2,1)S(1)}, bf16[144,576]{1,0:T(8,128)(2,1)S(1)}, u32[]{:S(2)}, u32[]{:S(2)}) collective-permute-start(bf16[144,576]{1,0:T(8,128)(2,1)S(1)} %copy-done.4), channel_id=1, source_target_pairs={{65,0},{64,1},{129,64},{128,65},{193,128},{192,129},{257,192},{256... | collective-permute-start | bytes 497672 | tf_op jit(solution)/shard_map/ppermute | solution.py:271
  134.5 7.5 %collective-permute-start.9 = (bf16[16,72,128]{2,1,0:T(8,128)(2,1)S(1)}, bf16[16,72,128]{2,1,0:T(8,128)(2,1)S(1)}, u32[]{:S(2)}, u32[]{:S(2)}) collective-permute-start(bf16[16,72,128]{2,1,0:T(8,128)(2,1)S(1)} %all_to_all.15.q0), channel_id=1, source_target_pairs={{0,2},{2,0},{1,3},{3,1},{4,6},{6,4},{5,7},{7,5},{8,10},{10,8},{9,1... | collective-permute-start | bytes 884744 | tf_op jit(solution)/shard_map/ppermute | solution.py:33
  141.9 12.0 %collective-permute-start.11 = (bf16[136,4096]{1,0:T(8,128)(2,1)}, bf16[136,4096]{1,0:T(8,128)(2,1)S(1)}, u32[]{:S(2)}, u32[]{:S(2)}) collective-permute-start(bf16[136,4096]{1,0:T(8,128)(2,1)} %get-tuple-element.41), channel_id=1, source_target_pairs={{0,1},{1,0},{2,3},{3,2},{4,5},{5,4},{6,7},{7,6},{8,9},{9,8},{10,11... | collective-permute-start | bytes 3342344 | tf_op jit(solution)/shard_map/ppermute | solution.py:33
  150.0 3.9 %collective-permute-start.10 = (bf16[2,16,72,128]{3,2,1,0:T(8,128)(2,1)S(1)}, bf16[2,16,72,128]{3,2,1,0:T(8,128)(2,1)S(1)}, u32[]{:S(2)}, u32[]{:S(2)}) collective-permute-start(bf16[2,16,72,128]{3,2,1,0:T(8,128)(2,1)S(1)} %pad_maximum_fusion), channel_id=1, source_target_pairs={{0,1},{1,0},{2,3},{3,2},{4,5},{5,4},{6,7},{7,6},{8,9},{9,8},{10,11... | collective-permute-start | bytes 1769480 | tf_op jit(solution)/shard_map/ppermute | solution.py:33
Sparse Core Ops, SparseCore 0:
  39.2 96.5 all-gather.2
